TPU v7x, 256 devices: a whole 4x4x8 slice. The times are simulated.
256 devices in a mesh: azim: 32 (over z, y_lo, core), radax: 8 (over x, y_hi).
Axes of the slice: x: 4, y: 4 (y_hi: 2, y_lo: 2; y = y_hi * 2 + y_lo), z: 8, core: 2. Of those that a mesh axis runs over, the one named last changes fastest.
Arguments:
- velocity: float32 [3, 256, 64, 1024], P(None, 'azim', None, 'radax')
- rotor_flux: float32 [256, 1024], P('azim', 'radax'), may hold values from -6 to 6
- correlation_weight: float32 [3, 256, 1024], P(None, 'azim', 'radax'), may hold values from 0.2 to 1
- damping: float32 [256, 64, 1024], P('azim', None, 'radax'), may hold values from 0.5 to 4
- offset: int32 [1], replicated, may hold values from 0 to 255
Outputs:
- new_velocity: float32 [3, 256, 64, 1024], P(None, 'azim', None, 'radax')
- pressure: float32 [256, 64, 1024], P('azim', None, 'radax')
All inputs are finite; a program needn't handle non-finite values.
Results may differ from a plain program's by a relative error of at most 0.0001.
Values sent between devices are 32-bit elements; how exact they have to be, the bound alone decides.
No kernel may reach another device: no remote copies, remote signals or barrier semaphores. Data moves between devices by JAX's collectives and lax.ppermute only.
A program may use at most 64 MiB of HBM per device.

v0:
```python
import jax
import jax.numpy as jnp
from jax import lax
from jax.sharding import PartitionSpec as P

ITERS = 3


viscosity = 0.1
courant = 0.2


def with_halo(array, sides, width):
    for axis, dim in sides:
        devices, length = (lax.axis_size(axis), array.shape[dim])
        up = [(i, (i + 1) % devices) for i in range(devices)]
        down = [(j, i) for i, j in up]
        last = lax.slice_in_dim(array, length - width, length, axis=dim)
        first = lax.slice_in_dim(array, 0, width, axis=dim)
        before = lax.ppermute(last, axis, up)
        after = lax.ppermute(first, axis, down)
        array = jnp.concatenate([before, array, after], axis=dim)
    return array


def stencil_parts(grown, inner):
    center = grown[:, 1:-1, :, 1:-1]
    east = grown[:, 2:, :, 1:-1]
    west = grown[:, :-2, :, 1:-1]
    above = grown[:, 1:-1, :, 2:]
    below = grown[:, 1:-1, :, :-2]
    outer = jnp.zeros_like(center[:, :, :1])
    radial = jnp.concatenate([inner[:, :, None, :], center, outer], axis=2)
    return (center, east, west, radial[:, :, 2:], radial[:, :, :-2], above, below)


def axial_walls(grown, depth):
    place = lax.axis_index("radax")
    count = lax.axis_size("radax")
    lower = jnp.where(place == 0, 0.0, grown[..., :depth])
    upper = jnp.where(place == count - 1, 0.0, grown[..., -depth:])
    return jnp.concatenate([lower, grown[..., depth:-depth], upper], axis=3)


def extend(field, inner):
    grown = with_halo(field, (("azim", 1), ("radax", 3)), 1)
    return stencil_parts(axial_walls(grown, 1), inner)


def momentum_extend(field, inner):
    grown = with_halo(field, (("azim", 1), ("radax", 3)), 1)
    return stencil_parts(axial_walls(grown, 1), inner)


def advance_cells(center, east, west, outward, inward, above, below):
    nearby = east + west + outward + inward + above + below
    return (
        center + viscosity * (nearby - 6.0 * center) - courant * center[0:1] * 0.5 * (east - west)
    )


def squares(residual):
    return lax.psum(jnp.sum(residual * residual), ("azim", "radax"))


def per_device(velocity, rotor_flux, correlation_weight, damping, offset):
    advance = offset[0]
    width = rotor_flux.shape[0]
    whole = lax.all_gather(rotor_flux, "azim", axis=0, tiled=True)
    total = whole.shape[0]
    cyclic = jnp.concatenate([whole, whole[:width]], axis=0)
    start = (lax.axis_index("azim") * width - advance) % total
    rotated = lax.dynamic_slice_in_dim(cyclic, start, width, 0)
    rim = with_halo(rotated, (("azim", 0),), 1)
    face_flux = (
        correlation_weight[0] * rim[:-2]
        + correlation_weight[1] * rim[1:-1]
        + correlation_weight[2] * rim[2:]
    )
    zero_face = jnp.zeros_like(face_flux)
    inner = jnp.stack([zero_face, face_flux, zero_face])
    predicted = advance_cells(*momentum_extend(velocity, inner))
    center, east, west, outward, inward, above, below = momentum_extend(predicted, inner)
    source = 0.5 * (east[0] - west[0] + outward[1] - inward[1] + above[2] - below[2])
    blank = jnp.zeros((1,) + face_flux.shape, jnp.float32)
    pressure = jnp.zeros_like(source)
    residual = source
    direction = source
    norm_now = squares(residual)
    for step in range(ITERS):
        (
            operate_center,
            operate_east,
            operate_west,
            operate_outward,
            operate_inward,
            operate_above,
            operate_below,
        ) = extend(direction[None], blank)
        image = (6.0 + damping) * operate_center[0] - (
            operate_east
            + operate_west
            + operate_outward
            + operate_inward
            + operate_above
            + operate_below
        )[0]
        alpha = norm_now / lax.psum(jnp.sum(direction * image), ("azim", "radax"))
        pressure = pressure + alpha * direction
        residual = residual - alpha * image
        norm_next = squares(residual)
        direction = residual + norm_next / norm_now * direction
        norm_now = norm_next
    center, east, west, outward, inward, above, below = extend(pressure[None], blank)
    gradient = jnp.stack(
        [0.5 * (east - west)[0], 0.5 * (outward - inward)[0], 0.5 * (above - below)[0]]
    )
    return (predicted - gradient, pressure)


def solution(mesh):
    in_specs = (
        P(None, "azim", None, "radax"),
        P("azim", "radax"),
        P(None, "azim", "radax"),
        P("azim", None, "radax"),
        P(),
    )
    out_specs = (P(None, "azim", None, "radax"), P("azim", None, "radax"))
    return jax.shard_map(
        per_device, mesh=mesh, in_specs=in_specs, out_specs=out_specs, check_vma=False
    )
```

profile of v0, /device:TPU:1, one launch (start us, length us, event | category | flops | bytes accessed | tf_op | source)
XLA Modules:
  0.0 548.1 jit_solution(12614246718032903987)
XLA Ops:
  1.3 39.2 %all_gather.3 = f32[256,128]{1,0:T(8,128)S(1)} all-gather(f32[8,128]{1,0:T(8,128)} %param.6), channel_id=1, replica_groups=mesh['azim'=32,'radax'=8] {'azim'}, dimensions={0}, use_global_device_ids=true | all-gather | bytes 135168 | tf_op jit(solution)/shard_map/all_gather | solution.py:69
  41.1 1.6 copy.29
  42.7 1.4 collective-permute-start.1
  44.1 2.3 collective-permute-start
  46.4 1.0 multiply_bitcast_fusion
  47.4 1.0 copy.30
  48.4 0.8 collective-permute-done
  49.2 0.6 pad_maximum_fusion.55
  49.9 4.8 collective-permute-start.4
  55.7 0.7 broadcast_select_fusion.3
  56.5 5.2 collective-permute-done.5
  61.7 3.1 fusion.4
  64.9 0.9 collective-permute-start.7
  65.8 5.1 collective-permute-start.6
  70.9 0.8 collective-permute-done.7
  72.1 3.0 collective-permute-start.9
  75.0 1.4 collective-permute-done.8
  76.5 1.9 collective-permute-done.9
  78.4 1.3 broadcast_multiply_fusion
  79.8 7.5 %collective-permute-start.10 = (f32[1,1,64,128]{2,3,1,0:T(8,128)S(1)}, f32[1,1,64,128]{2,3,1,0:T(8,128)S(1)}, u32[]{:S(2)}, u32[]{:S(2)}) collective-permute-start(f32[1,1,64,128]{2,3,1,0:T(8,128)S(1)} %get-tuple-element.43), channel_id=1, source_target_pairs={{8,0},{16,8},{24,16},{32,24},{40,32},{48,40},{56,48},{64,56},{72,6... | collective-permute-start | bytes 98312 | tf_op jit(solution)/shard_map/ppermute | solution.py:21
  88.2 0.6 pad_maximum_fusion.67
  89.0 2.0 copy.32
  90.9 2.8 collective-permute-start.13
  93.8 0.7 broadcast_select_fusion.11
  94.5 2.8 collective-permute-done.13
  97.2 5.0 fusion.41
  102.2 78.6 %all-reduce.10 = (f32[]{:T(128)}, f32[]{:T(128)}) all-reduce(f32[]{:T(128)} %get-tuple-element.7, f32[]{:T(128)} %get-tuple-element.6), channel_id=1, replica_groups=mesh['azim'=32,'radax'=8] {'azim','radax'}, use_global_device_ids=true, to_apply=%region_1.2 | all-reduce | flops 2 | bytes 16 | tf_op jit(solution)/shard_map/psum | solution.py:63
  182.2 2.8 multiply_reduce_fusion.2
  184.9 73.5 %psum.44 = f32[]{:T(128)} all-reduce(f32[]{:T(128)} %get-tuple-element.12), channel_id=1, replica_groups=mesh['azim'=32,'radax'=8] {'azim','radax'}, use_global_device_ids=true, to_apply=%region_5.6 | all-reduce | flops 1 | bytes 8 | tf_op jit(solution)/shard_map/psum | solution.py:63
  259.7 1.3 bitcast_add_fusion
  261.1 1.6 collective-permute-start.15
  262.7 1.3 collective-permute-done.15
  264.0 3.2 collective-permute-done.14
  267.2 0.6 collective-permute-start.16
  267.8 2.4 collective-permute-start.17
  270.3 1.0 collective-permute-done.16
  271.3 2.6 collective-permute-done.17
  273.9 1.9 multiply_reduce_fusion.1
  275.8 76.3 %psum.45 = f32[]{:T(128)} all-reduce(f32[]{:T(128)} %get-tuple-element.10), channel_id=1, replica_groups=mesh['azim'=32,'radax'=8] {'azim','radax'}, use_global_device_ids=true, to_apply=%region_7.8 | all-reduce | flops 1 | bytes 8 | tf_op jit(solution)/shard_map/psum | solution.py:108
  353.4 1.9 multiply_reduce_fusion
  355.4 72.6 %psum.46 = f32[]{:T(128)} all-reduce(f32[]{:T(128)} %multiply_reduce_fusion), channel_id=1, replica_groups=mesh['azim'=32,'radax'=8] {'azim','radax'}, use_global_device_ids=true, to_apply=%region_9.10 | all-reduce | flops 1 | bytes 8 | tf_op jit(solution)/shard_map/psum | solution.py:63
  429.2 1.5 multiply_add_fusion
  430.7 1.6 collective-permute-start.19
  432.3 1.3 collective-permute-done.19
  433.6 2.7 collective-permute-done.18
  436.3 1.2 collective-permute-start.20
  437.5 1.8 collective-permute-start.21
  439.4 1.0 collective-permute-done.20
  440.4 3.2 collective-permute-done.21
  443.6 1.1 fusion.19
  444.7 75.9 %psum.47 = f32[]{:T(128)} all-reduce(f32[]{:T(128)} %fusion.19), channel_id=1, replica_groups=mesh['azim'=32,'radax'=8] {'azim','radax'}, use_global_device_ids=true, to_apply=%region_11.12 | all-reduce | flops 1 | bytes 8 | tf_op jit(solution)/shard_map/psum | solution.py:108
  521.9 1.5 fusion.39
  523.4 0.8 collective-permute-start.23
  524.3 1.3 collective-permute-done.23
  525.6 2.4 collective-permute-done.22
  527.9 0.6 pad_maximum_fusion.58
  528.6 2.5 collective-permute-start.24
  531.0 1.9 copy.34
  533.0 0.7 collective-permute-start.25
  533.6 0.7 broadcast_select_fusion.8
  534.3 4.9 collective-permute-done.25
  539.3 2.9 fusion.14
  542.2 3.2 maximum_subtract_fusion
  545.3 2.7 copy.33
  (71 shorter events, 3.5 us)
Async XLA Ops:
  40.5 7.9 %collective-permute-start.2 = (f32[1,128]{1,0:T(1,128)S(1)}, f32[1,128]{1,0:T(1,128)S(1)}, u32[]{:S(2)}, u32[]{:S(2)}) collective-permute-start(f32[1,128]{1,0:T(1,128)S(1)} %get-tuple-element.44), channel_id=1, source_target_pairs={{0,8},{8,16},{16,24},{24,32},{32,40},{40,48},{48,56},{56,64},{64,7... | collective-permute-start | bytes 1544 | tf_op jit(solution)/shard_map/ppermute | solution.py:20
  40.6 7.8 %collective-permute-start.3 = (f32[1,128]{1,0:T(1,128)S(1)}, f32[1,128]{1,0:T(1,128)S(1)}, u32[]{:S(2)}, u32[]{:S(2)}) collective-permute-start(f32[1,128]{1,0:T(1,128)S(1)} %get-tuple-element.45), channel_id=1, source_target_pairs={{8,0},{16,8},{24,16},{32,24},{40,32},{48,40},{56,48},{64,56},{72,6... | collective-permute-start | bytes 1544 | tf_op jit(solution)/shard_map/ppermute | solution.py:21
  42.7 5.7 %copy-start.13 = (f32[3,8,128]{2,1,0:T(8,128)S(1)}, f32[3,8,128]{2,1,0:T(8,128)}, u32[]{:S(2)}) copy-start(f32[3,8,128]{2,1,0:T(8,128)} %param.7) | copy-start | bytes 36868
  42.7 5.7 %collective-permute-start.1 = (f32[3,1,64,128]{2,3,1,0:T(8,128)S(1)}, f32[3,1,64,128]{2,3,1,0:T(8,128)S(1)}, u32[]{:S(2)}, u32[]{:S(2)}) collective-permute-start(f32[3,1,64,128]{2,3,1,0:T(8,128)S(1)} %get-tuple-element.23), channel_id=1, source_target_pairs={{0,8},{8,16},{16,24},{24,32},{32,40},{40,48},{48,56},{56,64},{64,7... | collective-permute-start | bytes 294920 | tf_op jit(solution)/shard_map/ppermute | solution.py:20
  44.1 5.1 collective-permute-start
  49.9 5.9 %collective-permute-start.4 = (f32[3,10,64,1]{2,3,1,0:T(1,128)}, f32[3,10,64,1]{2,3,1,0:T(1,128)}, u32[]{:S(2)}, u32[]{:S(2)}) collective-permute-start(f32[3,10,64,1]{2,3,1,0:T(1,128)} %get-tuple-element.19), channel_id=1, source_target_pairs={{1,0},{2,1},{3,2},{4,3},{5,4},{6,5},{7,6},{0,7},{9,8},{10,9},{11,1... | collective-permute-start | bytes 23048 | tf_op jit(solution)/shard_map/ppermute | solution.py:21
  55.2 6.5 %collective-permute-start.5 = (f32[3,10,64,1]{2,3,1,0:T(1,128)}, f32[3,10,64,1]{2,3,1,0:T(1,128)S(1)}, u32[]{:S(2)}, u32[]{:S(2)}) collective-permute-start(f32[3,10,64,1]{2,3,1,0:T(1,128)} %get-tuple-element.20), channel_id=1, source_target_pairs={{0,1},{1,2},{2,3},{3,4},{4,5},{5,6},{6,7},{7,0},{8,9},{9,10},{10,1... | collective-permute-start | bytes 23048 | tf_op jit(solution)/shard_map/ppermute | solution.py:20
  61.7 3.1 copy-start.11
  64.9 6.9 %collective-permute-start.7 = (f32[3,1,64,128]{2,3,1,0:T(8,128)S(1)}, f32[3,1,64,128]{2,3,1,0:T(8,128)S(1)}, u32[]{:S(2)}, u32[]{:S(2)}) collective-permute-start(f32[3,1,64,128]{2,3,1,0:T(8,128)S(1)} %get-tuple-element.21), channel_id=1, source_target_pairs={{0,8},{8,16},{16,24},{24,32},{32,40},{40,48},{48,56},{56,64},{64,7... | collective-permute-start | bytes 294920 | tf_op jit(solution)/shard_map/ppermute | solution.py:20
  65.8 6.2 %collective-permute-start.6 = (f32[3,1,64,128]{2,3,1,0:T(8,128)S(1)}, f32[3,1,64,128]{2,3,1,0:T(8,128)S(1)}, u32[]{:S(2)}, u32[]{:S(2)}) collective-permute-start(f32[3,1,64,128]{2,3,1,0:T(8,128)S(1)} %get-tuple-element.22), channel_id=1, source_target_pairs={{8,0},{16,8},{24,16},{32,24},{40,32},{48,40},{56,48},{64,56},{72,6... | collective-permute-start | bytes 294920 | tf_op jit(solution)/shard_map/ppermute | solution.py:21
  72.0 4.5 collective-permute-start.8
  72.1 6.3 %collective-permute-start.9 = (f32[3,10,64,1]{2,3,1,0:T(1,128)S(1)}, f32[3,10,64,1]{2,3,1,0:T(1,128)S(1)}, u32[]{:S(2)}, u32[]{:S(2)}) collective-permute-start(f32[3,10,64,1]{2,3,1,0:T(1,128)S(1)} %get-tuple-element.18), channel_id=1, source_target_pairs={{0,1},{1,2},{2,3},{3,4},{4,5},{5,6},{6,7},{7,0},{8,9},{9,10},{10,1... | collective-permute-start | bytes 23048 | tf_op jit(solution)/shard_map/ppermute | solution.py:20
  79.6 8.6 %copy-start.5 = (f32[1,8,64,128]{2,3,1,0:T(8,128)}, f32[1,8,64,128]{2,3,1,0:T(8,128)S(1)}, u32[]{:S(2)}) copy-start(f32[1,8,64,128]{2,3,1,0:T(8,128)S(1)} %get-tuple-element.15) | copy-start | bytes 786436
  79.6 8.1 %collective-permute-start.11 = (f32[1,1,64,128]{2,3,1,0:T(8,128)S(1)}, f32[1,1,64,128]{2,3,1,0:T(8,128)S(1)}, u32[]{:S(2)}, u32[]{:S(2)}) collective-permute-start(f32[1,1,64,128]{2,3,1,0:T(8,128)S(1)} %get-tuple-element.42), channel_id=1, source_target_pairs={{0,8},{8,16},{16,24},{24,32},{32,40},{40,48},{48,56},{56,64},{64,7... | collective-permute-start | bytes 98312 | tf_op jit(solution)/shard_map/ppermute | solution.py:20
  79.8 8.4 %collective-permute-start.10 = (f32[1,1,64,128]{2,3,1,0:T(8,128)S(1)}, f32[1,1,64,128]{2,3,1,0:T(8,128)S(1)}, u32[]{:S(2)}, u32[]{:S(2)}) collective-permute-start(f32[1,1,64,128]{2,3,1,0:T(8,128)S(1)} %get-tuple-element.43), channel_id=1, source_target_pairs={{8,0},{16,8},{24,16},{32,24},{40,32},{48,40},{56,48},{64,56},{72,6... | collective-permute-start | bytes 98312 | tf_op jit(solution)/shard_map/ppermute | solution.py:21
  87.8 1.0 copy-start.8
  88.2 0.6 copy-start.10
  88.8 4.9 collective-permute-start.12
  90.9 6.3 %collective-permute-start.13 = (f32[1,10,64,1]{2,3,1,0:T(1,128)}, f32[1,10,64,1]{2,3,1,0:T(1,128)S(1)}, u32[]{:S(2)}, u32[]{:S(2)}) collective-permute-start(f32[1,10,64,1]{2,3,1,0:T(1,128)} %get-tuple-element.34), channel_id=1, source_target_pairs={{0,1},{1,2},{2,3},{3,4},{4,5},{5,6},{6,7},{7,0},{8,9},{9,10},{10,1... | collective-permute-start | bytes 7688 | tf_op jit(solution)/shard_map/ppermute | solution.py:20
  259.7 14.2 %copy-start.3 = (f32[8,64,128]{1,2,0:T(8,128)S(1)}, f32[8,64,128]{1,2,0:T(8,128)}, u32[]{:S(2)}) copy-start(f32[8,64,128]{1,2,0:T(8,128)} %copy.32) | copy-start | bytes 786436
  261.0 14.8 %copy-start = (f32[8,64,128]{1,2,0:T(8,128)}, f32[8,64,128]{1,2,0:T(8,128)S(1)}, u32[]{:S(2)}) copy-start(f32[8,64,128]{1,2,0:T(8,128)S(1)} %bitcast_add_fusion) | copy-start | bytes 786436
  261.1 3.0 collective-permute-start.15
  262.7 4.5 collective-permute-start.14
  267.2 4.1 collective-permute-start.16
  267.8 6.1 %collective-permute-start.17 = (f32[1,10,64,1]{2,3,1,0:T(1,128)S(1)}, f32[1,10,64,1]{2,3,1,0:T(1,128)S(1)}, u32[]{:S(2)}, u32[]{:S(2)}) collective-permute-start(f32[1,10,64,1]{2,3,1,0:T(1,128)S(1)} %get-tuple-element.32), channel_id=1, source_target_pairs={{0,1},{1,2},{2,3},{3,4},{4,5},{5,6},{6,7},{7,0},{8,9},{9,10},{10,1... | collective-permute-start | bytes 7688 | tf_op jit(solution)/shard_map/ppermute | solution.py:20
  429.2 14.4 %copy-start.4 = (f32[8,64,128]{1,2,0:T(8,128)S(1)}, f32[8,64,128]{1,2,0:T(8,128)}, u32[]{:S(2)}) copy-start(f32[8,64,128]{1,2,0:T(8,128)} %copy.32) | copy-start | bytes 786436
  430.7 12.9 %copy-start.1 = (f32[8,64,128]{1,2,0:T(8,128)}, f32[8,64,128]{1,2,0:T(8,128)S(1)}, u32[]{:S(2)}) copy-start(f32[8,64,128]{1,2,0:T(8,128)S(1)} %multiply_add_fusion) | copy-start | bytes 786436
  430.7 2.9 collective-permute-start.19
  432.3 4.0 collective-permute-start.18
  436.3 4.1 collective-permute-start.20
  437.5 6.1 %collective-permute-start.21 = (f32[1,10,64,1]{2,3,1,0:T(1,128)S(1)}, f32[1,10,64,1]{2,3,1,0:T(1,128)S(1)}, u32[]{:S(2)}, u32[]{:S(2)}) collective-permute-start(f32[1,10,64,1]{2,3,1,0:T(1,128)S(1)} %get-tuple-element.30), channel_id=1, source_target_pairs={{0,1},{1,2},{2,3},{3,4},{4,5},{5,6},{6,7},{7,0},{8,9},{9,10},{10,1... | collective-permute-start | bytes 7688 | tf_op jit(solution)/shard_map/ppermute | solution.py:20
  523.4 4.5 copy-start.2
  523.4 2.1 collective-permute-start.23
  524.2 3.7 collective-permute-start.22
  525.6 3.0 copy-start.7
  527.9 0.6 copy-start.9
  528.6 5.1 collective-permute-start.24
  533.0 9.2 %copy-start.6 = (f32[8,64,128]{1,2,0:T(8,128)S(1)}, f32[8,64,128]{1,2,0:T(8,128)}, u32[]{:S(2)}) copy-start(f32[8,64,128]{1,2,0:T(8,128)} %copy.30) | copy-start | bytes 786436
  533.0 9.2 %copy-start.12 = (f32[3,10,64,1]{2,3,1,0:T(1,128)S(1)}, f32[3,10,64,1]{2,3,1,0:T(1,128)}, u32[]{:S(2)}) copy-start(f32[3,10,64,1]{2,3,1,0:T(1,128)} %copy-done.11) | copy-start | bytes 23044
  533.0 6.3 %collective-permute-start.25 = (f32[1,10,64,1]{2,3,1,0:T(1,128)}, f32[1,10,64,1]{2,3,1,0:T(1,128)S(1)}, u32[]{:S(2)}, u32[]{:S(2)}) collective-permute-start(f32[1,10,64,1]{2,3,1,0:T(1,128)} %get-tuple-element.28), channel_id=1, source_target_pairs={{0,1},{1,2},{2,3},{3,4},{4,5},{5,6},{6,7},{7,0},{8,9},{9,10},{10,1... | collective-permute-start | bytes 7688 | tf_op jit(solution)/shard_map/ppermute | solution.py:20
where the time goes:
time: 549 us; the launch traced here: 548 us
  blocking collectives  416 us (76%)
  starting transfers between devices  42.1 us (8%)
  waiting for transfers between devices  39.5 us (7%)
  other arithmetic  32.5 us (6%)
  local copies, waits for them, and re-layouts  9.9 us (2%)
  between operations  8.06 us (1%)
    psum x3, blocking collectives, squares(): return lax.psum(jnp.sum(residual * residual), ('azim', 'radax'))  225 us
    psum x2, blocking collectives, per_device(): alpha = norm_now / lax.psum(jnp.sum(direction * image), ('azim', 'radax'))  152 us
    all_gather x1, blocking collectives, per_device(): whole = lax.all_gather(rotor_flux, 'azim', axis=0, tiled=True)  39.2 us
    ppermute x13, waiting for transfers between devices, with_halo(): before = lax.ppermute(last, axis, up)  26 us
    ppermute x13, starting transfers between devices, with_halo(): after = lax.ppermute(first, axis, down)  24.8 us
    ppermute x13, starting transfers between devices, with_halo(): before = lax.ppermute(last, axis, up)  17.3 us
    ppermute x13, waiting for transfers between devices, with_halo(): after = lax.ppermute(first, axis, down)  13.5 us
  transfers between devices with their start and end apart: 26, of which 21 were waited for; matrix products, arithmetic and copies ran while one was open for 2% of the time, Pallas kernels for 0%

commit v1 on v0

v1 whole, which is shorter than its diff:
```python
import jax
import jax.numpy as jnp
from jax import lax
from jax.experimental import pallas as pl
from jax.experimental.pallas import tpu as pltpu
from jax.sharding import PartitionSpec as P


CENTER = 8.0
HALO = 5
STRIP = 8
GROUP = 2 * STRIP
LANES = 128
VMEM_LIMIT = 48 * 1024 * 1024
DEPTHS = (5, 4, 4, 2)
STARTS = (0, 5, 9, 13)
PLANES = 15


def iota(shape, dim):
    return lax.broadcasted_iota(jnp.int32, shape, dim)


def pack_kernel(velocity, damping, weight, rotor, low, high, edge):
    cells = velocity.shape[1]
    rows = velocity.shape[2]
    fields = [velocity.at[0], velocity.at[1], velocity.at[2], damping]
    for field, depth, start in zip(fields, DEPTHS, STARTS):
        low[start : start + depth] = field[0:depth]
        high[start : start + depth] = field[cells - depth : cells]
    for message in (low, high):
        message[PLANES] = jnp.zeros((rows, LANES), jnp.float32)
        for tap in range(3):
            message[PLANES, tap * cells : (tap + 1) * cells] = weight[tap]
    group = iota((8, LANES), 1) // GROUP
    for number, field in enumerate(fields):

        def plane(p, carry):
            packed = jnp.zeros((8, LANES), jnp.float32)
            for t in range(rows // 8):
                tile = field[p, 8 * t : 8 * t + 8]
                turned = pltpu.roll(tile, (STRIP + GROUP * t) % LANES, 1)
                packed = jnp.where(group == t, turned, packed)
            edge[number * cells + p] = packed
            return carry

        lax.fori_loop(0, cells, plane, 0)
    packed = jnp.zeros((8, LANES), jnp.float32)
    for t, tile in enumerate([weight[0], weight[1], weight[2], rotor[...]]):
        turned = pltpu.roll(tile, STRIP + GROUP * t, 1)
        packed = jnp.where(group == t, turned, packed)
    edge[4 * cells] = packed


def corner_kernel(before, after, rotor, halo, low, high, spread):
    cells = rotor.shape[0]
    left = iota((1, 8, LANES), 2) % GROUP < STRIP
    halo[...] = jnp.where(left, before[...], after[...])
    for number, (depth, start) in enumerate(zip(DEPTHS, STARTS)):
        base = number * cells
        low[start : start + depth] = halo[base : base + depth]
        high[start : start + depth] = halo[base + cells - depth : base + cells]
    low[PLANES] = halo[4 * cells]
    high[PLANES] = halo[4 * cells]
    spread[:, 0:8] = jnp.broadcast_to(rotor[...][None], (spread.shape[0], 8, LANES))
    spread[:, 8:16] = jnp.broadcast_to(halo[4 * cells][None], (spread.shape[0], 8, LANES))


def beside(own, other, lane):
    before = pltpu.roll(jnp.where(lane == LANES - 1, other, own), 1, 1)
    after = pltpu.roll(jnp.where(lane == 0, other, own), LANES - 1, 1)
    return before, after


def across(own, row, inner):
    size = own.shape[0]
    inward = jnp.where(row == 0, inner, pltpu.roll(own, 1, 0))
    outward = jnp.where(row == size - 1, 0.0, pltpu.roll(own, size - 1, 0))
    return inward, outward


def fold(block):
    return jnp.sum(block.reshape(block.shape[0] // 8, 8, LANES), axis=0)


def basis_kernel(
    offset,
    velocity,
    damping,
    weight,
    low,
    high,
    halo,
    low_halo,
    high_halo,
    turned,
    predicted,
    base0,
    base1,
    base2,
    edges,
    sums,
    v0,
    v1,
    v2,
    diag,
    p0,
    p1,
    p2,
    s0,
    s1,
    s2,
    taps,
    rims,
    rot,
    face,
):
    cells, rows = damping.shape[0], damping.shape[1]
    blocks = turned.shape[0]
    total = blocks * cells
    place = lax.axis_index("radax")
    last_place = lax.axis_size("radax") - 1
    lane = iota((rows, LANES), 1)
    row = iota((rows, LANES), 0)
    after_ok = jnp.logical_and(lane < HALO, place < last_place)
    before_ok = jnp.logical_and(lane >= LANES - HALO, place > 0)
    mask = jnp.where(jnp.logical_or(after_ok, before_ok), 1.0, 0.0)
    mask8 = mask[0:8] > 0.5

    grown = ((v0, 0), (v1, 1), (v2, 2))
    for field, number in grown:
        depth, start = DEPTHS[number], STARTS[number]
        field[0, 0:depth] = high[start : start + depth]
        field[0, depth : depth + cells] = velocity[number]
        field[0, depth + cells : 2 * depth + cells] = low[start : start + depth]
    shift = 6.0 - CENTER
    depth, start = DEPTHS[3], STARTS[3]
    diag[0, 0:depth] = high[start : start + depth] + shift
    diag[0, depth : depth + cells] = damping[...] + shift
    diag[0, depth + cells : 2 * depth + cells] = low[start : start + depth] + shift

    def open_strip(packed, field, p):
        for t in range(rows // 8):
            tile = pltpu.roll(packed, (LANES - STRIP - GROUP * t) % LANES, 1)
            field[1, p, 8 * t : 8 * t + 8] = jnp.where(mask8, tile, 0.0)

    for number, field in enumerate((v0, v1, v2, diag)):
        depth, start = DEPTHS[number], STARTS[number]
        extra = shift if number == 3 else 0.0

        def outer(p, carry):
            open_strip(high_halo[start + p] + extra, field, p)
            open_strip(low_halo[start + p] + extra, field, depth + cells + p)
            return carry

        def middle(p, carry):
            open_strip(halo[number * cells + p] + extra, field, depth + p)
            return carry

        lax.fori_loop(0, depth, outer, 0)
        lax.fori_loop(0, cells, middle, 0)

    wide = cells + 6
    for tap in range(3):
        at = tap * cells
        taps[tap, 0:3] = high[PLANES, at + cells - 3 : at + cells]
        taps[tap, 3 : 3 + cells] = weight[tap]
        taps[tap, 3 + cells : wide] = low[PLANES, at : at + 3]
    rims[0:3] = high_halo[PLANES, cells - 3 : cells]
    rims[3 : 3 + cells] = halo[4 * cells]
    rims[3 + cells : wide] = low_halo[PLANES, 0:3]
    first = lax.axis_index("azim") * cells - offset[0] - 4 + 2 * total
    for i in range(wide + 2):
        source = lax.rem(first + i, total)
        block = source // cells
        line = lax.rem(source, cells)
        rot[0, i : i + 1] = turned[block, pl.ds(line, 1)]
        rot[1, i : i + 1] = turned[block, pl.ds(line + 8, 1)]
    own_face = jnp.zeros((wide, LANES), jnp.float32)
    rim_face = jnp.zeros((wide, LANES), jnp.float32)
    rim_taps = rims[0:wide]
    for tap in range(3):
        own_face += taps[tap, 0:wide] * rot[0, tap : tap + wide]
        line = pltpu.roll(rot[1, tap : tap + wide], LANES - 3 * GROUP, 1)
        rim_face += pltpu.roll(rim_taps, (LANES - tap * GROUP) % LANES, 1) * line
    face[0, 0:wide] = own_face
    face[1, 0:wide] = pltpu.roll(rim_face, LANES - STRIP, 1)

    def advance(field, speed, p, q, inner0, inner1):
        x, e = field[0, p + 1], field[1, p + 1]
        out = []
        for tile, (own, other, inner) in enumerate(((x, e, inner0), (e, x, inner1))):
            west, east = field[tile, p], field[tile, p + 2]
            before, after = beside(own, other, lane)
            inward, outward = across(own, row, inner)
            wind = speed[tile, q]
            around = (before + after) + (inward + outward)
            around = around + (east + west) - wind * (east - west)
            out.append(0.4 * own + 0.1 * around)
        return out[0], out[1] * mask

    def first_component(p, carry):
        own, rim = advance(v0, v0, p, p + 1, 0.0, 0.0)
        p0[0, p] = own
        p0[1, p] = rim
        return carry

    def other_components(p, carry):
        f0, f1 = face[0, pl.ds(p, 1)], face[1, pl.ds(p, 1)]
        own, rim = advance(v1, v0, p, p + 2, f0, f1)
        p1[0, p] = own
        p1[1, p] = rim
        own, rim = advance(v2, v0, p, p + 2, 0.0, 0.0)
        p2[0, p] = own
        p2[1, p] = rim
        return carry

    lax.fori_loop(0, cells + 8, first_component, 0)
    lax.fori_loop(0, cells + 6, other_components, 0)

    def divergence(p, carry):
        x, e = p2[0, p], p2[1, p]
        for tile, (own, other) in enumerate(((x, e), (e, x))):
            before, after = beside(own, other, lane)
            inward, outward = across(p1[tile, p], row, face[tile, pl.ds(p, 1)])
            value = 0.5 * (
                (p0[tile, p + 2] - p0[tile, p]) + (outward - inward) + (after - before)
            )
            s0[tile, p] = value if tile == 0 else value * mask
        return carry

    lax.fori_loop(0, cells + 6, divergence, 0)

    def apply(field, p, q, tiles):
        x, e = field[0, p + 1], field[1, p + 1]
        pairs = ((x, e), (e, x))
        out = []
        for tile in range(tiles):
            own, other = pairs[tile]
            before, after = beside(own, other, lane)
            inward, outward = across(own, row, 0.0)
            around = (before + after) + (inward + outward)
            around = around + (field[tile, p + 2] + field[tile, p])
            out.append(diag[tile, q] * own - around)
        return out

    def second(p, carry):
        own, rim = apply(s0, p, p, 2)
        s1[0, p] = own
        s1[1, p] = rim * mask
        return carry

    lax.fori_loop(0, cells + 4, second, 0)

    def third(p, carry):
        own, rim = apply(s1, p, p + 1, 2)
        s2[0, p] = own
        s2[1, p] = rim * mask
        return carry

    lax.fori_loop(0, cells + 2, third, 0)

    def products(p, carry):
        (fourth,) = apply(s2, p, p + 2, 1)
        a, b, c = s0[0, p + 3], s1[0, p + 2], s2[0, p + 1]
        pairs = ((a, a), (a, b), (b, b), (b, c), (c, c), (c, fourth))
        predicted[0, p] = p0[0, p + 4]
        predicted[1, p] = p1[0, p + 3]
        predicted[2, p] = p2[0, p + 3]
        edges[0, p] = s0[1, p + 3]
        edges[1, p] = s1[1, p + 2]
        edges[2, p] = s2[1, p + 1]
        return tuple(t + fold(x * y) for t, (x, y) in zip(carry, pairs))

    zero = jnp.zeros((8, LANES), jnp.float32)
    parts = lax.fori_loop(0, cells, products, (zero,) * 6)
    base0[...] = s0[0, 2 : cells + 4]
    base1[...] = s1[0, 1 : cells + 3]
    base2[...] = s2[0, 0 : cells + 2]

    group = iota((1, LANES), 1) // 16
    line = jnp.zeros((1, LANES), jnp.float32)
    for k, part in enumerate(parts):
        part = jnp.sum(part, axis=0, keepdims=True)
        for step in (64, 32, 16):
            part = part + pltpu.roll(part, step, 1)
        line = jnp.where(group == k, part, line)
    sums[...] = jnp.broadcast_to(line[None], sums.shape)


def coefficients(nu):
    def product(x, y):
        total = 0.0
        for i, a in enumerate(x):
            for j, b in enumerate(y):
                total = total + a * b * nu[i + j]
        return total

    def energy(x):
        total = 0.0
        for i, a in enumerate(x):
            for j, b in enumerate(x):
                total = total + a * b * (nu[i + j + 1] + CENTER * nu[i + j])
        return total

    def image(x):
        out = [CENTER * a for a in x] + [0.0 * x[0]]
        return [out[0]] + [out[i + 1] + x[i] for i in range(len(x))]

    def length(norm, bottom):
        return jnp.clip(norm / bottom, 0.0624, 2.01)

    one = jnp.ones_like(nu[0])
    residual, direction, norm = [one], [one], nu[0]
    answer = [0.0 * one] * 3
    for step in range(3):
        alpha = length(norm, energy(direction))
        answer = [
            a + alpha * direction[i] if i < len(direction) else a for i, a in enumerate(answer)
        ]
        if step == 2:
            break
        moved = image(direction)
        residual = residual + [0.0 * one] * (len(moved) - len(residual))
        residual = [r - alpha * m for r, m in zip(residual, moved)]
        after = product(residual, residual)
        beta = after / norm
        padded = direction + [0.0 * one]
        direction = [r + beta * d for r, d in zip(residual, padded)]
        norm = after
    return answer


def project_kernel(sums, predicted, base0, base1, base2, edges, velocity, pressure, grown):
    cells, rows = pressure.shape[0], pressure.shape[1]
    lane = iota((rows, LANES), 1)
    row = iota((rows, LANES), 0)
    line = jnp.sum(sums[...], axis=0)
    group = iota((1, LANES), 1) // 16
    nu = [
        jnp.sum(jnp.where(group == k, line, 0.0), axis=1, keepdims=True) for k in range(6)
    ]
    c0, c1, c2 = coefficients(nu)

    def combine(p, carry):
        grown[p] = c0 * base0[p] + c1 * base1[p] + c2 * base2[p]
        return carry

    lax.fori_loop(0, cells + 2, combine, 0)

    def gradient(p, carry):
        own = grown[p + 1]
        other = c0 * edges[0, p] + c1 * edges[1, p] + c2 * edges[2, p]
        before, after = beside(own, other, lane)
        inward, outward = across(own, row, 0.0)
        pressure[p] = own
        velocity[0, p] = predicted[0, p] - 0.5 * (grown[p + 2] - grown[p])
        velocity[1, p] = predicted[1, p] - 0.5 * (outward - inward)
        velocity[2, p] = predicted[2, p] - 0.5 * (after - before)
        return carry

    lax.fori_loop(0, cells, gradient, 0)


def call(kernel, shapes, scratch=(), scalars=0, operands=()):
    spec = pl.BlockSpec(memory_space=pltpu.VMEM)
    scalar = pl.BlockSpec(memory_space=pltpu.SMEM)
    specs = [scalar] * scalars + [spec] * (len(operands) - scalars)
    return pl.pallas_call(
        kernel,
        out_shape=[jax.ShapeDtypeStruct(s, jnp.float32) for s in shapes],
        in_specs=specs,
        out_specs=[spec] * len(shapes),
        scratch_shapes=[pltpu.VMEM(s, jnp.float32) for s in scratch],
        compiler_params=pltpu.CompilerParams(vmem_limit_bytes=VMEM_LIMIT),
    )(*operands)


def swap(low, high, axis):
    count = lax.axis_size(axis)
    up = [(i, (i + 1) % count) for i in range(count)]
    down = [(j, i) for i, j in up]
    return lax.ppermute(high, axis, up), lax.ppermute(low, axis, down)


def per_device(velocity, rotor_flux, correlation_weight, damping, offset):
    cells, rows = damping.shape[0], damping.shape[1]
    azim = lax.axis_size("azim")
    devices = azim * lax.axis_size("radax")
    message = (PLANES + 1, rows, LANES)
    strips = (4 * cells + 1, 8, LANES)
    low, high, edge = call(
        pack_kernel,
        [message, message, strips],
        operands=(velocity, damping, correlation_weight, rotor_flux),
    )
    before, after = swap(edge, edge, "radax")
    from_low, from_high = swap(low, high, "azim")
    corner = (PLANES + 1, 8, LANES)
    halo, low, high, spread = call(
        corner_kernel,
        [strips, corner, corner, (azim, 16, LANES)],
        operands=(before, after, rotor_flux),
    )
    low_halo, high_halo = swap(low, high, "azim")
    turned = lax.all_to_all(spread, "azim", 0, 0, tiled=True)
    plane = (rows, LANES)
    own = (cells + 2,) + plane
    predicted, base0, base1, base2, edges, sums = call(
        basis_kernel,
        [(3, cells) + plane, own, own, own, (3, cells) + plane, (devices, 1, LANES)],
        scratch=[
            (2, cells + 10) + plane,
            (2, cells + 8) + plane,
            (2, cells + 8) + plane,
            (2, cells + 4) + plane,
            (2, cells + 8) + plane,
            (2, cells + 6) + plane,
            (2, cells + 6) + plane,
            (2, cells + 6) + plane,
            (2, cells + 4) + plane,
            (2, cells + 2) + plane,
            (3, cells + 8, LANES),
            (cells + 8, LANES),
            (2, cells + 8, LANES),
            (2, cells + 8, LANES),
        ],
        scalars=1,
        operands=(
            offset,
            velocity,
            damping,
            correlation_weight,
            from_high,
            from_low,
            halo,
            high_halo,
            low_halo,
            turned,
        ),
    )
    sums = lax.all_to_all(sums, ("azim", "radax"), 0, 0, tiled=True)
    return call(
        project_kernel,
        [(3, cells) + plane, (cells,) + plane],
        scratch=[own],
        operands=(sums, predicted, base0, base1, base2, edges),
    )


def solution(mesh):
    in_specs = (
        P(None, "azim", None, "radax"),
        P("azim", "radax"),
        P(None, "azim", "radax"),
        P("azim", None, "radax"),
        P(),
    )
    out_specs = (P(None, "azim", None, "radax"), P("azim", None, "radax"))

    def run(*args):
        return tuple(per_device(*args))

    return jax.shard_map(run, mesh=mesh, in_specs=in_specs, out_specs=out_specs, check_vma=False)
```

time: 549 us -> 85.2 us (0.16)
  blocking collectives: 416 us -> 23.5 us
  other arithmetic: 32.5 us -> 0 us
  starting transfers between devices: 42.1 us -> 20.2 us
  waiting for transfers between devices: 39.5 us -> 17.6 us
  Pallas kernels: 0 us -> 18.8 us
  between operations: 8.06 us -> 1.32 us
  local copies, waits for them, and re-layouts: 9.9 us -> 3.48 us
    psum x5 -> x0, blocking collectives: 377 us -> none  [the longest x3 225 us: squares(): return lax.psum(jnp.sum(residual * residual), ('azim', 'radax'))]
    all_gather x1 -> x0, blocking collectives: 39.2 us -> none  [per_device(): whole = lax.all_gather(rotor_flux, 'azim', axis=0, tiled=True)]
    ppermute x26 -> x6, starting transfers between devices: 42.1 us -> 9.51 us  [swap(): return (lax.ppermute(high, axis, up), lax.ppermute(low, axis, down))]
    ppermute x26 -> x6, waiting for transfers between devices: 39.5 us -> 11.1 us  [swap(): return (lax.ppermute(high, axis, up), lax.ppermute(low, axis, down))]
    all_to_all x0 -> x1, blocking collectives: none -> 23.5 us  [per_device(): sums = lax.all_to_all(sums, ('azim', 'radax'), 0, 0, tiled=True)]
    pallas_call x0 -> x4, Pallas kernels: none -> 18.8 us  [call(): pl.pallas_call(kernel, out_shape=[jax.ShapeDtypeStruct(s, jnp.float32) fo...]
    reduce_sum x5 -> x0, other arithmetic: 12.7 us -> none  [the longest x3 7.95 us: per_device(): alpha = norm_now / lax.psum(jnp.sum(direction * image), ('azim', 'radax'))]
    all_to_all x0 -> x1, starting transfers between devices: none -> 10.7 us  [per_device(): turned = lax.all_to_all(spread, 'azim', 0, 0, tiled=True)]
  transfers between devices with their start and end apart: 26 -> 7, of which waited for: 21 -> 5; matrix products, arithmetic and copies ran while one was open for 2% -> 0% of each run, Pallas kernels for 0% -> 1%
where the time goes in v1:
time: 85.2 us; the launch traced here: 84.9 us
  blocking collectives  23.5 us (28%)
  starting transfers between devices  20.2 us (24%)
  Pallas kernels  18.8 us (22%)
  waiting for transfers between devices  17.6 us (21%)
  local copies, waits for them, and re-layouts  3.48 us (4%)
  between operations  1.32 us (2%)
    all_to_all x1, blocking collectives, per_device(): sums = lax.all_to_all(sums, ('azim', 'radax'), 0, 0, tiled=True)  23.5 us
    pallas_call x4, Pallas kernels, call(): pl.pallas_call(kernel, out_shape=[jax.ShapeDtypeStruct(s, jnp.float32) fo...  18.8 us
    ppermute x6, waiting for transfers between devices, swap(): return (lax.ppermute(high, axis, up), lax.ppermute(low, axis, down))  11.1 us
    all_to_all x1, starting transfers between devices, per_device(): turned = lax.all_to_all(spread, 'azim', 0, 0, tiled=True)  10.7 us
    ppermute x6, starting transfers between devices, swap(): return (lax.ppermute(high, axis, up), lax.ppermute(low, axis, down))  9.51 us
    all_to_all x1, waiting for transfers between devices, per_device(): turned = lax.all_to_all(spread, 'azim', 0, 0, tiled=True)  6.52 us
    unnamed x14, local copies, waits for them, and re-layouts  3.48 us
  transfers between devices with their start and end apart: 7, of which 5 were waited for; matrix products, arithmetic and copies ran while one was open for 0% of the time, Pallas kernels for 1%

profile of v1, /device:TPU:1, one launch (start us, length us, event | category | flops | bytes accessed | tf_op | source)
XLA Modules:
  0.0 84.9 jit_solution(12826717328527683763)
XLA Ops:
  0.6 0.0 copy-start
  0.6 1.1 %copy-done = f32[3,8,64,128]{3,2,1,0:T(8,128)S(1)} copy-done((f32[3,8,64,128]{3,2,1,0:T(8,128)S(1)}, f32[3,8,64,128]{3,2,1,0:T(8,128)}, u32[]{:S(2)}) %copy-start) | copy-done | bytes 786456
  1.8 0.0 copy-start.2
  1.8 0.9 %copy-done.2 = f32[8,64,128]{2,1,0:T(8,128)S(1)} copy-done((f32[8,64,128]{2,1,0:T(8,128)S(1)}, f32[8,64,128]{2,1,0:T(8,128)}, u32[]{:S(2)}) %copy-start.2) | copy-done | bytes 262168
  2.7 0.0 copy-start.4
  2.7 0.7 copy-done.4
  3.4 0.0 copy-start.6
  3.4 0.7 copy-done.6
  4.1 0.0 copy-start.1
  4.1 3.2 %shard_map.68 = (f32[16,64,128]{2,1,0:T(8,128)}, f32[16,64,128]{2,1,0:T(8,128)S(1)}, f32[33,8,128]{2,1,0:T(8,128)S(1)}) custom-call(f32[3,8,64,128]{3,2,1,0:T(8,128)S(1)} %copy-done, f32[8,64,128]{2,1,0:T(8,128)S(1)} %copy-done.2, f32[3,8,128]{2,1,0:T(8,128)S(1)} %copy-done.4, f32[8,128]{1,0:T(8,128)S(1)} %copy-done.6), custom_call_target="tpu_custom_call" | custom-call | tf_op jit(solution)/shard_map/pallas_call | solution.py:369
  7.3 5.9 %collective-permute-start.3 = (f32[33,8,128]{2,1,0:T(8,128)S(1)}, f32[33,8,128]{2,1,0:T(8,128)S(1)}, u32[]{:S(2)}, u32[]{:S(2)}) collective-permute-start(f32[33,8,128]{2,1,0:T(8,128)S(1)} %get-tuple-element.17), channel_id=1, source_target_pairs={{1,0},{2,1},{3,2},{4,3},{5,4},{6,5},{7,6},{0,7},{9,8},{10,9},{11,1... | collective-permute-start | bytes 405512 | tf_op jit(solution)/shard_map/ppermute | solution.py:383
  13.3 0.0 collective-permute-start.2
  13.3 1.0 %collective-permute-start = (f32[16,64,128]{2,1,0:T(8,128)}, f32[16,64,128]{2,1,0:T(8,128)S(1)}, u32[]{:S(2)}, u32[]{:S(2)}) collective-permute-start(f32[16,64,128]{2,1,0:T(8,128)} %get-tuple-element.15), channel_id=1, source_target_pairs={{8,0},{16,8},{24,16},{32,24},{40,32},{48,40},{56,48},{64,56},{72,6... | collective-permute-start | bytes 1572872 | tf_op jit(solution)/shard_map/ppermute | solution.py:383
  14.2 0.8 collective-permute-start.1
  15.0 0.5 collective-permute-done.3.after
  15.5 8.3 %collective-permute-done.2.before = f32[33,8,128]{2,1,0:T(8,128)S(1)} collective-permute-done((f32[33,8,128]{2,1,0:T(8,128)S(1)}, f32[33,8,128]{2,1,0:T(8,128)S(1)}, u32[]{:S(2)}, u32[]{:S(2)}) %collective-permute-start.2) | collective-permute-done | bytes 135200 | tf_op jit(solution)/shard_map/ppermute | solution.py:383
  23.8 0.7 shard_map.69
  24.5 0.0 copy-start.3
  24.5 0.0 copy-start.5
  24.5 10.7 %all-to-all-start = ((f32[32,16,128]{2,1,0:T(8,128)}), f32[32,16,128]{2,1,0:T(8,128)S(1)}, u32[]{:S(2)}, u32[]{:S(2)}) async-start(f32[32,16,128]{2,1,0:T(8,128)} %get-tuple-element.21), calls=%async_computation | async-start | bytes 524288 | tf_op jit(solution)/shard_map/all_to_all | solution.py:406
  35.2 0.3 collective-permute-start.4
  35.5 1.5 %collective-permute-start.5 = (f32[16,8,128]{2,1,0:T(8,128)S(1)}, f32[16,8,128]{2,1,0:T(8,128)S(1)}, u32[]{:S(2)}, u32[]{:S(2)}) collective-permute-start(f32[16,8,128]{2,1,0:T(8,128)S(1)} %get-tuple-element.20), channel_id=1, source_target_pairs={{0,8},{8,16},{16,24},{24,32},{32,40},{40,48},{48,56},{56,64},{64,7... | collective-permute-start | bytes 196616 | tf_op jit(solution)/shard_map/ppermute | solution.py:383
  37.7 1.7 %collective-permute-done.4.low_halo = f32[16,8,128]{2,1,0:T(8,128)S(1)} collective-permute-done((f32[16,8,128]{2,1,0:T(8,128)S(1)}, f32[16,8,128]{2,1,0:T(8,128)S(1)}, u32[]{:S(2)}, u32[]{:S(2)}) %collective-permute-start.4) | collective-permute-done | bytes 65568 | tf_op jit(solution)/shard_map/ppermute | solution.py:383
  39.4 0.7 collective-permute-done.5.high_halo
  40.0 0.0 collective-permute-done.low
  40.0 0.0 collective-permute-done.1.high
  40.0 6.5 %all-to-all-done.turned = f32[32,16,128]{2,1,0:T(8,128)S(1)} async-done(((f32[32,16,128]{2,1,0:T(8,128)}), f32[32,16,128]{2,1,0:T(8,128)S(1)}, u32[]{:S(2)}, u32[]{:S(2)}) %all-to-all-start) | async-done | bytes 262176 | tf_op jit(solution)/shard_map/all_to_all | solution.py:406
  46.5 0.0 copy-done.1
  46.5 0.0 copy-done.3
  46.5 0.0 copy-done.5
  46.5 12.7 %shard_map.70 = (f32[3,8,64,128]{3,2,1,0:T(8,128)S(1)}, f32[10,64,128]{2,1,0:T(8,128)S(1)}, f32[10,64,128]{2,1,0:T(8,128)S(1)}, f32[10,64,128]{2,1,0:T(8,128)S(1...) custom-call(s32[1]{0:T(128)S(6)} %copy.7.offset, f32[3,8,64,128]{3,2,1,0:T(8,128)S(1)} %copy-done.1, ...), custom_call_target="tpu_custom_call" | custom-call | tf_op jit(solution)/shard_map/pallas_call | solution.py:369
  59.2 23.5 %all_to_all.10.sums = f32[256,1,128]{2,1,0:T(1,128)S(1)} all-to-all(f32[256,1,128]{2,1,0:T(1,128)S(1)} %get-tuple-element.22), channel_id=1, replica_groups=mesh['azim'=32,'radax'=8] {'azim','radax'}, dimensions={0} | all-to-all | bytes 262144 | tf_op jit(solution)/shard_map/all_to_all | solution.py:442
  82.7 2.2 %shard_map.71 = (f32[3,8,64,128]{3,2,1,0:T(8,128)}, f32[8,64,128]{2,1,0:T(8,128)}) custom-call(f32[256,1,128]{2,1,0:T(1,128)S(1)} %all_to_all.10.sums, f32[3,8,64,128]{3,2,1,0:T(8,128)S(1)} %get-tuple-element.23.predicted, f32[10,64,128]{2,1,0:T(8,128)S(1)} %get-tuple-element.24.base0, f32[10,64,128]{2,1,0:T(8,128)S(1)} %get-tuple-element.25.base1, ...), custom_call_target="tpu_custom_call" | custom-call | tf_op jit(solution)/shard_map/pallas_call | solution.py:369
Async XLA Ops:
  0.6 1.1 %copy-start = (f32[3,8,64,128]{3,2,1,0:T(8,128)S(1)}, f32[3,8,64,128]{3,2,1,0:T(8,128)}, u32[]{:S(2)}) copy-start(f32[3,8,64,128]{3,2,1,0:T(8,128)} %velocity.3) | copy-start | bytes 2359300
  1.8 0.9 %copy-start.2 = (f32[8,64,128]{2,1,0:T(8,128)S(1)}, f32[8,64,128]{2,1,0:T(8,128)}, u32[]{:S(2)}) copy-start(f32[8,64,128]{2,1,0:T(8,128)} %damping.3) | copy-start | bytes 786436
  2.7 0.7 copy-start.4
  3.4 0.7 copy-start.6
  4.1 42.4 %copy-start.1 = (f32[3,8,64,128]{3,2,1,0:T(8,128)S(1)}, f32[3,8,64,128]{3,2,1,0:T(8,128)}, u32[]{:S(2)}) copy-start(f32[3,8,64,128]{3,2,1,0:T(8,128)} %velocity.3) | copy-start | bytes 2359300
  7.3 8.2 %collective-permute-start.3 = (f32[33,8,128]{2,1,0:T(8,128)S(1)}, f32[33,8,128]{2,1,0:T(8,128)S(1)}, u32[]{:S(2)}, u32[]{:S(2)}) collective-permute-start(f32[33,8,128]{2,1,0:T(8,128)S(1)} %get-tuple-element.17), channel_id=1, source_target_pairs={{1,0},{2,1},{3,2},{4,3},{5,4},{6,5},{7,6},{0,7},{9,8},{10,9},{11,1... | collective-permute-start | bytes 405512 | tf_op jit(solution)/shard_map/ppermute | solution.py:383
  13.3 10.5 %collective-permute-start.2 = (f32[33,8,128]{2,1,0:T(8,128)S(1)}, f32[33,8,128]{2,1,0:T(8,128)S(1)}, u32[]{:S(2)}, u32[]{:S(2)}) collective-permute-start(f32[33,8,128]{2,1,0:T(8,128)S(1)} %get-tuple-element.17), channel_id=1, source_target_pairs={{0,1},{1,2},{2,3},{3,4},{4,5},{5,6},{6,7},{7,0},{8,9},{9,10},{10,1... | collective-permute-start | bytes 405512 | tf_op jit(solution)/shard_map/ppermute | solution.py:383
  13.3 26.7 %collective-permute-start = (f32[16,64,128]{2,1,0:T(8,128)}, f32[16,64,128]{2,1,0:T(8,128)S(1)}, u32[]{:S(2)}, u32[]{:S(2)}) collective-permute-start(f32[16,64,128]{2,1,0:T(8,128)} %get-tuple-element.15), channel_id=1, source_target_pairs={{8,0},{16,8},{24,16},{32,24},{40,32},{48,40},{56,48},{64,56},{72,6... | collective-permute-start | bytes 1572872 | tf_op jit(solution)/shard_map/ppermute | solution.py:383
  14.2 25.8 %collective-permute-start.1 = (f32[16,64,128]{2,1,0:T(8,128)S(1)}, f32[16,64,128]{2,1,0:T(8,128)S(1)}, u32[]{:S(2)}, u32[]{:S(2)}) collective-permute-start(f32[16,64,128]{2,1,0:T(8,128)S(1)} %get-tuple-element.16), channel_id=1, source_target_pairs={{0,8},{8,16},{16,24},{24,32},{32,40},{40,48},{48,56},{56,64},{64,7... | collective-permute-start | bytes 1572872 | tf_op jit(solution)/shard_map/ppermute | solution.py:383
  24.5 22.0 %copy-start.3 = (f32[8,64,128]{2,1,0:T(8,128)S(1)}, f32[8,64,128]{2,1,0:T(8,128)}, u32[]{:S(2)}) copy-start(f32[8,64,128]{2,1,0:T(8,128)} %damping.3) | copy-start | bytes 786436
  24.5 22.0 %copy-start.5 = (f32[3,8,128]{2,1,0:T(8,128)S(1)}, f32[3,8,128]{2,1,0:T(8,128)}, u32[]{:S(2)}) copy-start(f32[3,8,128]{2,1,0:T(8,128)} %weight.3) | copy-start | bytes 36868
  24.5 22.0 %all-to-all-start = ((f32[32,16,128]{2,1,0:T(8,128)}), f32[32,16,128]{2,1,0:T(8,128)S(1)}, u32[]{:S(2)}, u32[]{:S(2)}) async-start(f32[32,16,128]{2,1,0:T(8,128)} %get-tuple-element.21), calls=%async_computation | async-start | bytes 524288 | tf_op jit(solution)/shard_map/all_to_all | solution.py:406
  35.2 4.1 %collective-permute-start.4 = (f32[16,8,128]{2,1,0:T(8,128)S(1)}, f32[16,8,128]{2,1,0:T(8,128)S(1)}, u32[]{:S(2)}, u32[]{:S(2)}) collective-permute-start(f32[16,8,128]{2,1,0:T(8,128)S(1)} %get-tuple-element.19), channel_id=1, source_target_pairs={{8,0},{16,8},{24,16},{32,24},{40,32},{48,40},{56,48},{64,56},{72,6... | collective-permute-start | bytes 196616 | tf_op jit(solution)/shard_map/ppermute | solution.py:383
  35.5 4.5 %collective-permute-start.5 = (f32[16,8,128]{2,1,0:T(8,128)S(1)}, f32[16,8,128]{2,1,0:T(8,128)S(1)}, u32[]{:S(2)}, u32[]{:S(2)}) collective-permute-start(f32[16,8,128]{2,1,0:T(8,128)S(1)} %get-tuple-element.20), channel_id=1, source_target_pairs={{0,8},{8,16},{16,24},{24,32},{32,40},{40,48},{48,56},{56,64},{64,7... | collective-permute-start | bytes 196616 | tf_op jit(solution)/shard_map/ppermute | solution.py:383

commit v2 on v1

v2 whole, which is shorter than its diff:
```python
import jax
import jax.numpy as jnp
from jax import lax
from jax.experimental import pallas as pl
from jax.experimental.pallas import tpu as pltpu
from jax.sharding import PartitionSpec as P


CENTER = 8.0
HALO = 5
STRIP = 8
GROUP = 2 * STRIP
LANES = 128
VMEM_LIMIT = 48 * 1024 * 1024
DEPTHS = (5, 4, 4, 2)
STARTS = (0, 5, 9, 13)
PLANES = 15
PAD = 8


def iota(shape, dim):
    return lax.broadcasted_iota(jnp.int32, shape, dim)


def merge(parts, slot):
    out = parts[0]
    for k, part in enumerate(parts[1:], 1):
        out = jnp.where(slot == k, part, out)
    return out


def spin(tile, steps):
    return pltpu.roll(tile, steps % LANES, 1) if steps % LANES else tile


def edge_kernel(velocity, damping, weight, rotor, to_left, to_right, vel, damp, wt, rt, sems):
    cells, rows = damping.shape[0], damping.shape[1]
    copies = [
        pltpu.make_async_copy(velocity.at[0], vel.at[0], sems.at[0]),
        pltpu.make_async_copy(velocity.at[1], vel.at[1], sems.at[1]),
        pltpu.make_async_copy(velocity.at[2], vel.at[2], sems.at[2]),
        pltpu.make_async_copy(damping, damp, sems.at[3]),
        pltpu.make_async_copy(weight, wt, sems.at[4]),
        pltpu.make_async_copy(rotor, rt, sems.at[5]),
    ]
    for copy in copies:
        copy.start()
    lane = iota((8, LANES), 1)
    group = lane // GROUP
    within = lane % GROUP
    slot = (
        (within >= 4).astype(jnp.int32)
        + (within >= 8).astype(jnp.int32)
        + (within >= 13).astype(jnp.int32)
    )
    fields = [vel.at[0], vel.at[1], vel.at[2], damp]

    def pack(field, p):
        return merge(
            [
                spin(field[p, 8 * t : 8 * t + 8], STRIP + GROUP * t)
                for t in range(rows // 8)
            ],
            group,
        )

    for copy in copies:
        copy.wait()
    for p in range(cells):
        packed = [pack(field, p) for field in fields]
        to_right[p] = merge([spin(x, k) for x, k in zip(packed, (-4, 0, 5, 7))], slot)
        to_left[p] = merge([spin(x, k) for x, k in zip(packed, (-8, -4, 0, 5))], slot)
    tiles = [wt[0], wt[1], wt[2], rt[...]]
    packed = merge([spin(x, STRIP + GROUP * t) for t, x in enumerate(tiles)], group)
    to_right[cells] = packed
    to_left[cells] = packed


def plane_kernel(velocity, damping, weight, order, low, high, sems):
    cells, rows = damping.shape[0], damping.shape[1]
    fields = [velocity.at[0], velocity.at[1], velocity.at[2], damping]
    copies = []
    for field, depth, start in zip(fields, DEPTHS, STARTS):
        copies.append((field.at[0:depth], low.at[start : start + depth]))
        copies.append((field.at[cells - depth : cells], high.at[start : start + depth]))
    for tap in range(3):
        for message in (low, high):
            copies.append((weight.at[tap], message.at[PLANES, tap * cells : (tap + 1) * cells]))
    copies = [
        pltpu.make_async_copy(source, target, sems.at[k])
        for k, (source, target) in enumerate(copies)
    ]
    for copy in copies:
        copy.start()
    for copy in copies:
        copy.wait()


def corner_kernel(before, after, rotor, low, high, spread):
    cells = rotor.shape[0]
    depth = HALO
    for k, side in enumerate((before, after)):
        low[k, 0:depth] = side[0:depth]
        high[k, 0:depth] = side[cells - depth : cells]
    within = iota((8, LANES), 1) % GROUP
    lines = jnp.where(within < STRIP, before[cells], after[cells])
    for message in (low, high):
        message[0, depth] = lines
        message[1, depth] = lines
    own = rotor[...]
    for k in range(spread.shape[0]):
        spread[k, 0:8] = own
        spread[k, 8:16] = lines


def beside(own, other, lane):
    before = pltpu.roll(jnp.where(lane == LANES - 1, other, own), 1, 1)
    after = pltpu.roll(jnp.where(lane == 0, other, own), LANES - 1, 1)
    return before, after


def basis_kernel(
    offset,
    velocity,
    damping,
    weight,
    low,
    high,
    before_own,
    after_own,
    low_halo,
    high_halo,
    turned,
    predicted,
    base0,
    base1,
    base2,
    edges,
    sums,
    v0,
    v1,
    v2,
    diag,
    p0,
    p1,
    p2,
    s0,
    s1,
    s2,
    taps,
    rims,
    rot,
    face,
):
    cells, rows = damping.shape[0], damping.shape[1]
    blocks = turned.shape[0]
    total = blocks * cells
    tiles = range(rows // 8)
    place = lax.axis_index("radax")
    last_place = lax.axis_size("radax") - 1
    lane = iota((8, LANES), 1)
    within = lane % GROUP
    after_ok = jnp.logical_and(lane < HALO, place < last_place)
    before_ok = jnp.logical_and(lane >= LANES - HALO, place > 0)
    keep = jnp.logical_or(after_ok, before_ok)
    zero = jnp.zeros((8, LANES), jnp.float32)

    def at(t, shift=0):
        return slice(PAD + 8 * t + shift, PAD + 8 * t + 8 + shift)

    for field in (v0, v1, v2, p1, s0, s1, s2):
        planes = field.shape[1]
        for tile in range(2):

            def clear(p, carry):
                field[tile, p, 0:PAD] = zero
                field[tile, p, PAD + rows : PAD + rows + PAD] = zero
                return carry

            lax.fori_loop(0, planes, clear, 0, unroll=4)

    body = slice(PAD, PAD + rows)
    for number, field in enumerate((v0, v1, v2)):
        depth, start = DEPTHS[number], STARTS[number]
        for p in range(depth):
            field[0, p, body] = high[start + p]
            field[0, depth + cells + p, body] = low[start + p]

        def fill(p, carry):
            field[0, depth + p, body] = velocity[number, p]
            return carry

        lax.fori_loop(0, cells, fill, 0, unroll=4)
    shift = 6.0 - CENTER
    depth, start = DEPTHS[3], STARTS[3]
    for p in range(depth):
        diag[0, p] = high[start + p] + shift
        diag[0, depth + cells + p] = low[start + p] + shift

    def fill_diag(p, carry):
        diag[0, depth + p] = damping[p] + shift
        return carry

    lax.fori_loop(0, cells, fill_diag, 0, unroll=4)

    turns = ((4, 8), (0, 4), (-5, 0), (-7, -5))

    def open_strips(before, after, plane, numbers):
        for number in numbers:
            field, (a, b) = (v0, v1, v2, diag)[number], turns[number]
            strip = jnp.where(within < STRIP, spin(before, a), spin(after, b))
            q = plane + DEPTHS[number]
            for t in tiles:
                tile = jnp.where(keep, spin(strip, -STRIP - GROUP * t), 0.0)
                if number == 3:
                    field[1, q, 8 * t : 8 * t + 8] = tile + shift
                else:
                    field[1, q, at(t)] = tile

    for k in range(HALO):
        numbers = [n for n in range(4) if DEPTHS[n] >= HALO - k]
        open_strips(high_halo[0, k], high_halo[1, k], k - HALO, numbers)
        numbers = [n for n in range(4) if DEPTHS[n] > k]
        open_strips(low_halo[0, k], low_halo[1, k], cells + k, numbers)

    def middle(p, carry):
        open_strips(before_own[p], after_own[p], p, range(4))
        return carry

    lax.fori_loop(0, cells, middle, 0, unroll=4)

    wide = cells + 6
    for tap in range(3):
        line = tap * cells
        taps[tap, 0:3] = high[PLANES, line + cells - 3 : line + cells]
        taps[tap, 3 : 3 + cells] = weight[tap]
        taps[tap, 3 + cells : wide] = low[PLANES, line : line + 3]
    rims[0:3] = high_halo[0, HALO, cells - 3 : cells]
    rims[3 : 3 + cells] = jnp.where(within < STRIP, before_own[cells], after_own[cells])
    rims[3 + cells : wide] = low_halo[0, HALO, 0:3]
    first = lax.axis_index("azim") * cells - offset[0] - 4 + 2 * total
    for i in range(wide + 2):
        source = lax.rem(first + i, total)
        block = source // cells
        line = lax.rem(source, cells)
        rot[0, i : i + 1] = turned[block, pl.ds(line, 1)]
        rot[1, i : i + 1] = turned[block, pl.ds(line + 8, 1)]
    own_face = jnp.zeros((wide, LANES), jnp.float32)
    rim_face = jnp.zeros((wide, LANES), jnp.float32)
    rim_taps = rims[0:wide]
    for tap in range(3):
        own_face += taps[tap, 0:wide] * rot[0, tap : tap + wide]
        rim_face += spin(rim_taps, -tap * GROUP) * spin(rot[1, tap : tap + wide], -3 * GROUP)
    face[0, 0:wide] = own_face
    face[1, 0:wide] = spin(rim_face, -STRIP)

    def set_face(p, carry):
        for tile in range(2):
            line = face[tile, pl.ds(p, 1)]
            v1[tile, p + 1, PAD - 1 : PAD] = line
            p1[tile, p, PAD - 1 : PAD] = line
        return carry

    lax.fori_loop(0, wide, set_face, 0, unroll=4)

    def pair(field, p, t):
        x, e = field[0, p, at(t)], field[1, p, at(t)]
        return (x, e), (e, x)

    def advance(field, speed, p, q, t):
        out = []
        for tile, (own, other) in enumerate(pair(field, p + 1, t)):
            west, east = field[tile, p, at(t)], field[tile, p + 2, at(t)]
            before, after = beside(own, other, lane)
            inward, outward = field[tile, p + 1, at(t, -1)], field[tile, p + 1, at(t, 1)]
            wind = speed[tile, q, at(t)]
            around = (before + after) + (inward + outward)
            around = around + ((east + west) - wind * (east - west))
            out.append(0.4 * own + 0.1 * around)
        return out[0], jnp.where(keep, out[1], 0.0)

    def first_component(p, carry):
        for t in tiles:
            own, rim = advance(v0, v0, p, p + 1, t)
            p0[0, p, at(t, -PAD)] = own
            p0[1, p, at(t, -PAD)] = rim
        return carry

    def other_components(p, carry):
        for t in tiles:
            own, rim = advance(v1, v0, p, p + 2, t)
            p1[0, p, at(t)] = own
            p1[1, p, at(t)] = rim
            own, rim = advance(v2, v0, p, p + 2, t)
            p2[0, p, at(t, -PAD)] = own
            p2[1, p, at(t, -PAD)] = rim
        return carry

    lax.fori_loop(0, cells + 8, first_component, 0, unroll=4)
    lax.fori_loop(0, cells + 6, other_components, 0)

    def divergence(p, carry):
        for t in tiles:
            x, e = p2[0, p, at(t, -PAD)], p2[1, p, at(t, -PAD)]
            for tile, (own, other) in enumerate(((x, e), (e, x))):
                before, after = beside(own, other, lane)
                inward, outward = p1[tile, p, at(t, -1)], p1[tile, p, at(t, 1)]
                west, east = p0[tile, p, at(t, -PAD)], p0[tile, p + 2, at(t, -PAD)]
                value = 0.5 * ((east - west) + (outward - inward) + (after - before))
                s0[tile, p, at(t)] = value if tile == 0 else jnp.where(keep, value, 0.0)
        return carry

    lax.fori_loop(0, cells + 6, divergence, 0, unroll=4)

    def apply(field, p, q, t, count):
        out = []
        for tile, (own, other) in list(enumerate(pair(field, p + 1, t)))[:count]:
            before, after = beside(own, other, lane)
            inward, outward = field[tile, p + 1, at(t, -1)], field[tile, p + 1, at(t, 1)]
            around = (before + after) + (inward + outward)
            around = around + (field[tile, p + 2, at(t)] + field[tile, p, at(t)])
            out.append(diag[tile, q, at(t, -PAD)] * own - around)
        return out

    def second(p, carry):
        for t in tiles:
            own, rim = apply(s0, p, p, t, 2)
            s1[0, p, at(t)] = own
            s1[1, p, at(t)] = jnp.where(keep, rim, 0.0)
        return carry

    lax.fori_loop(0, cells + 4, second, 0, unroll=4)

    def third(p, carry):
        for t in tiles:
            own, rim = apply(s1, p, p + 1, t, 2)
            s2[0, p, at(t)] = own
            s2[1, p, at(t)] = jnp.where(keep, rim, 0.0)
        return carry

    lax.fori_loop(0, cells + 2, third, 0, unroll=4)

    def products(p, carry):
        for t in tiles:
            (fourth,) = apply(s2, p, p + 2, t, 1)
            a, b, c = s0[0, p + 3, at(t)], s1[0, p + 2, at(t)], s2[0, p + 1, at(t)]
            pairs = ((a, a), (a, b), (b, b), (b, c), (c, c), (c, fourth))
            carry = tuple(s + x * y for s, (x, y) in zip(carry, pairs))
        predicted[0, p] = p0[0, p + 4]
        predicted[1, p] = p1[0, p + 3, body]
        predicted[2, p] = p2[0, p + 3]
        edges[0, p] = s0[1, p + 3, body]
        edges[1, p] = s1[1, p + 2, body]
        edges[2, p] = s2[1, p + 1, body]
        return carry

    parts = lax.fori_loop(0, cells, products, (zero,) * 6)

    def give(p, carry):
        base0[p] = s0[0, p + 2, body]
        base1[p] = s1[0, p + 1, body]
        base2[p] = s2[0, p, body]
        return carry

    lax.fori_loop(0, cells + 2, give, 0, unroll=4)

    group = iota((1, LANES), 1) // 16
    lines = []
    for part in parts:
        part = jnp.sum(part, axis=0, keepdims=True)
        for step in (64, 32, 16):
            part = part + pltpu.roll(part, step, 1)
        lines.append(part)
    sums[...] = jnp.broadcast_to(merge(lines, group)[None], sums.shape)


def across(own, row, inner):
    size = own.shape[0]
    inward = jnp.where(row == 0, inner, pltpu.roll(own, 1, 0))
    outward = jnp.where(row == size - 1, 0.0, pltpu.roll(own, size - 1, 0))
    return inward, outward


def coefficients(nu):
    def product(x, y):
        total = 0.0
        for i, a in enumerate(x):
            for j, b in enumerate(y):
                total = total + a * b * nu[i + j]
        return total

    def energy(x):
        total = 0.0
        for i, a in enumerate(x):
            for j, b in enumerate(x):
                total = total + a * b * (nu[i + j + 1] + CENTER * nu[i + j])
        return total

    def image(x):
        out = [CENTER * a for a in x] + [0.0 * x[0]]
        return [out[0]] + [out[i + 1] + x[i] for i in range(len(x))]

    def length(norm, bottom):
        return jnp.clip(norm / bottom, 0.0624, 2.01)

    one = jnp.ones_like(nu[0])
    residual, direction, norm = [one], [one], nu[0]
    answer = [0.0 * one] * 3
    for step in range(3):
        alpha = length(norm, energy(direction))
        answer = [
            a + alpha * direction[i] if i < len(direction) else a for i, a in enumerate(answer)
        ]
        if step == 2:
            break
        moved = image(direction)
        residual = residual + [0.0 * one] * (len(moved) - len(residual))
        residual = [r - alpha * m for r, m in zip(residual, moved)]
        after = product(residual, residual)
        beta = after / norm
        padded = direction + [0.0 * one]
        direction = [r + beta * d for r, d in zip(residual, padded)]
        norm = after
    return answer


def project_kernel(sums, predicted, base0, base1, base2, edges, velocity, pressure, grown):
    cells, rows = pressure.shape[0], pressure.shape[1]
    lane = iota((rows, LANES), 1)
    row = iota((rows, LANES), 0)
    line = jnp.sum(sums[...], axis=0)
    group = iota((1, LANES), 1) // 16
    nu = [
        jnp.sum(jnp.where(group == k, line, 0.0), axis=1, keepdims=True) for k in range(6)
    ]
    c0, c1, c2 = coefficients(nu)

    def combine(p, carry):
        grown[p] = c0 * base0[p] + c1 * base1[p] + c2 * base2[p]
        return carry

    lax.fori_loop(0, cells + 2, combine, 0)

    def gradient(p, carry):
        own = grown[p + 1]
        other = c0 * edges[0, p] + c1 * edges[1, p] + c2 * edges[2, p]
        before, after = beside(own, other, lane)
        inward, outward = across(own, row, 0.0)
        pressure[p] = own
        velocity[0, p] = predicted[0, p] - 0.5 * (grown[p + 2] - grown[p])
        velocity[1, p] = predicted[1, p] - 0.5 * (outward - inward)
        velocity[2, p] = predicted[2, p] - 0.5 * (after - before)
        return carry

    lax.fori_loop(0, cells, gradient, 0)


def call(kernel, shapes, operands, scratch=(), spaces=None, outs=pltpu.VMEM, sems=0):
    spec = lambda space: pl.BlockSpec(memory_space=space)
    spaces = spaces or [pltpu.VMEM] * len(operands)
    buffers = [pltpu.VMEM(s, jnp.float32) for s in scratch]
    if sems:
        buffers.append(pltpu.SemaphoreType.DMA((sems,)))
    return pl.pallas_call(
        kernel,
        out_shape=[jax.ShapeDtypeStruct(s, jnp.float32) for s in shapes],
        in_specs=[spec(space) for space in spaces],
        out_specs=[spec(outs)] * len(shapes),
        scratch_shapes=buffers,
        compiler_params=pltpu.CompilerParams(vmem_limit_bytes=VMEM_LIMIT),
    )(*operands)


def swap(low, high, axis):
    count = lax.axis_size(axis)
    up = [(i, (i + 1) % count) for i in range(count)]
    down = [(j, i) for i, j in up]
    return lax.ppermute(high, axis, up), lax.ppermute(low, axis, down)


def per_device(velocity, rotor_flux, correlation_weight, damping, offset):
    cells, rows = damping.shape[0], damping.shape[1]
    azim = lax.axis_size("azim")
    devices = azim * lax.axis_size("radax")
    plane = (rows, LANES)
    strips = (cells + 1, 8, LANES)
    to_left, to_right = call(
        edge_kernel,
        [strips, strips],
        (velocity, damping, correlation_weight, rotor_flux),
        scratch=[(3, cells) + plane, (cells,) + plane, (3, cells, LANES), (cells, LANES)],
        spaces=[pltpu.HBM] * 4,
        sems=6,
    )
    before, after = swap(to_left, to_right, "radax")
    message = (PLANES + 1,) + plane
    low, high = call(
        plane_kernel,
        [message, message],
        (velocity, damping, correlation_weight, to_left),
        spaces=[pltpu.HBM] * 3 + [pl.ANY],
        outs=pl.ANY,
        sems=14,
    )
    from_low, from_high = swap(low, high, "azim")
    corner = (2, HALO + 1, 8, LANES)
    low, high, spread = call(
        corner_kernel,
        [corner, corner, (azim, 16, LANES)],
        (before, after, rotor_flux),
    )
    low_halo, high_halo = swap(low, high, "azim")
    turned = lax.all_to_all(spread, "azim", 0, 0, tiled=True)
    own = (cells + 2,) + plane
    high_plane = (rows + 2 * PAD, LANES)
    predicted, base0, base1, base2, edges, sums = call(
        basis_kernel,
        [(3, cells) + plane, own, own, own, (3, cells) + plane, (devices, 1, LANES)],
        (
            offset,
            velocity,
            damping,
            correlation_weight,
            from_high,
            from_low,
            before,
            after,
            high_halo,
            low_halo,
            turned,
        ),
        scratch=[
            (2, cells + 10) + high_plane,
            (2, cells + 8) + high_plane,
            (2, cells + 8) + high_plane,
            (2, cells + 4) + plane,
            (2, cells + 8) + plane,
            (2, cells + 6) + high_plane,
            (2, cells + 6) + plane,
            (2, cells + 6) + high_plane,
            (2, cells + 4) + high_plane,
            (2, cells + 2) + high_plane,
            (3, cells + 8, LANES),
            (cells + 8, LANES),
            (2, cells + 8, LANES),
            (2, cells + 8, LANES),
        ],
        spaces=[pltpu.SMEM] + [pltpu.VMEM] * 10,
    )
    sums = lax.all_to_all(sums, ("azim", "radax"), 0, 0, tiled=True)
    return call(
        project_kernel,
        [(3, cells) + plane, (cells,) + plane],
        (sums, predicted, base0, base1, base2, edges),
        scratch=[own],
    )


def solution(mesh):
    in_specs = (
        P(None, "azim", None, "radax"),
        P("azim", "radax"),
        P(None, "azim", "radax"),
        P("azim", None, "radax"),
        P(),
    )
    out_specs = (P(None, "azim", None, "radax"), P("azim", None, "radax"))

    def run(*args):
        return tuple(per_device(*args))

    return jax.shard_map(run, mesh=mesh, in_specs=in_specs, out_specs=out_specs, check_vma=False)
```

time: 85.2 us -> 71.5 us (0.84)
  waiting for transfers between devices: 17.6 us -> 8.85 us
  Pallas kernels: 18.8 us -> 14.4 us
    ppermute x6, waiting for transfers between devices: 11.1 us -> 2.62 us  [swap(): return (lax.ppermute(high, axis, up), lax.ppermute(low, axis, down))]
    pallas_call x4 -> x5, Pallas kernels: 18.8 us -> 14.4 us  [call(): pl.pallas_call(kernel, out_shape=[jax.ShapeDtypeStruct(s, jnp.float32) fo...]
    ppermute x6, starting transfers between devices: 9.51 us -> 10.9 us  [swap(): return (lax.ppermute(high, axis, up), lax.ppermute(low, axis, down))]
    all_to_all x1, starting transfers between devices: 10.7 us -> 9.55 us  [per_device(): turned = lax.all_to_all(spread, 'azim', 0, 0, tiled=True)]
  transfers between devices with their start and end apart: 7 -> 7, of which waited for: 5 -> 2; matrix products, arithmetic and copies ran while one was open for 0% -> 0% of each run, Pallas kernels for 1% -> 3%
where the time goes in v2:
time: 71.5 us; the launch traced here: 71.2 us
  blocking collectives  22.8 us (32%)
  starting transfers between devices  20.4 us (29%)
  Pallas kernels  14.4 us (20%)
  waiting for transfers between devices  8.85 us (12%)
  local copies, waits for them, and re-layouts  3.48 us (5%)
  between operations  1.34 us (2%)
    all_to_all x1, blocking collectives, per_device(): sums = lax.all_to_all(sums, ('azim', 'radax'), 0, 0, tiled=True)  22.8 us
    pallas_call x5, Pallas kernels, call(): pl.pallas_call(kernel, out_shape=[jax.ShapeDtypeStruct(s, jnp.float32) fo...  14.4 us
    ppermute x6, starting transfers between devices, swap(): return (lax.ppermute(high, axis, up), lax.ppermute(low, axis, down))  10.9 us
    all_to_all x1, starting transfers between devices, per_device(): turned = lax.all_to_all(spread, 'azim', 0, 0, tiled=True)  9.55 us
    all_to_all x1, waiting for transfers between devices, per_device(): turned = lax.all_to_all(spread, 'azim', 0, 0, tiled=True)  6.23 us
    unnamed x14, local copies, waits for them, and re-layouts  3.48 us
    ppermute x6, waiting for transfers between devices, swap(): return (lax.ppermute(high, axis, up), lax.ppermute(low, axis, down))  2.62 us
  transfers between devices with their start and end apart: 7, of which 2 were waited for; matrix products, arithmetic and copies ran while one was open for 0% of the time, Pallas kernels for 3%

profile of v2, /device:TPU:1, one launch (start us, length us, event | category | flops | bytes accessed | tf_op | source)
XLA Modules:
  0.0 71.2 jit_solution(1781996609142192014)
XLA Ops:
  0.6 0.0 copy-start
  0.6 1.1 %copy-done = f32[3,8,64,128]{3,2,1,0:T(8,128)S(1)} copy-done((f32[3,8,64,128]{3,2,1,0:T(8,128)S(1)}, f32[3,8,64,128]{3,2,1,0:T(8,128)}, u32[]{:S(2)}) %copy-start) | copy-done | bytes 786456
  1.8 0.0 copy-start.2
  1.8 0.9 %copy-done.2 = f32[8,64,128]{2,1,0:T(8,128)S(1)} copy-done((f32[8,64,128]{2,1,0:T(8,128)S(1)}, f32[8,64,128]{2,1,0:T(8,128)}, u32[]{:S(2)}) %copy-start.2) | copy-done | bytes 262168
  2.7 0.0 copy-start.4
  2.7 0.7 copy-done.4
  3.4 0.0 copy-start.6
  3.4 0.7 copy-done.6
  4.1 0.9 %shard_map.68 = (f32[9,8,128]{2,1,0:T(8,128)S(1)}, f32[9,8,128]{2,1,0:T(8,128)S(1)}) custom-call(f32[3,8,64,128]{3,2,1,0:T(8,128)S(1)} %copy-done, f32[8,64,128]{2,1,0:T(8,128)S(1)} %copy-done.2, f32[3,8,128]{2,1,0:T(8,128)S(1)} %copy-done.4, f32[8,128]{1,0:T(8,128)S(1)} %copy-done.6), custom_call_target="tpu_custom_call" | custom-call | tf_op jit(solution)/shard_map/pallas_call | solution.py:464
  5.0 3.8 %collective-permute-start.2 = (f32[9,8,128]{2,1,0:T(8,128)S(1)}, f32[9,8,128]{2,1,0:T(8,128)S(1)}, u32[]{:S(2)}, u32[]{:S(2)}) collective-permute-start(f32[9,8,128]{2,1,0:T(8,128)S(1)} %get-tuple-element.18), channel_id=1, source_target_pairs={{0,1},{1,2},{2,3},{3,4},{4,5},{5,6},{6,7},{7,0},{8,9},{9,10},{10,1... | collective-permute-start | bytes 110600 | tf_op jit(solution)/shard_map/ppermute | solution.py:478
  8.9 0.0 copy-start.1
  8.9 2.3 %collective-permute-start.3 = (f32[9,8,128]{2,1,0:T(8,128)S(1)}, f32[9,8,128]{2,1,0:T(8,128)S(1)}, u32[]{:S(2)}, u32[]{:S(2)}) collective-permute-start(f32[9,8,128]{2,1,0:T(8,128)S(1)} %get-tuple-element.15.order), channel_id=1, source_target_pairs={{1,0},{2,1},{3,2},{4,3},{5,4},{6,5},{7,6},{0,7},{9,8},{10,9},{11,1... | collective-permute-start | bytes 110600 | tf_op jit(solution)/shard_map/ppermute | solution.py:478
  11.2 1.3 %shard_map.69 = (f32[16,64,128]{2,1,0:T(8,128)}, f32[16,64,128]{2,1,0:T(8,128)S(1)}) custom-call(f32[3,8,64,128]{3,2,1,0:T(8,128)S(1)} %copy-done, f32[8,64,128]{2,1,0:T(8,128)S(1)} %copy-done.2, f32[3,8,128]{2,1,0:T(8,128)S(1)} %copy-done.4, f32[9,8,128]{2,1,0:T(8,128)S(1)} %get-tuple-element.15.order), custom_call_target="tpu_custom_call" | custom-call | tf_op jit(solution)/shard_map/pallas_call | solution.py:464
  12.5 2.9 %collective-permute-start = (f32[16,64,128]{2,1,0:T(8,128)}, f32[16,64,128]{2,1,0:T(8,128)S(1)}, u32[]{:S(2)}, u32[]{:S(2)}) collective-permute-start(f32[16,64,128]{2,1,0:T(8,128)} %get-tuple-element.16), channel_id=1, source_target_pairs={{8,0},{16,8},{24,16},{32,24},{40,32},{48,40},{56,48},{64,56},{72,6... | collective-permute-start | bytes 1572872 | tf_op jit(solution)/shard_map/ppermute | solution.py:478
  15.4 0.0 collective-permute-start.1
  15.4 0.0 collective-permute-done.2.before.before_own
  15.4 0.0 collective-permute-done.3.after.after_own
  15.4 0.7 %shard_map.70 = (f32[2,6,8,128]{3,2,1,0:T(8,128)S(1)}, f32[2,6,8,128]{3,2,1,0:T(8,128)S(1)}, f32[32,16,128]{2,1,0:T(8,128)}) custom-call(f32[9,8,128]{2,1,0:T(8,128)S(1)} %collective-permute-done.2.before.before_own, f32[9,8,128]{2,1,0:T(8,128)S(1)} %collective-permute-done.3.after.after_own, f32[8,128]{1,0:T(8,128)S(1)} %copy-done.6), custom_call_target="tpu_custom_call" | custom-call | tf_op jit(solution)/shard_map/pallas_call | solution.py:464
  16.2 0.0 copy-start.3
  16.2 0.0 copy-start.5
  16.2 9.5 %all-to-all-start = ((f32[32,16,128]{2,1,0:T(8,128)}), f32[32,16,128]{2,1,0:T(8,128)S(1)}, u32[]{:S(2)}, u32[]{:S(2)}) async-start(f32[32,16,128]{2,1,0:T(8,128)} %get-tuple-element.21), calls=%async_computation | async-start | bytes 524288 | tf_op jit(solution)/shard_map/all_to_all | solution.py:513
  25.7 0.3 collective-permute-start.4
  26.0 1.5 %collective-permute-start.5 = (f32[2,6,8,128]{3,2,1,0:T(8,128)S(1)}, f32[2,6,8,128]{3,2,1,0:T(8,128)S(1)}, u32[]{:S(2)}, u32[]{:S(2)}) collective-permute-start(f32[2,6,8,128]{3,2,1,0:T(8,128)S(1)} %get-tuple-element.20), channel_id=1, source_target_pairs={{0,8},{8,16},{16,24},{24,32},{32,40},{40,48},{48,56},{56,64},{64,7... | collective-permute-start | bytes 147464 | tf_op jit(solution)/shard_map/ppermute | solution.py:478
  28.2 2.6 %collective-permute-done.4.low_halo = f32[2,6,8,128]{3,2,1,0:T(8,128)S(1)} collective-permute-done((f32[2,6,8,128]{3,2,1,0:T(8,128)S(1)}, f32[2,6,8,128]{3,2,1,0:T(8,128)S(1)}, u32[]{:S(2)}, u32[]{:S(2)}) %collective-permute-start.4) | collective-permute-done | bytes 49184 | tf_op jit(solution)/shard_map/ppermute | solution.py:478
  30.8 0.0 collective-permute-done.5.high_halo
  30.8 0.0 collective-permute-done.low
  30.8 0.0 collective-permute-done.1.high
  30.8 6.2 %all-to-all-done.turned = f32[32,16,128]{2,1,0:T(8,128)S(1)} async-done(((f32[32,16,128]{2,1,0:T(8,128)}), f32[32,16,128]{2,1,0:T(8,128)S(1)}, u32[]{:S(2)}, u32[]{:S(2)}) %all-to-all-start) | async-done | bytes 262176 | tf_op jit(solution)/shard_map/all_to_all | solution.py:513
  37.0 0.0 copy-done.1
  37.1 0.0 copy-done.3
  37.1 0.0 copy-done.5
  37.1 9.1 %shard_map.71 = (f32[3,8,64,128]{3,2,1,0:T(8,128)S(1)}, f32[10,64,128]{2,1,0:T(8,128)S(1)}, f32[10,64,128]{2,1,0:T(8,128)S(1)}, f32[10,64,128]{2,1,0:T(8,128)S(1...) custom-call(s32[1]{0:T(128)S(6)} %copy.7.offset, f32[3,8,64,128]{3,2,1,0:T(8,128)S(1)} %copy-done.1, ...), custom_call_target="tpu_custom_call" | custom-call | tf_op jit(solution)/shard_map/pallas_call | solution.py:464
  46.2 22.8 %all_to_all.10.sums = f32[256,1,128]{2,1,0:T(1,128)S(1)} all-to-all(f32[256,1,128]{2,1,0:T(1,128)S(1)} %get-tuple-element.22), channel_id=1, replica_groups=mesh['azim'=32,'radax'=8] {'azim','radax'}, dimensions={0} | all-to-all | bytes 262144 | tf_op jit(solution)/shard_map/all_to_all | solution.py:550
  69.0 2.2 %shard_map.72 = (f32[3,8,64,128]{3,2,1,0:T(8,128)}, f32[8,64,128]{2,1,0:T(8,128)}) custom-call(f32[256,1,128]{2,1,0:T(1,128)S(1)} %all_to_all.10.sums, f32[3,8,64,128]{3,2,1,0:T(8,128)S(1)} %get-tuple-element.23.predicted, f32[10,64,128]{2,1,0:T(8,128)S(1)} %get-tuple-element.24.base0, f32[10,64,128]{2,1,0:T(8,128)S(1)} %get-tuple-element.25.base1, ...), custom_call_target="tpu_custom_call" | custom-call | tf_op jit(solution)/shard_map/pallas_call | solution.py:464
Async XLA Ops:
  0.6 1.1 %copy-start = (f32[3,8,64,128]{3,2,1,0:T(8,128)S(1)}, f32[3,8,64,128]{3,2,1,0:T(8,128)}, u32[]{:S(2)}) copy-start(f32[3,8,64,128]{3,2,1,0:T(8,128)} %velocity.5) | copy-start | bytes 2359300
  1.8 0.9 %copy-start.2 = (f32[8,64,128]{2,1,0:T(8,128)S(1)}, f32[8,64,128]{2,1,0:T(8,128)}, u32[]{:S(2)}) copy-start(f32[8,64,128]{2,1,0:T(8,128)} %damping.5) | copy-start | bytes 786436
  2.7 0.7 copy-start.4
  3.4 0.7 copy-start.6
  5.0 10.4 %collective-permute-start.2 = (f32[9,8,128]{2,1,0:T(8,128)S(1)}, f32[9,8,128]{2,1,0:T(8,128)S(1)}, u32[]{:S(2)}, u32[]{:S(2)}) collective-permute-start(f32[9,8,128]{2,1,0:T(8,128)S(1)} %get-tuple-element.18), channel_id=1, source_target_pairs={{0,1},{1,2},{2,3},{3,4},{4,5},{5,6},{6,7},{7,0},{8,9},{9,10},{10,1... | collective-permute-start | bytes 110600 | tf_op jit(solution)/shard_map/ppermute | solution.py:478
  8.9 28.2 %copy-start.1 = (f32[3,8,64,128]{3,2,1,0:T(8,128)S(1)}, f32[3,8,64,128]{3,2,1,0:T(8,128)}, u32[]{:S(2)}) copy-start(f32[3,8,64,128]{3,2,1,0:T(8,128)} %velocity.5) | copy-start | bytes 2359300
  8.9 6.6 %collective-permute-start.3 = (f32[9,8,128]{2,1,0:T(8,128)S(1)}, f32[9,8,128]{2,1,0:T(8,128)S(1)}, u32[]{:S(2)}, u32[]{:S(2)}) collective-permute-start(f32[9,8,128]{2,1,0:T(8,128)S(1)} %get-tuple-element.15.order), channel_id=1, source_target_pairs={{1,0},{2,1},{3,2},{4,3},{5,4},{6,5},{7,6},{0,7},{9,8},{10,9},{11,1... | collective-permute-start | bytes 110600 | tf_op jit(solution)/shard_map/ppermute | solution.py:478
  12.5 18.3 %collective-permute-start = (f32[16,64,128]{2,1,0:T(8,128)}, f32[16,64,128]{2,1,0:T(8,128)S(1)}, u32[]{:S(2)}, u32[]{:S(2)}) collective-permute-start(f32[16,64,128]{2,1,0:T(8,128)} %get-tuple-element.16), channel_id=1, source_target_pairs={{8,0},{16,8},{24,16},{32,24},{40,32},{48,40},{56,48},{64,56},{72,6... | collective-permute-start | bytes 1572872 | tf_op jit(solution)/shard_map/ppermute | solution.py:478
  15.4 15.4 %collective-permute-start.1 = (f32[16,64,128]{2,1,0:T(8,128)S(1)}, f32[16,64,128]{2,1,0:T(8,128)S(1)}, u32[]{:S(2)}, u32[]{:S(2)}) collective-permute-start(f32[16,64,128]{2,1,0:T(8,128)S(1)} %get-tuple-element.17), channel_id=1, source_target_pairs={{0,8},{8,16},{16,24},{24,32},{32,40},{40,48},{48,56},{56,64},{64,7... | collective-permute-start | bytes 1572872 | tf_op jit(solution)/shard_map/ppermute | solution.py:478
  16.2 20.9 %copy-start.3 = (f32[8,64,128]{2,1,0:T(8,128)S(1)}, f32[8,64,128]{2,1,0:T(8,128)}, u32[]{:S(2)}) copy-start(f32[8,64,128]{2,1,0:T(8,128)} %damping.5) | copy-start | bytes 786436
  16.2 20.9 %copy-start.5 = (f32[3,8,128]{2,1,0:T(8,128)S(1)}, f32[3,8,128]{2,1,0:T(8,128)}, u32[]{:S(2)}) copy-start(f32[3,8,128]{2,1,0:T(8,128)} %weight.5) | copy-start | bytes 36868
  16.2 20.9 %all-to-all-start = ((f32[32,16,128]{2,1,0:T(8,128)}), f32[32,16,128]{2,1,0:T(8,128)S(1)}, u32[]{:S(2)}, u32[]{:S(2)}) async-start(f32[32,16,128]{2,1,0:T(8,128)} %get-tuple-element.21), calls=%async_computation | async-start | bytes 524288 | tf_op jit(solution)/shard_map/all_to_all | solution.py:513
  25.7 5.1 %collective-permute-start.4 = (f32[2,6,8,128]{3,2,1,0:T(8,128)S(1)}, f32[2,6,8,128]{3,2,1,0:T(8,128)S(1)}, u32[]{:S(2)}, u32[]{:S(2)}) collective-permute-start(f32[2,6,8,128]{3,2,1,0:T(8,128)S(1)} %get-tuple-element.19), channel_id=1, source_target_pairs={{8,0},{16,8},{24,16},{32,24},{40,32},{48,40},{56,48},{64,56},{72,6... | collective-permute-start | bytes 147464 | tf_op jit(solution)/shard_map/ppermute | solution.py:478
  26.0 4.8 %collective-permute-start.5 = (f32[2,6,8,128]{3,2,1,0:T(8,128)S(1)}, f32[2,6,8,128]{3,2,1,0:T(8,128)S(1)}, u32[]{:S(2)}, u32[]{:S(2)}) collective-permute-start(f32[2,6,8,128]{3,2,1,0:T(8,128)S(1)} %get-tuple-element.20), channel_id=1, source_target_pairs={{0,8},{8,16},{16,24},{24,32},{32,40},{40,48},{48,56},{56,64},{64,7... | collective-permute-start | bytes 147464 | tf_op jit(solution)/shard_map/ppermute | solution.py:478

commit v3 on v0

v3 whole, which is shorter than its diff:
```python
import jax
import jax.numpy as jnp
from jax import lax
from jax.experimental import pallas as pl
from jax.experimental.pallas import tpu as pltpu
from jax.sharding import PartitionSpec as P


CENTER = 8.0
HALO = 5
LANES = 128
HALF = 64
FRONT = 16
TALL = LANES + 2 * FRONT
TILES = LANES // 8
VMEM_LIMIT = 48 * 1024 * 1024
WHOLE_VMEM = 62 * 1024 * 1024
DEPTHS = (5, 4, 4, 2)
STARTS = (0, 5, 9, 13)
PLANES = 15
REACH = (4, 4, 5, 2)
FROM = (0, 4, 8, 13)
STRIP = 16
BODY = slice(FRONT, FRONT + LANES)


def iota(shape, dim):
    return lax.broadcasted_iota(jnp.int32, shape, dim)


def spin(tile, steps):
    return pltpu.roll(tile, steps % LANES, 1) if steps % LANES else tile


def at(t, shift=0):
    start = FRONT - 8 + 8 * t + shift
    return slice(start, start + 8)


def paired(first, second):
    return jnp.concatenate([first, second], axis=0).T


def edge_kernel(velocity, damping, weight, to_left, to_right, vel, damp, wt, turned, sems):
    cells = damping.shape[0]
    pairs = cells // 2
    copies = [pltpu.make_async_copy(damping, damp, sems.at[3])]
    copies += [pltpu.make_async_copy(velocity.at[k], vel.at[k], sems.at[k]) for k in range(3)]
    copies += [pltpu.make_async_copy(weight, wt, sems.at[4])]
    for copy in copies:
        copy.start()
    for copy in copies:
        copy.wait()
    fields = [vel.at[0], vel.at[1], vel.at[2], damp]
    for i in range(pairs):
        base = STRIP * i
        for field, reach, start in zip(fields, REACH, FROM):
            turned[...] = paired(field[i], field[cells - 1 - i])
            rows = slice(base + start, base + start + reach)
            to_left[rows] = turned[0:reach]
            to_right[rows] = turned[LANES - reach : LANES]
        for message in (to_left, to_right):
            message[base + STRIP - 1 : base + STRIP] = jnp.zeros((1, LANES), jnp.float32)
    for tap in range(3):
        rows = slice(STRIP * pairs + tap * cells, STRIP * pairs + (tap + 1) * cells)
        to_left[rows] = wt[tap]
        to_right[rows] = wt[tap]


def plane_kernel(velocity, damping, weight, order, low, high, own):
    cells, rows = damping.shape[0], damping.shape[1]
    fields = [velocity.at[0], velocity.at[1], velocity.at[2], damping]
    for number, (field, depth, start) in enumerate(zip(fields, DEPTHS, STARTS)):
        low[start : start + depth] = field[0:depth]
        high[start : start + depth] = field[cells - depth : cells]
        for i in range(cells // 2):
            own[number, i] = paired(field[i], field[cells - 1 - i])
    for message in (low, high):
        for tap in range(3):
            message[PLANES, tap * cells : (tap + 1) * cells] = weight[tap]
        message[PLANES, 3 * cells : rows] = jnp.zeros((rows - 3 * cells, LANES), jnp.float32)


def spread_kernel(before, after, rotor, spread):
    own = rotor[...]
    rim = jnp.where(iota(own.shape, 1) < HALF, after[...], before[...])
    for k in range(spread.shape[0]):
        spread[k, 0:8] = own
        spread[k, 8:16] = rim


def corner_kernel(before, after, corner):
    strips = before.shape[0] - 24
    corner[0:strips] = before[0:strips]
    corner[strips : 2 * strips] = after[0:strips]
    left = iota((24, LANES), 1) < HALF
    corner[2 * strips : 2 * strips + 24] = jnp.where(left, after[strips:], before[strips:])


def basis_kernel(
    offset,
    weight,
    own,
    lower,
    upper,
    before,
    after,
    lower_rim,
    upper_rim,
    turned,
    p0,
    p1,
    p2,
    s0,
    s1,
    s2,
    sums,
    v0,
    v1,
    v2,
    diag,
    strip,
    taps,
    rot,
    mirror,
    line,
    face,
):
    cells = weight.shape[1]
    pairs = cells // 2
    last = HALO + pairs - 1
    total = turned.shape[0] * cells
    every = range(TILES + 2)
    place = lax.axis_index("radax")
    has_before, has_after = place > 0, place < lax.axis_size("radax") - 1
    lane = iota((8, LANES), 1)
    first_cell = lane % HALF == 0
    last_cell = lane % HALF == HALF - 1
    sign = jnp.where(lane < HALF, 1.0, -1.0)
    tenth = 0.1 * sign

    def walled(t, value):
        if t == 0:
            return jnp.where(has_before, value, 0.0)
        if t == TILES + 1:
            return jnp.where(has_after, value, 0.0)
        return value

    def seam(field):
        for t in every:
            field[last + 1, at(t)] = spin(field[last, at(t)], HALF)

    shift = 6.0 - CENTER
    for number, field in enumerate((v0, v1, v2, diag)):
        extra = shift if number == 3 else 0.0
        depth, start = DEPTHS[number], STARTS[number]
        for i in range(HALO - depth, HALO):
            block = paired(lower[start + i - HALO + depth], upper[start + HALO - 1 - i])
            field[i, BODY] = block + extra if number == 3 else block

        def fill(i, carry):
            block = own[number, i]
            field[HALO + i, BODY] = block + extra if number == 3 else block
            return carry

        lax.fori_loop(0, pairs, fill, 0, unroll=True)

    left = iota((STRIP, LANES), 1) < HALF
    size = STRIP * pairs
    for side, message in enumerate((before, after)):
        for i in range(HALO + pairs):
            pair = max(HALO - 1 - i, 0) if i else pairs - 1
            rows = slice(side * size + STRIP * pair, side * size + STRIP * pair + STRIP)
            if i >= HALO:
                strip[side, i] = message[STRIP * (i - HALO) : STRIP * (i - HALO) + STRIP]
            elif i:
                strip[side, i] = spin(jnp.where(left, upper_rim[rows], lower_rim[rows]), HALF)
            else:
                strip[side, i] = jnp.where(left, lower_rim[rows], upper_rim[rows])
    for number, field in enumerate((v0, v1, v2, diag)):
        reach, start = REACH[number], FROM[number]
        for i in range(HALO - DEPTHS[number], HALO + pairs):
            for side, t in ((0, 0), (1, TILES + 1)):
                value = walled(t, strip[side, i, start : start + reach])
                value = value + shift if number == 3 else value
                row = FRONT - reach if side == 0 else FRONT + LANES
                field[i, row : row + reach] = value
    for field in (v0, v1, v2):
        seam(field)

    wide = cells + 6
    rim_left = iota((cells, LANES), 1) < HALF
    for tap in range(3):
        k = tap * cells
        taps[0, tap, 0:3] = lower[PLANES, k + cells - 3 : k + cells]
        taps[0, tap, 3 : 3 + cells] = weight[tap]
        taps[0, tap, 3 + cells : wide] = upper[PLANES, k : k + 3]
        k += 2 * size
        taps[1, tap, 0:3] = lower_rim[k + cells - 3 : k + cells]
        k -= size
        taps[1, tap, 3 : 3 + cells] = jnp.where(
            rim_left, after[k : k + cells], before[k : k + cells]
        )
        k += size
        taps[1, tap, 3 + cells : wide] = upper_rim[k : k + 3]
    begin = lax.axis_index("azim") * cells - offset[0] - 4 + 2 * total
    for k in range(wide + 2):
        source = lax.rem(begin + k, total)
        block = source // cells
        row = lax.rem(source, cells)
        rot[0, k : k + 1] = turned[block, pl.ds(row, 1)]
        rot[1, k : k + 1] = turned[block, pl.ds(row + 8, 1)]
    for part in range(2):
        flux = jnp.zeros((wide, LANES), jnp.float32)
        for tap in range(3):
            flux += taps[part, tap, 0:wide] * rot[part, tap : tap + wide]
        mirror[2 : 2 + wide // 2] = flux[0 : wide // 2]
        for i in range(2, last + 1):
            mirror[HALF + i : HALF + i + 1] = flux[wide + 1 - i : wide + 2 - i]
        columns = mirror[...].T
        if part == 0:
            line[BODY] = columns
        else:
            line[FRONT + LANES : FRONT + LANES + 8] = columns[0:8]
            line[FRONT - 8 : FRONT] = columns[LANES - 8 : LANES]
    for i in range(2, last + 1):
        for t in every:
            face[i, at(t)] = spin(line[at(t)], -i)

    def radial(tile, inner):
        inward = jnp.where(first_cell, inner, spin(tile, 1))
        outward = jnp.where(last_cell, 0.0, spin(tile, -1))
        return inward, outward

    def advance(field, i, t, inner):
        x, lo, hi = field[i, at(t)], field[i - 1, at(t)], field[i + 1, at(t)]
        inward, outward = radial(x, inner)
        around = (field[i, at(t, -1)] + field[i, at(t, 1)]) + (inward + outward) + (lo + hi)
        wind = tenth * v0[i, at(t)]
        return walled(t, (0.4 * x + 0.1 * around) - wind * (hi - lo))

    def first_component(i, carry):
        for t in every:
            p0[i, at(t)] = advance(v0, i, t, 0.0)
        return carry

    def other_components(i, carry):
        for t in every:
            p1[i, at(t)] = advance(v1, i, t, face[i, at(t)])
            p2[i, at(t)] = advance(v2, i, t, 0.0)
        return carry

    def divergence(i, carry):
        for t in every:
            inward, outward = radial(p1[i, at(t)], face[i, at(t)])
            value = sign * (p0[i + 1, at(t)] - p0[i - 1, at(t)]) + (outward - inward)
            value = value + (p2[i, at(t, 1)] - p2[i, at(t, -1)])
            s0[i, at(t)] = walled(t, 0.5 * value)
        return carry

    def apply(field, i, t):
        x = field[i, at(t)]
        inward, outward = radial(x, 0.0)
        around = (field[i, at(t, -1)] + field[i, at(t, 1)]) + (inward + outward)
        around = around + (field[i - 1, at(t)] + field[i + 1, at(t)])
        return walled(t, diag[i, at(t)] * x - around)

    def second(i, carry):
        for t in every:
            s1[i, at(t)] = apply(s0, i, t)
        return carry

    def third(i, carry):
        for t in every:
            s2[i, at(t)] = apply(s1, i, t)
        return carry

    def products(i, carry):
        for t in range(1, TILES + 1):
            fourth = apply(s2, i, t)
            a, b, c = s0[i, at(t)], s1[i, at(t)], s2[i, at(t)]
            factors = ((a, a), (a, b), (b, b), (b, c), (c, c), (c, fourth))
            carry = tuple(s + x * y for s, (x, y) in zip(carry, factors))
        return carry

    lax.fori_loop(1, last + 1, first_component, 0, unroll=True)
    seam(p0)
    lax.fori_loop(2, last + 1, other_components, 0, unroll=True)
    lax.fori_loop(2, last + 1, divergence, 0, unroll=True)
    seam(s0)
    lax.fori_loop(3, last + 1, second, 0, unroll=True)
    seam(s1)
    lax.fori_loop(4, last + 1, third, 0, unroll=True)
    seam(s2)
    zero = jnp.zeros((8, LANES), jnp.float32)
    parts = lax.fori_loop(HALO, last + 1, products, (zero,) * 6, unroll=True)

    group = iota((1, LANES), 1) // 16
    packed = jnp.zeros((1, LANES), jnp.float32)
    for k, part in enumerate(parts):
        part = jnp.sum(part, axis=0, keepdims=True)
        for step in (64, 32, 16):
            part = part + pltpu.roll(part, step, 1)
        packed = jnp.where(group == k, part, packed)
    sums[...] = jnp.broadcast_to(packed[None], sums.shape)


def coefficients(nu):
    def product(x, y):
        total = 0.0
        for i, a in enumerate(x):
            for j, b in enumerate(y):
                total = total + a * b * nu[i + j]
        return total

    def energy(x):
        total = 0.0
        for i, a in enumerate(x):
            for j, b in enumerate(x):
                total = total + a * b * (nu[i + j + 1] + CENTER * nu[i + j])
        return total

    def image(x):
        out = [CENTER * a for a in x] + [0.0 * x[0]]
        return [out[0]] + [out[i + 1] + x[i] for i in range(len(x))]

    def length(norm, bottom):
        return jnp.clip(norm / bottom, 0.0624, 2.01)

    one = jnp.ones_like(nu[0])
    residual, direction, norm = [one], [one], nu[0]
    answer = [0.0 * one] * 3
    for step in range(3):
        alpha = length(norm, energy(direction))
        answer = [
            a + alpha * direction[i] if i < len(direction) else a for i, a in enumerate(answer)
        ]
        if step == 2:
            break
        moved = image(direction)
        residual = residual + [0.0 * one] * (len(moved) - len(residual))
        residual = [r - alpha * m for r, m in zip(residual, moved)]
        after = product(residual, residual)
        beta = after / norm
        padded = direction + [0.0 * one]
        direction = [r + beta * d for r, d in zip(residual, padded)]
        norm = after
    return answer


def project_kernel(sums, p0, p1, p2, s0, s1, s2, velocity, pressure, field, done):
    cells, rows = pressure.shape[0], pressure.shape[1]
    pairs = cells // 2
    last = HALO + pairs - 1
    lane = iota((8, LANES), 1)
    first_cell = lane % HALF == 0
    last_cell = lane % HALF == HALF - 1
    half = jnp.where(lane < HALF, 0.5, -0.5)
    total = jnp.sum(sums[...], axis=0)
    group = iota((1, LANES), 1) // 16
    nu = [jnp.sum(jnp.where(group == k, total, 0.0), axis=1, keepdims=True) for k in range(6)]
    c0, c1, c2 = coefficients(nu)

    def combine(i, carry):
        for t in range(TILES + 2):
            value = c0 * s0[i, at(t)] + c1 * s1[i, at(t)] + c2 * s2[i, at(t)]
            field[i, at(t)] = value
        return carry

    lax.fori_loop(HALO - 1, last + 1, combine, 0, unroll=True)
    for t in range(1, TILES + 1):
        field[last + 1, at(t)] = spin(field[last, at(t)], HALF)

    def gradient(i, carry):
        for t in range(1, TILES + 1):
            x = field[i, at(t)]
            inward = jnp.where(first_cell, 0.0, spin(x, 1))
            outward = jnp.where(last_cell, 0.0, spin(x, -1))
            around = half * (field[i + 1, at(t)] - field[i - 1, at(t)])
            along = 0.5 * (field[i, at(t, 1)] - field[i, at(t, -1)])
            own = slice(8 * t - 8, 8 * t)
            done[0, own] = p0[i, at(t)] - around
            done[1, own] = p1[i, at(t)] - 0.5 * (outward - inward)
            done[2, own] = p2[i, at(t)] - along
        for k in range(3):
            planes = done[k].T
            velocity[k, i - HALO] = planes[0:rows]
            velocity[k, last + pairs - i] = planes[rows:]
        planes = field[i, BODY].T
        pressure[i - HALO] = planes[0:rows]
        pressure[last + pairs - i] = planes[rows:]
        return carry

    lax.fori_loop(HALO, last + 1, gradient, 0, unroll=True)


def call(kernel, shapes, operands, scratch=(), spaces=None, sems=0, limit=VMEM_LIMIT):
    spec = lambda space: pl.BlockSpec(memory_space=space)
    spaces = spaces or [pltpu.VMEM] * len(operands)
    buffers = [pltpu.VMEM(s, jnp.float32) for s in scratch]
    if sems:
        buffers.append(pltpu.SemaphoreType.DMA((sems,)))
    return pl.pallas_call(
        kernel,
        out_shape=[jax.ShapeDtypeStruct(s, jnp.float32) for s in shapes],
        in_specs=[spec(space) for space in spaces],
        out_specs=[spec(pltpu.VMEM)] * len(shapes),
        scratch_shapes=buffers,
        compiler_params=pltpu.CompilerParams(vmem_limit_bytes=limit),
    )(*operands)


def swap(low, high, axis):
    count = lax.axis_size(axis)
    up = [(i, (i + 1) % count) for i in range(count)]
    down = [(j, i) for i, j in up]
    return lax.ppermute(high, axis, up), lax.ppermute(low, axis, down)


def per_device(velocity, rotor_flux, correlation_weight, damping, offset):
    cells, rows = damping.shape[0], damping.shape[1]
    azim = lax.axis_size("azim")
    devices = azim * lax.axis_size("radax")
    plane = (rows, LANES)
    block = (LANES, LANES)
    pairs = cells // 2
    rotor_before, rotor_after = swap(rotor_flux, rotor_flux, "radax")
    strips = (STRIP * pairs + 3 * cells, LANES)
    to_left, to_right = call(
        edge_kernel,
        [strips, strips],
        (velocity, damping, correlation_weight),
        scratch=[(3, cells) + plane, (cells,) + plane, (3, cells, LANES), block],
        spaces=[pl.ANY] * 3,
        sems=5,
        limit=WHOLE_VMEM,
    )
    before, after = swap(to_left, to_right, "radax")
    message = (PLANES + 1,) + plane
    low, high, own = call(
        plane_kernel,
        [message, message, (4, pairs) + block],
        (velocity, damping, correlation_weight, to_left),
        spaces=[pltpu.VMEM] * 3 + [pl.ANY],
    )
    lower, upper = swap(low, high, "azim")
    (spread,) = call(
        spread_kernel, [(azim, 16, LANES)], (rotor_before, rotor_after, rotor_flux)
    )
    turned = lax.all_to_all(spread, "azim", 0, 0, tiled=True)
    (corner,) = call(
        corner_kernel, [(2 * STRIP * pairs + 3 * cells, LANES)], (before, after)
    )
    lower_rim, upper_rim = swap(corner, corner, "azim")
    field = (HALO + pairs + 1, TALL, LANES)
    *fields, sums = call(
        basis_kernel,
        [field] * 6 + [(devices, 1, LANES)],
        (
            offset,
            correlation_weight,
            own,
            lower,
            upper,
            before,
            after,
            lower_rim,
            upper_rim,
            turned,
        ),
        scratch=[field] * 4
        + [
            (2, HALO + pairs, STRIP, LANES),
            (2, 3, cells + 8, LANES),
            (2, cells + 8, LANES),
            block,
            (TALL, LANES),
            field,
        ],
        spaces=[pltpu.SMEM] + [pltpu.VMEM] * 9,
    )
    sums = lax.all_to_all(sums, ("azim", "radax"), 0, 0, tiled=True)
    return call(
        project_kernel,
        [(3, cells) + plane, (cells,) + plane],
        (sums, *fields),
        scratch=[field, (3,) + block],
    )


def solution(mesh):
    in_specs = (
        P(None, "azim", None, "radax"),
        P("azim", "radax"),
        P(None, "azim", "radax"),
        P("azim", None, "radax"),
        P(),
    )
    out_specs = (P(None, "azim", None, "radax"), P("azim", None, "radax"))

    def run(*args):
        return tuple(per_device(*args))

    return jax.shard_map(run, mesh=mesh, in_specs=in_specs, out_specs=out_specs, check_vma=False)
```

time: 549 us -> 83.5 us (0.15)
  blocking collectives: 416 us -> 27.1 us
  other arithmetic: 32.5 us -> 0 us
  waiting for transfers between devices: 39.5 us -> 14.5 us
  starting transfers between devices: 42.1 us -> 26 us
  Pallas kernels: 0 us -> 11.1 us
  local copies, waits for them, and re-layouts: 9.9 us -> 2.94 us
  between operations: 8.06 us -> 1.39 us
    psum x5 -> x0, blocking collectives: 377 us -> none  [the longest x3 225 us: squares(): return lax.psum(jnp.sum(residual * residual), ('azim', 'radax'))]
    all_gather x1 -> x0, blocking collectives: 39.2 us -> none  [per_device(): whole = lax.all_gather(rotor_flux, 'azim', axis=0, tiled=True)]
    all_to_all x0 -> x1, blocking collectives: none -> 27.1 us  [per_device(): sums = lax.all_to_all(sums, ('azim', 'radax'), 0, 0, tiled=True)]
    ppermute x26 -> x8, starting transfers between devices: 42.1 us -> 15.7 us  [swap(): return (lax.ppermute(high, axis, up), lax.ppermute(low, axis, down))]
    ppermute x26 -> x8, waiting for transfers between devices: 39.5 us -> 14.5 us  [swap(): return (lax.ppermute(high, axis, up), lax.ppermute(low, axis, down))]
    reduce_sum x5 -> x0, other arithmetic: 12.7 us -> none  [the longest x3 7.95 us: per_device(): alpha = norm_now / lax.psum(jnp.sum(direction * image), ('azim', 'radax'))]
    pallas_call x0 -> x6, Pallas kernels: none -> 11.1 us  [call(): pl.pallas_call(kernel, out_shape=[jax.ShapeDtypeStruct(s, jnp.float32) fo...]
    all_to_all x0 -> x1, starting transfers between devices: none -> 10.4 us  [per_device(): turned = lax.all_to_all(spread, 'azim', 0, 0, tiled=True)]
  transfers between devices with their start and end apart: 26 -> 9, of which waited for: 21 -> 5; matrix products, arithmetic and copies ran while one was open for 2% -> 0% of each run, Pallas kernels for 0% -> 1%
where the time goes in v3:
time: 83.5 us; the launch traced here: 83.1 us
  blocking collectives  27.1 us (32%)
  starting transfers between devices  26 us (31%)
  waiting for transfers between devices  14.5 us (17%)
  Pallas kernels  11.1 us (13%)
  local copies, waits for them, and re-layouts  2.94 us (4%)
  between operations  1.39 us (2%)
    all_to_all x1, blocking collectives, per_device(): sums = lax.all_to_all(sums, ('azim', 'radax'), 0, 0, tiled=True)  27.1 us
    ppermute x8, starting transfers between devices, swap(): return (lax.ppermute(high, axis, up), lax.ppermute(low, axis, down))  15.7 us
    ppermute x8, waiting for transfers between devices, swap(): return (lax.ppermute(high, axis, up), lax.ppermute(low, axis, down))  14.5 us
    pallas_call x6, Pallas kernels, call(): pl.pallas_call(kernel, out_shape=[jax.ShapeDtypeStruct(s, jnp.float32) fo...  11.1 us
    all_to_all x1, starting transfers between devices, per_device(): turned = lax.all_to_all(spread, 'azim', 0, 0, tiled=True)  10.4 us
    unnamed x18, local copies, waits for them, and re-layouts  2.94 us
  transfers between devices with their start and end apart: 9, of which 5 were waited for; matrix products, arithmetic and copies ran while one was open for 0% of the time, Pallas kernels for 1%

profile of v3, /device:TPU:1, one launch (start us, length us, event | category | flops | bytes accessed | tf_op | source)
XLA Modules:
  0.0 83.1 jit_solution(6213864681533334551)
XLA Ops:
  0.6 0.0 copy-start.4
  0.6 0.0 copy-start.2
  0.6 0.0 copy-start
  0.7 2.3 %shard_map.68 = (f32[88,128]{1,0:T(8,128)}, f32[88,128]{1,0:T(8,128)}) custom-call(f32[3,8,64,128]{3,2,1,0:T(8,128)} %velocity.3, f32[8,64,128]{2,1,0:T(8,128)} %damping.3, f32[3,8,128]{2,1,0:T(8,128)} %weight.5), custom_call_target="tpu_custom_call" | custom-call | tf_op jit(solution)/shard_map/pallas_call | solution.py:403
  3.0 0.0 copy-done.4
  3.0 0.0 copy-done.2
  3.0 0.0 copy-done
  3.0 0.0 copy-start.5
  3.0 0.8 copy-done.5
  3.8 0.0 copy-start.7
  3.8 1.1 %shard_map.69 = (f32[16,64,128]{2,1,0:T(8,128)S(1)}, f32[16,64,128]{2,1,0:T(8,128)}, f32[4,4,128,128]{3,2,1,0:T(8,128)S(1)}) custom-call(f32[3,8,64,128]{3,2,1,0:T(8,128)S(1)} %copy-done, f32[8,64,128]{2,1,0:T(8,128)S(1)} %copy-done.2, f32[3,8,128]{2,1,0:T(8,128)S(1)} %copy-done.4, f32[88,128]{1,0:T(8,128)S(1)} %copy-done.5), custom_call_target="tpu_custom_call" | custom-call | tf_op jit(solution)/shard_map/pallas_call | solution.py:403
  4.9 0.0 copy-start.1
  4.9 1.0 %copy-done.1 = f32[4,4,128,128]{3,2,1,0:T(8,128)} copy-done((f32[4,4,128,128]{3,2,1,0:T(8,128)}, f32[4,4,128,128]{3,2,1,0:T(8,128)S(1)}, u32[]{:S(2)}) %copy-start.1) | copy-done | bytes 1048600
  5.9 2.7 %collective-permute-start = (f32[16,64,128]{2,1,0:T(8,128)}, f32[16,64,128]{2,1,0:T(8,128)S(1)}, u32[]{:S(2)}, u32[]{:S(2)}) collective-permute-start(f32[16,64,128]{2,1,0:T(8,128)} %get-tuple-element.16), channel_id=1, source_target_pairs={{0,8},{8,16},{16,24},{24,32},{32,40},{40,48},{48,56},{56,64},{64,7... | collective-permute-start | bytes 1572872 | tf_op jit(solution)/shard_map/ppermute | solution.py:417
  8.6 0.6 collective-permute-start.1
  9.1 0.0 copy-done.7
  9.1 2.1 %collective-permute-start.6 = (f32[8,128]{1,0:T(8,128)S(1)}, f32[8,128]{1,0:T(8,128)S(1)}, u32[]{:S(2)}, u32[]{:S(2)}) collective-permute-start(f32[8,128]{1,0:T(8,128)S(1)} %copy-done.7), channel_id=1, source_target_pairs={{0,1},{1,2},{2,3},{3,4},{4,5},{5,6},{6,7},{7,0},{8,9},{9,10},{10,1... | collective-permute-start | bytes 12296 | tf_op jit(solution)/shard_map/ppermute | solution.py:417
  11.2 3.0 %collective-permute-start.7 = (f32[8,128]{1,0:T(8,128)S(1)}, f32[8,128]{1,0:T(8,128)S(1)}, u32[]{:S(2)}, u32[]{:S(2)}) collective-permute-start(f32[8,128]{1,0:T(8,128)S(1)} %copy-done.7), channel_id=1, source_target_pairs={{1,0},{2,1},{3,2},{4,3},{5,4},{6,5},{7,6},{0,7},{9,8},{10,9},{11,1... | collective-permute-start | bytes 12296 | tf_op jit(solution)/shard_map/ppermute | solution.py:417
  14.2 6.6 %collective-permute-done.6.before = f32[8,128]{1,0:T(8,128)S(1)} collective-permute-done((f32[8,128]{1,0:T(8,128)S(1)}, f32[8,128]{1,0:T(8,128)S(1)}, u32[]{:S(2)}, u32[]{:S(2)}) %collective-permute-start.6) | collective-permute-done | bytes 4128 | tf_op jit(solution)/shard_map/ppermute | solution.py:417
  20.8 3.0 %collective-permute-done.7.after = f32[8,128]{1,0:T(8,128)S(1)} collective-permute-done((f32[8,128]{1,0:T(8,128)S(1)}, f32[8,128]{1,0:T(8,128)S(1)}, u32[]{:S(2)}, u32[]{:S(2)}) %collective-permute-start.7) | collective-permute-done | bytes 4128 | tf_op jit(solution)/shard_map/ppermute | solution.py:417
  23.8 0.7 shard_map.71
  24.5 0.0 copy-start.8
  24.5 0.0 copy-start.6
  24.5 10.4 %all-to-all-start = ((f32[32,16,128]{2,1,0:T(8,128)}), f32[32,16,128]{2,1,0:T(8,128)S(1)}, u32[]{:S(2)}, u32[]{:S(2)}) async-start(f32[32,16,128]{2,1,0:T(8,128)} %shard_map.71), calls=%async_computation | async-start | bytes 524288 | tf_op jit(solution)/shard_map/all_to_all | solution.py:450
  34.9 0.0 copy-done.8
  34.9 1.6 %collective-permute-start.2 = (f32[88,128]{1,0:T(8,128)S(1)}, f32[88,128]{1,0:T(8,128)S(1)}, u32[]{:S(2)}, u32[]{:S(2)}) collective-permute-start(f32[88,128]{1,0:T(8,128)S(1)} %copy-done.8), channel_id=1, source_target_pairs={{0,1},{1,2},{2,3},{3,4},{4,5},{5,6},{6,7},{7,0},{8,9},{9,10},{10,1... | collective-permute-start | bytes 135176 | tf_op jit(solution)/shard_map/ppermute | solution.py:417
  36.5 0.0 copy-done.6
  36.5 3.5 %collective-permute-start.3 = (f32[88,128]{1,0:T(8,128)S(1)}, f32[88,128]{1,0:T(8,128)S(1)}, u32[]{:S(2)}, u32[]{:S(2)}) collective-permute-start(f32[88,128]{1,0:T(8,128)S(1)} %copy-done.6), channel_id=1, source_target_pairs={{1,0},{2,1},{3,2},{4,3},{5,4},{6,5},{7,6},{0,7},{9,8},{10,9},{11,1... | collective-permute-start | bytes 135176 | tf_op jit(solution)/shard_map/ppermute | solution.py:417
  40.1 1.7 %collective-permute-done.2.before = f32[88,128]{1,0:T(8,128)S(1)} collective-permute-done((f32[88,128]{1,0:T(8,128)S(1)}, f32[88,128]{1,0:T(8,128)S(1)}, u32[]{:S(2)}, u32[]{:S(2)}) %collective-permute-start.2) | collective-permute-done | bytes 45088 | tf_op jit(solution)/shard_map/ppermute | solution.py:417
  41.8 1.9 %collective-permute-done.3.after = f32[88,128]{1,0:T(8,128)S(1)} collective-permute-done((f32[88,128]{1,0:T(8,128)S(1)}, f32[88,128]{1,0:T(8,128)S(1)}, u32[]{:S(2)}, u32[]{:S(2)}) %collective-permute-start.3) | collective-permute-done | bytes 45088 | tf_op jit(solution)/shard_map/ppermute | solution.py:417
  43.7 1.2 %collective-permute-start.5 = (f32[152,128]{1,0:T(8,128)S(1)}, f32[152,128]{1,0:T(8,128)S(1)}, u32[]{:S(2)}, u32[]{:S(2)}) collective-permute-start(f32[152,128]{1,0:T(8,128)S(1)} %shard_map.70), channel_id=1, source_target_pairs={{8,0},{16,8},{24,16},{32,24},{40,32},{48,40},{56,48},{64,56},{72,6... | collective-permute-start | bytes 233480 | tf_op jit(solution)/shard_map/ppermute | solution.py:417
  44.9 1.0 %collective-permute-start.4 = (f32[152,128]{1,0:T(8,128)S(1)}, f32[152,128]{1,0:T(8,128)S(1)}, u32[]{:S(2)}, u32[]{:S(2)}) collective-permute-start(f32[152,128]{1,0:T(8,128)S(1)} %shard_map.70), channel_id=1, source_target_pairs={{0,8},{8,16},{16,24},{24,32},{32,40},{40,48},{48,56},{56,64},{64,7... | collective-permute-start | bytes 233480 | tf_op jit(solution)/shard_map/ppermute | solution.py:417
  46.5 1.3 %collective-permute-done.5.upper_rim = f32[152,128]{1,0:T(8,128)S(1)} collective-permute-done((f32[152,128]{1,0:T(8,128)S(1)}, f32[152,128]{1,0:T(8,128)S(1)}, u32[]{:S(2)}, u32[]{:S(2)}) %collective-permute-start.5) | collective-permute-done | bytes 77856 | tf_op jit(solution)/shard_map/ppermute | solution.py:417
  47.9 0.0 collective-permute-done.4.lower_rim
  47.9 0.0 all-to-all-done.turned
  47.9 0.0 collective-permute-done.lower
  47.9 0.0 collective-permute-done.1.upper
  47.9 5.1 %shard_map.72 = (f32[10,160,128]{2,1,0:T(8,128)S(1)}, f32[10,160,128]{2,1,0:T(8,128)S(1)}, f32[10,160,128]{2,1,0:T(8,128)S(1)}, f32[10,160,128]{2,1,0:T(8,128)S(...) custom-call(s32[1]{0:T(128)S(6)} %copy.7.offset, ...), custom_call_target="tpu_custom_call" | custom-call | tf_op jit(solution)/shard_map/pallas_call | solution.py:403
  53.0 27.1 %all_to_all.10.sums = f32[256,1,128]{2,1,0:T(1,128)S(1)} all-to-all(f32[256,1,128]{2,1,0:T(1,128)S(1)} %get-tuple-element.19), channel_id=1, replica_groups=mesh['azim'=32,'radax'=8] {'azim','radax'}, dimensions={0} | all-to-all | bytes 262144 | tf_op jit(solution)/shard_map/all_to_all | solution.py:482
  80.1 0.0 copy-start.3
  80.1 1.1 %copy-done.3 = f32[10,160,128]{2,1,0:T(8,128)S(1)} copy-done((f32[10,160,128]{2,1,0:T(8,128)S(1)}, f32[10,160,128]{2,1,0:T(8,128)}, u32[]{:S(2)}) %copy-start.3) | copy-done | bytes 819224
  81.2 1.9 %shard_map.73 = (f32[3,8,64,128]{3,2,1,0:T(8,128)}, f32[8,64,128]{2,1,0:T(8,128)}) custom-call(f32[256,1,128]{2,1,0:T(1,128)S(1)} %all_to_all.10.sums, f32[10,160,128]{2,1,0:T(8,128)S(1)} %get-tuple-element.20.p0, f32[10,160,128]{2,1,0:T(8,128)S(1)} %get-tuple-element.21.p1, f32[10,160,128]{2,1,0:T(8,128)S(1)} %get-tuple-element.22.p2, ...), custom_call_target="tpu_custom_call" | custom-call | tf_op jit(solution)/shard_map/pallas_call | solution.py:403
  (1 shorter events, 0.0 us)
Async XLA Ops:
  0.6 2.3 %copy-start.4 = (f32[3,8,128]{2,1,0:T(8,128)S(1)}, f32[3,8,128]{2,1,0:T(8,128)}, u32[]{:S(2)}) copy-start(f32[3,8,128]{2,1,0:T(8,128)} %weight.5) | copy-start | bytes 36868
  0.6 2.3 %copy-start.2 = (f32[8,64,128]{2,1,0:T(8,128)S(1)}, f32[8,64,128]{2,1,0:T(8,128)}, u32[]{:S(2)}) copy-start(f32[8,64,128]{2,1,0:T(8,128)} %damping.3) | copy-start | bytes 786436
  0.6 2.3 %copy-start = (f32[3,8,64,128]{3,2,1,0:T(8,128)S(1)}, f32[3,8,64,128]{3,2,1,0:T(8,128)}, u32[]{:S(2)}) copy-start(f32[3,8,64,128]{3,2,1,0:T(8,128)} %velocity.3) | copy-start | bytes 2359300
  3.0 0.8 copy-start.5
  3.8 5.3 %copy-start.7 = (f32[8,128]{1,0:T(8,128)S(1)}, f32[8,128]{1,0:T(8,128)}, u32[]{:S(2)}) copy-start(f32[8,128]{1,0:T(8,128)} %rotor.1) | copy-start | bytes 12292
  4.9 1.0 %copy-start.1 = (f32[4,4,128,128]{3,2,1,0:T(8,128)}, f32[4,4,128,128]{3,2,1,0:T(8,128)S(1)}, u32[]{:S(2)}) copy-start(f32[4,4,128,128]{3,2,1,0:T(8,128)S(1)} %get-tuple-element.15.own) | copy-start | bytes 3145732
  5.9 42.0 %collective-permute-start = (f32[16,64,128]{2,1,0:T(8,128)}, f32[16,64,128]{2,1,0:T(8,128)S(1)}, u32[]{:S(2)}, u32[]{:S(2)}) collective-permute-start(f32[16,64,128]{2,1,0:T(8,128)} %get-tuple-element.16), channel_id=1, source_target_pairs={{0,8},{8,16},{16,24},{24,32},{32,40},{40,48},{48,56},{56,64},{64,7... | collective-permute-start | bytes 1572872 | tf_op jit(solution)/shard_map/ppermute | solution.py:417
  8.6 39.3 %collective-permute-start.1 = (f32[16,64,128]{2,1,0:T(8,128)S(1)}, f32[16,64,128]{2,1,0:T(8,128)S(1)}, u32[]{:S(2)}, u32[]{:S(2)}) collective-permute-start(f32[16,64,128]{2,1,0:T(8,128)S(1)} %get-tuple-element.17), channel_id=1, source_target_pairs={{8,0},{16,8},{24,16},{32,24},{40,32},{48,40},{56,48},{64,56},{72,6... | collective-permute-start | bytes 1572872 | tf_op jit(solution)/shard_map/ppermute | solution.py:417
  9.1 11.6 %collective-permute-start.6 = (f32[8,128]{1,0:T(8,128)S(1)}, f32[8,128]{1,0:T(8,128)S(1)}, u32[]{:S(2)}, u32[]{:S(2)}) collective-permute-start(f32[8,128]{1,0:T(8,128)S(1)} %copy-done.7), channel_id=1, source_target_pairs={{0,1},{1,2},{2,3},{3,4},{4,5},{5,6},{6,7},{7,0},{8,9},{9,10},{10,1... | collective-permute-start | bytes 12296 | tf_op jit(solution)/shard_map/ppermute | solution.py:417
  11.2 12.6 %collective-permute-start.7 = (f32[8,128]{1,0:T(8,128)S(1)}, f32[8,128]{1,0:T(8,128)S(1)}, u32[]{:S(2)}, u32[]{:S(2)}) collective-permute-start(f32[8,128]{1,0:T(8,128)S(1)} %copy-done.7), channel_id=1, source_target_pairs={{1,0},{2,1},{3,2},{4,3},{5,4},{6,5},{7,6},{0,7},{9,8},{10,9},{11,1... | collective-permute-start | bytes 12296 | tf_op jit(solution)/shard_map/ppermute | solution.py:417
  24.5 10.4 %copy-start.8 = (f32[88,128]{1,0:T(8,128)S(1)}, f32[88,128]{1,0:T(8,128)}, u32[]{:S(2)}) copy-start(f32[88,128]{1,0:T(8,128)} %get-tuple-element.18) | copy-start | bytes 135172
  24.5 12.0 %copy-start.6 = (f32[88,128]{1,0:T(8,128)S(1)}, f32[88,128]{1,0:T(8,128)}, u32[]{:S(2)}) copy-start(f32[88,128]{1,0:T(8,128)} %get-tuple-element.14.order) | copy-start | bytes 135172
  24.5 23.4 %all-to-all-start = ((f32[32,16,128]{2,1,0:T(8,128)}), f32[32,16,128]{2,1,0:T(8,128)S(1)}, u32[]{:S(2)}, u32[]{:S(2)}) async-start(f32[32,16,128]{2,1,0:T(8,128)} %shard_map.71), calls=%async_computation | async-start | bytes 524288 | tf_op jit(solution)/shard_map/all_to_all | solution.py:450
  34.9 6.9 %collective-permute-start.2 = (f32[88,128]{1,0:T(8,128)S(1)}, f32[88,128]{1,0:T(8,128)S(1)}, u32[]{:S(2)}, u32[]{:S(2)}) collective-permute-start(f32[88,128]{1,0:T(8,128)S(1)} %copy-done.8), channel_id=1, source_target_pairs={{0,1},{1,2},{2,3},{3,4},{4,5},{5,6},{6,7},{7,0},{8,9},{9,10},{10,1... | collective-permute-start | bytes 135176 | tf_op jit(solution)/shard_map/ppermute | solution.py:417
  36.5 7.1 %collective-permute-start.3 = (f32[88,128]{1,0:T(8,128)S(1)}, f32[88,128]{1,0:T(8,128)S(1)}, u32[]{:S(2)}, u32[]{:S(2)}) collective-permute-start(f32[88,128]{1,0:T(8,128)S(1)} %copy-done.6), channel_id=1, source_target_pairs={{1,0},{2,1},{3,2},{4,3},{5,4},{6,5},{7,6},{0,7},{9,8},{10,9},{11,1... | collective-permute-start | bytes 135176 | tf_op jit(solution)/shard_map/ppermute | solution.py:417
  43.7 4.2 %collective-permute-start.5 = (f32[152,128]{1,0:T(8,128)S(1)}, f32[152,128]{1,0:T(8,128)S(1)}, u32[]{:S(2)}, u32[]{:S(2)}) collective-permute-start(f32[152,128]{1,0:T(8,128)S(1)} %shard_map.70), channel_id=1, source_target_pairs={{8,0},{16,8},{24,16},{32,24},{40,32},{48,40},{56,48},{64,56},{72,6... | collective-permute-start | bytes 233480 | tf_op jit(solution)/shard_map/ppermute | solution.py:417
  44.9 3.0 %collective-permute-start.4 = (f32[152,128]{1,0:T(8,128)S(1)}, f32[152,128]{1,0:T(8,128)S(1)}, u32[]{:S(2)}, u32[]{:S(2)}) collective-permute-start(f32[152,128]{1,0:T(8,128)S(1)} %shard_map.70), channel_id=1, source_target_pairs={{0,8},{8,16},{16,24},{24,32},{32,40},{40,48},{48,56},{56,64},{64,7... | collective-permute-start | bytes 233480 | tf_op jit(solution)/shard_map/ppermute | solution.py:417
  80.1 1.1 %copy-start.3 = (f32[10,160,128]{2,1,0:T(8,128)S(1)}, f32[10,160,128]{2,1,0:T(8,128)}, u32[]{:S(2)}) copy-start(f32[10,160,128]{2,1,0:T(8,128)} %get-tuple-element.25.s2) | copy-start | bytes 2457604

commit v4 on v3

--- a/solution.py
+++ b/solution.py
@@ -13,14 +13,14 @@
 FRONT = 16
 TALL = LANES + 2 * FRONT
 TILES = LANES // 8
-VMEM_LIMIT = 48 * 1024 * 1024
-WHOLE_VMEM = 62 * 1024 * 1024
+VMEM_LIMIT = 32 * 1024 * 1024
 DEPTHS = (5, 4, 4, 2)
 STARTS = (0, 5, 9, 13)
 PLANES = 15
 REACH = (4, 4, 5, 2)
 FROM = (0, 4, 8, 13)
 STRIP = 16
+RIM = 16
 BODY = slice(FRONT, FRONT + LANES)
 
 
@@ -41,72 +41,95 @@
     return jnp.concatenate([first, second], axis=0).T
 
 
-def edge_kernel(velocity, damping, weight, to_left, to_right, vel, damp, wt, turned, sems):
-    cells = damping.shape[0]
+def edge_kernel(
+    velocity,
+    damping,
+    weight,
+    rotor,
+    to_left,
+    to_right,
+    low,
+    high,
+    own,
+    vel,
+    damp,
+    wt,
+    rt,
+    sems,
+):
+    cells, rows = damping.shape[0], damping.shape[1]
     pairs = cells // 2
-    copies = [pltpu.make_async_copy(damping, damp, sems.at[3])]
-    copies += [pltpu.make_async_copy(velocity.at[k], vel.at[k], sems.at[k]) for k in range(3)]
+    copies = [pltpu.make_async_copy(velocity.at[k], vel.at[k], sems.at[k]) for k in range(3)]
+    copies += [pltpu.make_async_copy(damping, damp, sems.at[3])]
     copies += [pltpu.make_async_copy(weight, wt, sems.at[4])]
+    copies += [pltpu.make_async_copy(rotor, rt, sems.at[5])]
     for copy in copies:
         copy.start()
-    for copy in copies:
+    fields = [vel.at[0], vel.at[1], vel.at[2], damp]
+    for number, field in enumerate(fields):
+        copies[number].wait()
+        reach, start = REACH[number], FROM[number]
+        for i in range(pairs):
+            base = STRIP * i + start
+            own[number, i] = paired(field[i], field[cells - 1 - i])
+            to_left[base : base + reach] = own[number, i, 0:reach]
+            to_right[base : base + reach] = own[number, i, LANES - reach : LANES]
+        depth, start = DEPTHS[number], STARTS[number]
+        low[start : start + depth] = field[0:depth]
+        high[start : start + depth] = field[cells - depth : cells]
+    for message in (to_left, to_right):
+        for i in range(pairs):
+            row = STRIP * i + STRIP - 1
+            message[row : row + 1] = jnp.zeros((1, LANES), jnp.float32)
+    for copy in copies[4:]:
         copy.wait()
-    fields = [vel.at[0], vel.at[1], vel.at[2], damp]
-    for i in range(pairs):
-        base = STRIP * i
-        for field, reach, start in zip(fields, REACH, FROM):
-            turned[...] = paired(field[i], field[cells - 1 - i])
-            rows = slice(base + start, base + start + reach)
-            to_left[rows] = turned[0:reach]
-            to_right[rows] = turned[LANES - reach : LANES]
-        for message in (to_left, to_right):
-            message[base + STRIP - 1 : base + STRIP] = jnp.zeros((1, LANES), jnp.float32)
+    base = STRIP * pairs
     for tap in range(3):
-        rows = slice(STRIP * pairs + tap * cells, STRIP * pairs + (tap + 1) * cells)
+        rows = slice(tap * cells, (tap + 1) * cells)
+        low[PLANES, rows] = wt[tap]
+        high[PLANES, rows] = wt[tap]
+        rows = slice(base + tap * cells, base + (tap + 1) * cells)
         to_left[rows] = wt[tap]
         to_right[rows] = wt[tap]
-
-
-def plane_kernel(velocity, damping, weight, order, low, high, own):
-    cells, rows = damping.shape[0], damping.shape[1]
-    fields = [velocity.at[0], velocity.at[1], velocity.at[2], damping]
-    for number, (field, depth, start) in enumerate(zip(fields, DEPTHS, STARTS)):
-        low[start : start + depth] = field[0:depth]
-        high[start : start + depth] = field[cells - depth : cells]
-        for i in range(cells // 2):
-            own[number, i] = paired(field[i], field[cells - 1 - i])
-    for message in (low, high):
-        for tap in range(3):
-            message[PLANES, tap * cells : (tap + 1) * cells] = weight[tap]
-        message[PLANES, 3 * cells : rows] = jnp.zeros((rows - 3 * cells, LANES), jnp.float32)
-
-
-def spread_kernel(before, after, rotor, spread):
-    own = rotor[...]
-    rim = jnp.where(iota(own.shape, 1) < HALF, after[...], before[...])
-    for k in range(spread.shape[0]):
-        spread[k, 0:8] = own
-        spread[k, 8:16] = rim
-
-
-def corner_kernel(before, after, corner):
-    strips = before.shape[0] - 24
-    corner[0:strips] = before[0:strips]
-    corner[strips : 2 * strips] = after[0:strips]
-    left = iota((24, LANES), 1) < HALF
-    corner[2 * strips : 2 * strips + 24] = jnp.where(left, after[strips:], before[strips:])
+    rows = slice(base + 3 * cells, base + 4 * cells)
+    to_left[rows] = rt[...]
+    to_right[rows] = rt[...]
+
+
+def corner_kernel(before, after, sent, low_in, high_in, low, high, spread, ready, sem):
+    rows, cells = low.shape[1], ready.shape[2] // LANES - 1
+    strips = before.shape[0] - 4 * cells
+    lines = strips + 3 * cells
+    left = iota((3 * cells, LANES), 1) < HALF
+    rims = jnp.where(left, after[strips:lines], before[strips:lines])
+    own = sent[lines : lines + cells]
+    rim = jnp.where(left[0:cells], after[lines : lines + cells], before[lines : lines + cells])
+    group = iota((1, LANES), 1) // RIM
+    packed = jnp.zeros((1, LANES), jnp.float32)
+    for r in range(cells):
+        packed = jnp.where(group == r, spin(rim[r : r + 1], RIM // 2 + RIM * r), packed)
+    for k in range(ready.shape[0]):
+        for r in range(cells):
+            ready[k, :, LANES * r : LANES * r + LANES] = own[r : r + 1]
+        ready[k, :, LANES * cells :] = packed
+    copy = pltpu.make_async_copy(ready, spread, sem.at[0])
+    copy.start()
+    for message, base in ((low, low_in), (high, high_in)):
+        message[0:PLANES] = base[0:PLANES]
+        message[PLANES, 0 : 3 * cells] = base[PLANES, 0 : 3 * cells]
+        message[PLANES, 3 * cells : 6 * cells] = rims
+        message[PLANES, 6 * cells : rows] = jnp.zeros((rows - 6 * cells, LANES), jnp.float32)
+        message[PLANES + 1] = before[0:strips]
+        message[PLANES + 2] = after[0:strips]
+    copy.wait()
 
 
 def basis_kernel(
     offset,
-    weight,
     own,
+    mine,
     lower,
     upper,
-    before,
-    after,
-    lower_rim,
-    upper_rim,
     turned,
     p0,
     p1,
@@ -126,8 +149,8 @@
     line,
     face,
 ):
-    cells = weight.shape[1]
-    pairs = cells // 2
+    pairs = own.shape[1]
+    cells = 2 * pairs
     last = HALO + pairs - 1
     total = turned.shape[0] * cells
     every = range(TILES + 2)
@@ -166,17 +189,17 @@
         lax.fori_loop(0, pairs, fill, 0, unroll=True)
 
     left = iota((STRIP, LANES), 1) < HALF
-    size = STRIP * pairs
-    for side, message in enumerate((before, after)):
+    for side in range(2):
         for i in range(HALO + pairs):
-            pair = max(HALO - 1 - i, 0) if i else pairs - 1
-            rows = slice(side * size + STRIP * pair, side * size + STRIP * pair + STRIP)
+            pair = i - HALO if i >= HALO else min(HALO - 1 - i, pairs - 1)
+            rows = slice(STRIP * pair, STRIP * pair + STRIP)
+            under, over = lower[PLANES + 1 + side, rows], upper[PLANES + 1 + side, rows]
             if i >= HALO:
-                strip[side, i] = message[STRIP * (i - HALO) : STRIP * (i - HALO) + STRIP]
+                strip[side, i] = mine[PLANES + 1 + side, rows]
             elif i:
-                strip[side, i] = spin(jnp.where(left, upper_rim[rows], lower_rim[rows]), HALF)
+                strip[side, i] = spin(jnp.where(left, over, under), HALF)
             else:
-                strip[side, i] = jnp.where(left, lower_rim[rows], upper_rim[rows])
+                strip[side, i] = jnp.where(left, under, over)
     for number, field in enumerate((v0, v1, v2, diag)):
         reach, start = REACH[number], FROM[number]
         for i in range(HALO - DEPTHS[number], HALO + pairs):
@@ -189,27 +212,20 @@
         seam(field)
 
     wide = cells + 6
-    rim_left = iota((cells, LANES), 1) < HALF
-    for tap in range(3):
-        k = tap * cells
-        taps[0, tap, 0:3] = lower[PLANES, k + cells - 3 : k + cells]
-        taps[0, tap, 3 : 3 + cells] = weight[tap]
-        taps[0, tap, 3 + cells : wide] = upper[PLANES, k : k + 3]
-        k += 2 * size
-        taps[1, tap, 0:3] = lower_rim[k + cells - 3 : k + cells]
-        k -= size
-        taps[1, tap, 3 : 3 + cells] = jnp.where(
-            rim_left, after[k : k + cells], before[k : k + cells]
-        )
-        k += size
-        taps[1, tap, 3 + cells : wide] = upper_rim[k : k + 3]
+    for part in range(2):
+        for tap in range(3):
+            k = (3 * part + tap) * cells
+            taps[part, tap, 0:3] = lower[PLANES, k + cells - 3 : k + cells]
+            taps[part, tap, 3 : 3 + cells] = mine[PLANES, k : k + cells]
+            taps[part, tap, 3 + cells : wide] = upper[PLANES, k : k + 3]
     begin = lax.axis_index("azim") * cells - offset[0] - 4 + 2 * total
     for k in range(wide + 2):
         source = lax.rem(begin + k, total)
         block = source // cells
         row = lax.rem(source, cells)
-        rot[0, k : k + 1] = turned[block, pl.ds(row, 1)]
-        rot[1, k : k + 1] = turned[block, pl.ds(row + 8, 1)]
+        rot[0, k : k + 1] = turned[block, :, pl.ds(pl.multiple_of(row * LANES, LANES), LANES)]
+        packed = turned[block, :, LANES * cells :]
+        rot[1, k : k + 1] = pltpu.roll(packed, 2 * LANES - RIM // 2 - RIM * row, 1)
     for part in range(2):
         flux = jnp.zeros((wide, LANES), jnp.float32)
         for tap in range(3):
@@ -394,19 +410,29 @@
     lax.fori_loop(HALO, last + 1, gradient, 0, unroll=True)
 
 
-def call(kernel, shapes, operands, scratch=(), spaces=None, sems=0, limit=VMEM_LIMIT):
+def call(
+    kernel, shapes, operands, scratch=(), spaces=None, outs=None, sems=0
+):
     spec = lambda space: pl.BlockSpec(memory_space=space)
     spaces = spaces or [pltpu.VMEM] * len(operands)
+    outs = outs or [pltpu.VMEM] * len(shapes)
+    operands = [
+        pltpu.with_memory_space_constraint(x, pltpu.HBM) if space is pltpu.HBM else x
+        for x, space in zip(operands, spaces)
+    ]
     buffers = [pltpu.VMEM(s, jnp.float32) for s in scratch]
     if sems:
         buffers.append(pltpu.SemaphoreType.DMA((sems,)))
     return pl.pallas_call(
         kernel,
-        out_shape=[jax.ShapeDtypeStruct(s, jnp.float32) for s in shapes],
+        out_shape=[
+            space(s, jnp.float32) if space is pltpu.HBM else jax.ShapeDtypeStruct(s, jnp.float32)
+            for s, space in zip(shapes, outs)
+        ],
         in_specs=[spec(space) for space in spaces],
-        out_specs=[spec(pltpu.VMEM)] * len(shapes),
+        out_specs=[spec(space) for space in outs],
         scratch_shapes=buffers,
-        compiler_params=pltpu.CompilerParams(vmem_limit_bytes=limit),
+        compiler_params=pltpu.CompilerParams(vmem_limit_bytes=VMEM_LIMIT),
     )(*operands)
 
 
@@ -424,50 +450,32 @@
     plane = (rows, LANES)
     block = (LANES, LANES)
     pairs = cells // 2
-    rotor_before, rotor_after = swap(rotor_flux, rotor_flux, "radax")
-    strips = (STRIP * pairs + 3 * cells, LANES)
-    to_left, to_right = call(
+    strips = (STRIP * pairs + 4 * cells, LANES)
+    message = (PLANES + 3,) + plane
+    to_left, to_right, low, high, own = call(
         edge_kernel,
-        [strips, strips],
-        (velocity, damping, correlation_weight),
-        scratch=[(3, cells) + plane, (cells,) + plane, (3, cells, LANES), block],
-        spaces=[pl.ANY] * 3,
-        sems=5,
-        limit=WHOLE_VMEM,
+        [strips, strips, message, message, (4, pairs) + block],
+        (velocity, damping, correlation_weight, rotor_flux),
+        scratch=[(3, cells) + plane, (cells,) + plane, (3, cells, LANES), (cells, LANES)],
+        spaces=[pltpu.HBM] * 4,
+        sems=6,
     )
     before, after = swap(to_left, to_right, "radax")
-    message = (PLANES + 1,) + plane
-    low, high, own = call(
-        plane_kernel,
-        [message, message, (4, pairs) + block],
-        (velocity, damping, correlation_weight, to_left),
-        spaces=[pltpu.VMEM] * 3 + [pl.ANY],
+    low, high, spread = call(
+        corner_kernel,
+        [message, message, (azim, 1, LANES * (cells + 1))],
+        (before, after, to_left, low, high),
+        scratch=[(azim, 1, LANES * (cells + 1))],
+        outs=[pltpu.VMEM, pltpu.VMEM, pltpu.HBM],
+        sems=1,
     )
     lower, upper = swap(low, high, "azim")
-    (spread,) = call(
-        spread_kernel, [(azim, 16, LANES)], (rotor_before, rotor_after, rotor_flux)
-    )
     turned = lax.all_to_all(spread, "azim", 0, 0, tiled=True)
-    (corner,) = call(
-        corner_kernel, [(2 * STRIP * pairs + 3 * cells, LANES)], (before, after)
-    )
-    lower_rim, upper_rim = swap(corner, corner, "azim")
     field = (HALO + pairs + 1, TALL, LANES)
     *fields, sums = call(
         basis_kernel,
         [field] * 6 + [(devices, 1, LANES)],
-        (
-            offset,
-            correlation_weight,
-            own,
-            lower,
-            upper,
-            before,
-            after,
-            lower_rim,
-            upper_rim,
-            turned,
-        ),
+        (offset, own, low, lower, upper, turned),
         scratch=[field] * 4
         + [
             (2, HALO + pairs, STRIP, LANES),
@@ -477,7 +485,7 @@
             (TALL, LANES),
             field,
         ],
-        spaces=[pltpu.SMEM] + [pltpu.VMEM] * 9,
+        spaces=[pltpu.SMEM] + [pltpu.VMEM] * 5,
     )
     sums = lax.all_to_all(sums, ("azim", "radax"), 0, 0, tiled=True)
     return call(

time: 83.5 us -> 63.8 us (0.76)
  starting transfers between devices: 26 us -> 20.8 us
  blocking collectives: 27.1 us -> 23.2 us
  Pallas kernels: 11.1 us -> 7.3 us
  waiting for transfers between devices: 14.5 us -> 11 us
  local copies, waits for them, and re-layouts: 2.94 us -> 0 us
    ppermute x8 -> x4, waiting for transfers between devices: 14.5 us -> 2.16 us  [swap(): return (lax.ppermute(high, axis, up), lax.ppermute(low, axis, down))]
    all_to_all x1, waiting for transfers between devices: 0.01 us -> 8.87 us  [per_device(): turned = lax.all_to_all(spread, 'azim', 0, 0, tiled=True)]
    ppermute x8 -> x4, starting transfers between devices: 15.7 us -> 9.03 us  [swap(): return (lax.ppermute(high, axis, up), lax.ppermute(low, axis, down))]
    all_to_all x1, blocking collectives: 27.1 us -> 23.2 us  [per_device(): sums = lax.all_to_all(sums, ('azim', 'radax'), 0, 0, tiled=True)]
    pallas_call x6 -> x4, Pallas kernels: 11.1 us -> 7.3 us  [call(): pl.pallas_call(kernel, out_shape=[space(s, jnp.float32) if space is pltpu...]
    unnamed x18 -> x0, local copies, waits for them, and re-layouts: 2.94 us -> none
    all_to_all x1, starting transfers between devices: 10.4 us -> 11.7 us  [per_device(): turned = lax.all_to_all(spread, 'azim', 0, 0, tiled=True)]
  transfers between devices with their start and end apart: 9 -> 5, of which waited for: 5 -> 3; matrix products, arithmetic and copies ran while one was open for 0% -> 0% of each run, Pallas kernels for 1% -> 0%
where the time goes in v4:
time: 63.8 us; the launch traced here: 63.6 us
  blocking collectives  23.2 us (36%)
  starting transfers between devices  20.8 us (33%)
  waiting for transfers between devices  11 us (17%)
  Pallas kernels  7.3 us (11%)
  between operations  1.31 us (2%)
    all_to_all x1, blocking collectives, per_device(): sums = lax.all_to_all(sums, ('azim', 'radax'), 0, 0, tiled=True)  23.2 us
    all_to_all x1, starting transfers between devices, per_device(): turned = lax.all_to_all(spread, 'azim', 0, 0, tiled=True)  11.7 us
    ppermute x4, starting transfers between devices, swap(): return (lax.ppermute(high, axis, up), lax.ppermute(low, axis, down))  9.03 us
    all_to_all x1, waiting for transfers between devices, per_device(): turned = lax.all_to_all(spread, 'azim', 0, 0, tiled=True)  8.87 us
    pallas_call x4, Pallas kernels, call(): pl.pallas_call(kernel, out_shape=[space(s, jnp.float32) if space is pltpu...  7.3 us
    ppermute x4, waiting for transfers between devices, swap(): return (lax.ppermute(high, axis, up), lax.ppermute(low, axis, down))  2.16 us
  transfers between devices with their start and end apart: 5, of which 3 were waited for; matrix products, arithmetic and copies ran while one was open for 0% of the time, Pallas kernels for 0%

profile of v4, /device:TPU:1, one launch (start us, length us, event | category | flops | bytes accessed | tf_op | source)
XLA Modules:
  0.0 63.6 jit_solution(14183222974354011932)
XLA Ops:
  0.6 1.6 %shard_map.68 = (f32[96,128]{1,0:T(8,128)S(1)}, f32[96,128]{1,0:T(8,128)S(1)}, f32[18,64,128]{2,1,0:T(8,128)S(1)}, f32[18,64,128]{2,1,0:T(8,128)S(1)}, f32[4,4,128,128]{3,2,1,0:T(8,128)S(1)}) custom-call(f32[3,8,64,128]{3,2,1,0:T(8,128)} %velocity.1, f32[8,64,128]{2,1,0:T(8,128)} %damping.1, f32[3,8,128]{2,1,0:T(8,128)} %weight.1, f32[8,128]{1,0:T(8,128)} %rotor.1), custom_call_target="tpu_custom_call" | custom-call | tf_op jit(solution)/shard_map/pallas_call | solution.py:426
  2.2 3.8 %collective-permute-start = (f32[96,128]{1,0:T(8,128)S(1)}, f32[96,128]{1,0:T(8,128)S(1)}, u32[]{:S(2)}, u32[]{:S(2)}) collective-permute-start(f32[96,128]{1,0:T(8,128)S(1)} %get-tuple-element.18), channel_id=1, source_target_pairs={{0,1},{1,2},{2,3},{3,4},{4,5},{5,6},{6,7},{7,0},{8,9},{9,10},{10,1... | collective-permute-start | bytes 147464 | tf_op jit(solution)/shard_map/ppermute | solution.py:443
  6.1 2.3 %collective-permute-start.1 = (f32[96,128]{1,0:T(8,128)S(1)}, f32[96,128]{1,0:T(8,128)S(1)}, u32[]{:S(2)}, u32[]{:S(2)}) collective-permute-start(f32[96,128]{1,0:T(8,128)S(1)} %get-tuple-element.19.sent), channel_id=1, source_target_pairs={{1,0},{2,1},{3,2},{4,3},{5,4},{6,5},{7,6},{0,7},{9,8},{10,9},{11,1... | collective-permute-start | bytes 147464 | tf_op jit(solution)/shard_map/ppermute | solution.py:443
  8.3 1.4 %collective-permute-done.before = f32[96,128]{1,0:T(8,128)S(1)} collective-permute-done((f32[96,128]{1,0:T(8,128)S(1)}, f32[96,128]{1,0:T(8,128)S(1)}, u32[]{:S(2)}, u32[]{:S(2)}) %collective-permute-start) | collective-permute-done | bytes 49184 | tf_op jit(solution)/shard_map/ppermute | solution.py:443
  9.7 0.8 %collective-permute-done.1.after = f32[96,128]{1,0:T(8,128)S(1)} collective-permute-done((f32[96,128]{1,0:T(8,128)S(1)}, f32[96,128]{1,0:T(8,128)S(1)}, u32[]{:S(2)}, u32[]{:S(2)}) %collective-permute-start.1) | collective-permute-done | bytes 49184 | tf_op jit(solution)/shard_map/ppermute | solution.py:443
  10.5 0.8 %shard_map.69 = (f32[18,64,128]{2,1,0:T(8,128)S(1)}, f32[18,64,128]{2,1,0:T(8,128)S(1)}, f32[32,1,1152]{2,1,0:T(1,128)}) custom-call(f32[96,128]{1,0:T(8,128)S(1)} %collective-permute-done.before, f32[96,128]{1,0:T(8,128)S(1)} %collective-permute-done.1.after, f32[96,128]{1,0:T(8,128)S(1)} %get-tuple-element.19.sent, ...), custom_call_target="tpu_custom_call" | custom-call | tf_op jit(solution)/shard_map/pallas_call | solution.py:426
  11.3 2.8 %collective-permute-start.2 = (f32[18,64,128]{2,1,0:T(8,128)S(1)}, f32[18,64,128]{2,1,0:T(8,128)S(1)}, u32[]{:S(2)}, u32[]{:S(2)}) collective-permute-start(f32[18,64,128]{2,1,0:T(8,128)S(1)} %get-tuple-element.23), channel_id=1, source_target_pairs={{0,8},{8,16},{16,24},{24,32},{32,40},{40,48},{48,56},{56,64},{64,7... | collective-permute-start | bytes 1769480 | tf_op jit(solution)/shard_map/ppermute | solution.py:443
  14.1 0.1 collective-permute-start.3
  14.3 11.7 %all-to-all-start = ((f32[32,1,1152]{2,1,0:T(1,128)}), f32[32,1,1152]{2,1,0:T(1,128)S(1)}, u32[]{:S(2)}, u32[]{:S(2)}) async-start(f32[32,1,1152]{2,1,0:T(1,128)} %get-tuple-element.24), calls=%async_computation | async-start | bytes 294912 | tf_op jit(solution)/shard_map/all_to_all | solution.py:473
  26.6 8.9 %all-to-all-done.turned = f32[32,1,1152]{2,1,0:T(1,128)S(1)} async-done(((f32[32,1,1152]{2,1,0:T(1,128)}), f32[32,1,1152]{2,1,0:T(1,128)S(1)}, u32[]{:S(2)}, u32[]{:S(2)}) %all-to-all-start) | async-done | bytes 147488 | tf_op jit(solution)/shard_map/all_to_all | solution.py:473
  35.5 0.0 collective-permute-done.2.lower
  35.5 0.0 collective-permute-done.3.upper
  35.5 3.0 %shard_map.70 = (f32[10,160,128]{2,1,0:T(8,128)S(1)}, f32[10,160,128]{2,1,0:T(8,128)S(1)}, f32[10,160,128]{2,1,0:T(8,128)S(1)}, f32[10,160,128]{2,1,0:T(8,128)S(...) custom-call(s32[1]{0:T(128)S(6)} %copy.7.offset, ...), custom_call_target="tpu_custom_call" | custom-call | tf_op jit(solution)/shard_map/pallas_call | solution.py:426
  38.5 23.2 %all_to_all.10.sums = f32[256,1,128]{2,1,0:T(1,128)S(1)} all-to-all(f32[256,1,128]{2,1,0:T(1,128)S(1)} %get-tuple-element.25), channel_id=1, replica_groups=mesh['azim'=32,'radax'=8] {'azim','radax'}, dimensions={0} | all-to-all | bytes 262144 | tf_op jit(solution)/shard_map/all_to_all | solution.py:490
  61.7 1.9 %shard_map.71 = (f32[3,8,64,128]{3,2,1,0:T(8,128)}, f32[8,64,128]{2,1,0:T(8,128)}) custom-call(f32[256,1,128]{2,1,0:T(1,128)S(1)} %all_to_all.10.sums, f32[10,160,128]{2,1,0:T(8,128)S(1)} %get-tuple-element.26.p0, f32[10,160,128]{2,1,0:T(8,128)S(1)} %get-tuple-element.27.p1, f32[10,160,128]{2,1,0:T(8,128)S(1)} %get-tuple-element.28.p2, ...), custom_call_target="tpu_custom_call" | custom-call | tf_op jit(solution)/shard_map/pallas_call | solution.py:426
Async XLA Ops:
  2.2 7.5 %collective-permute-start = (f32[96,128]{1,0:T(8,128)S(1)}, f32[96,128]{1,0:T(8,128)S(1)}, u32[]{:S(2)}, u32[]{:S(2)}) collective-permute-start(f32[96,128]{1,0:T(8,128)S(1)} %get-tuple-element.18), channel_id=1, source_target_pairs={{0,1},{1,2},{2,3},{3,4},{4,5},{5,6},{6,7},{7,0},{8,9},{9,10},{10,1... | collective-permute-start | bytes 147464 | tf_op jit(solution)/shard_map/ppermute | solution.py:443
  6.1 4.4 %collective-permute-start.1 = (f32[96,128]{1,0:T(8,128)S(1)}, f32[96,128]{1,0:T(8,128)S(1)}, u32[]{:S(2)}, u32[]{:S(2)}) collective-permute-start(f32[96,128]{1,0:T(8,128)S(1)} %get-tuple-element.19.sent), channel_id=1, source_target_pairs={{1,0},{2,1},{3,2},{4,3},{5,4},{6,5},{7,6},{0,7},{9,8},{10,9},{11,1... | collective-permute-start | bytes 147464 | tf_op jit(solution)/shard_map/ppermute | solution.py:443
  11.3 24.2 %collective-permute-start.2 = (f32[18,64,128]{2,1,0:T(8,128)S(1)}, f32[18,64,128]{2,1,0:T(8,128)S(1)}, u32[]{:S(2)}, u32[]{:S(2)}) collective-permute-start(f32[18,64,128]{2,1,0:T(8,128)S(1)} %get-tuple-element.23), channel_id=1, source_target_pairs={{0,8},{8,16},{16,24},{24,32},{32,40},{40,48},{48,56},{56,64},{64,7... | collective-permute-start | bytes 1769480 | tf_op jit(solution)/shard_map/ppermute | solution.py:443
  14.1 21.4 %collective-permute-start.3 = (f32[18,64,128]{2,1,0:T(8,128)S(1)}, f32[18,64,128]{2,1,0:T(8,128)S(1)}, u32[]{:S(2)}, u32[]{:S(2)}) collective-permute-start(f32[18,64,128]{2,1,0:T(8,128)S(1)} %get-tuple-element.22.mine), channel_id=1, source_target_pairs={{8,0},{16,8},{24,16},{32,24},{40,32},{48,40},{56,48},{64,56},{72,6... | collective-permute-start | bytes 1769480 | tf_op jit(solution)/shard_map/ppermute | solution.py:443
  14.3 21.3 %all-to-all-start = ((f32[32,1,1152]{2,1,0:T(1,128)}), f32[32,1,1152]{2,1,0:T(1,128)S(1)}, u32[]{:S(2)}, u32[]{:S(2)}) async-start(f32[32,1,1152]{2,1,0:T(1,128)} %get-tuple-element.24), calls=%async_computation | async-start | bytes 294912 | tf_op jit(solution)/shard_map/all_to_all | solution.py:473

commit v5 on v4

--- a/solution.py
+++ b/solution.py
@@ -46,10 +46,10 @@
     damping,
     weight,
     rotor,
-    to_left,
-    to_right,
-    low,
-    high,
+    beside_near,
+    beside_far,
+    near,
+    far,
     own,
     vel,
     damp,
@@ -59,6 +59,8 @@
 ):
     cells, rows = damping.shape[0], damping.shape[1]
     pairs = cells // 2
+    even = lax.rem(lax.axis_index("azim"), 2) == 0
+    even_axial = lax.rem(lax.axis_index("radax"), 2) == 0
     copies = [pltpu.make_async_copy(velocity.at[k], vel.at[k], sems.at[k]) for k in range(3)]
     copies += [pltpu.make_async_copy(damping, damp, sems.at[3])]
     copies += [pltpu.make_async_copy(weight, wt, sems.at[4])]
@@ -72,12 +74,13 @@
         for i in range(pairs):
             base = STRIP * i + start
             own[number, i] = paired(field[i], field[cells - 1 - i])
-            to_left[base : base + reach] = own[number, i, 0:reach]
-            to_right[base : base + reach] = own[number, i, LANES - reach : LANES]
+            first, final = own[number, i, 0:reach], own[number, i, LANES - reach : LANES]
+            beside_near[base : base + reach] = jnp.where(even_axial, final, first)
+            beside_far[base : base + reach] = jnp.where(even_axial, first, final)
         depth, start = DEPTHS[number], STARTS[number]
-        low[start : start + depth] = field[0:depth]
-        high[start : start + depth] = field[cells - depth : cells]
-    for message in (to_left, to_right):
+        near[start : start + depth] = field[pl.ds(jnp.where(even, cells - depth, 0), depth)]
+        far[start : start + depth] = field[pl.ds(jnp.where(even, 0, cells - depth), depth)]
+    for message in (beside_near, beside_far):
         for i in range(pairs):
             row = STRIP * i + STRIP - 1
             message[row : row + 1] = jnp.zeros((1, LANES), jnp.float32)
@@ -86,18 +89,24 @@
     base = STRIP * pairs
     for tap in range(3):
         rows = slice(tap * cells, (tap + 1) * cells)
-        low[PLANES, rows] = wt[tap]
-        high[PLANES, rows] = wt[tap]
+        near[PLANES, rows] = wt[tap]
+        far[PLANES, rows] = wt[tap]
         rows = slice(base + tap * cells, base + (tap + 1) * cells)
-        to_left[rows] = wt[tap]
-        to_right[rows] = wt[tap]
+        beside_near[rows] = wt[tap]
+        beside_far[rows] = wt[tap]
     rows = slice(base + 3 * cells, base + 4 * cells)
-    to_left[rows] = rt[...]
-    to_right[rows] = rt[...]
-
-
-def corner_kernel(before, after, sent, low_in, high_in, low, high, spread, ready, sem):
-    rows, cells = low.shape[1], ready.shape[2] // LANES - 1
+    beside_near[rows] = rt[...]
+    beside_far[rows] = rt[...]
+
+
+def corner_kernel(
+    from_near, from_far, sent, near_in, far_in, near, far, spread, both, ready, sem
+):
+    odd = lax.rem(lax.axis_index("radax"), 2)
+    both[1 - odd] = from_near[...]
+    both[odd] = from_far[...]
+    before, after = both.at[0], both.at[1]
+    rows, cells = near.shape[1], ready.shape[2] // LANES - 1
     strips = before.shape[0] - 4 * cells
     lines = strips + 3 * cells
     left = iota((3 * cells, LANES), 1) < HALF
@@ -114,7 +123,7 @@
         ready[k, :, LANES * cells :] = packed
     copy = pltpu.make_async_copy(ready, spread, sem.at[0])
     copy.start()
-    for message, base in ((low, low_in), (high, high_in)):
+    for message, base in ((near, near_in), (far, far_in)):
         message[0:PLANES] = base[0:PLANES]
         message[PLANES, 0 : 3 * cells] = base[PLANES, 0 : 3 * cells]
         message[PLANES, 3 * cells : 6 * cells] = rims
@@ -128,8 +137,8 @@
     offset,
     own,
     mine,
-    lower,
-    upper,
+    near,
+    far,
     turned,
     p0,
     p1,
@@ -148,7 +157,12 @@
     mirror,
     line,
     face,
+    halves,
 ):
+    odd = lax.rem(lax.axis_index("azim"), 2)
+    halves[1 - odd] = near[...]
+    halves[odd] = far[...]
+    lower, upper = halves.at[0], halves.at[1]
     pairs = own.shape[1]
     cells = 2 * pairs
     last = HALO + pairs - 1
@@ -436,11 +450,11 @@
     )(*operands)
 
 
-def swap(low, high, axis):
+def trade(near, far, axis):
     count = lax.axis_size(axis)
-    up = [(i, (i + 1) % count) for i in range(count)]
-    down = [(j, i) for i, j in up]
-    return lax.ppermute(high, axis, up), lax.ppermute(low, axis, down)
+    first = [(i, i ^ 1) for i in range(count)]
+    second = [(i, (i + 2 * (i % 2) - 1) % count) for i in range(count)]
+    return lax.ppermute(near, axis, first), lax.ppermute(far, axis, second)
 
 
 def per_device(velocity, rotor_flux, correlation_weight, damping, offset):
@@ -452,7 +466,7 @@
     pairs = cells // 2
     strips = (STRIP * pairs + 4 * cells, LANES)
     message = (PLANES + 3,) + plane
-    to_left, to_right, low, high, own = call(
+    beside_near, beside_far, near, far, own = call(
         edge_kernel,
         [strips, strips, message, message, (4, pairs) + block],
         (velocity, damping, correlation_weight, rotor_flux),
@@ -460,22 +474,22 @@
         spaces=[pltpu.HBM] * 4,
         sems=6,
     )
-    before, after = swap(to_left, to_right, "radax")
-    low, high, spread = call(
+    from_near, from_far = trade(beside_near, beside_far, "radax")
+    near, far, spread = call(
         corner_kernel,
         [message, message, (azim, 1, LANES * (cells + 1))],
-        (before, after, to_left, low, high),
-        scratch=[(azim, 1, LANES * (cells + 1))],
+        (from_near, from_far, beside_near, near, far),
+        scratch=[(2,) + strips, (azim, 1, LANES * (cells + 1))],
         outs=[pltpu.VMEM, pltpu.VMEM, pltpu.HBM],
         sems=1,
     )
-    lower, upper = swap(low, high, "azim")
+    from_near, from_far = trade(near, far, "azim")
     turned = lax.all_to_all(spread, "azim", 0, 0, tiled=True)
     field = (HALO + pairs + 1, TALL, LANES)
     *fields, sums = call(
         basis_kernel,
         [field] * 6 + [(devices, 1, LANES)],
-        (offset, own, low, lower, upper, turned),
+        (offset, own, near, from_near, from_far, turned),
         scratch=[field] * 4
         + [
             (2, HALO + pairs, STRIP, LANES),
@@ -484,6 +498,7 @@
             block,
             (TALL, LANES),
             field,
+            (2,) + message,
         ],
         spaces=[pltpu.SMEM] + [pltpu.VMEM] * 5,
     )

time: 63.8 us -> 61.7 us (0.967)
  blocking collectives: 23.2 us -> 20.3 us
  waiting for transfers between devices: 11 us -> 13.7 us
  starting transfers between devices: 20.8 us -> 18.5 us
    all_to_all x1, starting transfers between devices: 11.7 us -> 6.67 us  [per_device(): turned = lax.all_to_all(spread, 'azim', 0, 0, tiled=True)]
    all_to_all x1, blocking collectives: 23.2 us -> 20.3 us  [per_device(): sums = lax.all_to_all(sums, ('azim', 'radax'), 0, 0, tiled=True)]
    ppermute x4, starting transfers between devices: 9.03 us -> 11.8 us  [trade(): return (lax.ppermute(near, axis, first), lax.ppermute(far, axis, second))]
    ppermute x4, waiting for transfers between devices: 2.16 us -> 4.84 us  [trade(): return (lax.ppermute(near, axis, first), lax.ppermute(far, axis, second))]
where the time goes in v5:
time: 61.7 us; the launch traced here: 61.5 us
  blocking collectives  20.3 us (33%)
  starting transfers between devices  18.5 us (30%)
  waiting for transfers between devices  13.7 us (22%)
  Pallas kernels  7.62 us (12%)
  between operations  1.31 us (2%)
    all_to_all x1, blocking collectives, per_device(): sums = lax.all_to_all(sums, ('azim', 'radax'), 0, 0, tiled=True)  20.3 us
    ppermute x4, starting transfers between devices, trade(): return (lax.ppermute(near, axis, first), lax.ppermute(far, axis, second))  11.8 us
    all_to_all x1, waiting for transfers between devices, per_device(): turned = lax.all_to_all(spread, 'azim', 0, 0, tiled=True)  8.87 us
    pallas_call x4, Pallas kernels, call(): pl.pallas_call(kernel, out_shape=[space(s, jnp.float32) if space is pltpu...  7.62 us
    all_to_all x1, starting transfers between devices, per_device(): turned = lax.all_to_all(spread, 'azim', 0, 0, tiled=True)  6.67 us
    ppermute x4, waiting for transfers between devices, trade(): return (lax.ppermute(near, axis, first), lax.ppermute(far, axis, second))  4.84 us
  transfers between devices with their start and end apart: 5, of which 3 were waited for; matrix products, arithmetic and copies ran while one was open for 0% of the time, Pallas kernels for 0%

profile of v5, /device:TPU:1, one launch (start us, length us, event | category | flops | bytes accessed | tf_op | source)
XLA Modules:
  0.0 61.5 jit_solution(17275655072418399379)
XLA Ops:
  0.6 1.7 %shard_map.68 = (f32[96,128]{1,0:T(8,128)S(1)}, f32[96,128]{1,0:T(8,128)S(1)}, f32[18,64,128]{2,1,0:T(8,128)S(1)}, f32[18,64,128]{2,1,0:T(8,128)S(1)}, f32[4,4,128,128]{3,2,1,0:T(8,128)S(1)}) custom-call(f32[3,8,64,128]{3,2,1,0:T(8,128)} %velocity.1, f32[8,64,128]{2,1,0:T(8,128)} %damping.1, f32[3,8,128]{2,1,0:T(8,128)} %weight.1, f32[8,128]{1,0:T(8,128)} %rotor.1), custom_call_target="tpu_custom_call" | custom-call | tf_op jit(solution)/shard_map/pallas_call | solution.py:440
  2.3 6.0 %collective-permute-start.1 = (f32[96,128]{1,0:T(8,128)S(1)}, f32[96,128]{1,0:T(8,128)S(1)}, u32[]{:S(2)}, u32[]{:S(2)}) collective-permute-start(f32[96,128]{1,0:T(8,128)S(1)} %get-tuple-element.19), channel_id=1, source_target_pairs={{0,7},{1,2},{2,1},{3,4},{4,3},{5,6},{6,5},{7,0},{8,15},{9,10},{10,... | collective-permute-start | bytes 147464 | tf_op jit(solution)/shard_map/ppermute | solution.py:457
  8.3 0.0 collective-permute-start
  8.3 1.5 %collective-permute-done.1.from_far = f32[96,128]{1,0:T(8,128)S(1)} collective-permute-done((f32[96,128]{1,0:T(8,128)S(1)}, f32[96,128]{1,0:T(8,128)S(1)}, u32[]{:S(2)}, u32[]{:S(2)}) %collective-permute-start.1) | collective-permute-done | bytes 49184 | tf_op jit(solution)/shard_map/ppermute | solution.py:457
  9.8 3.4 %collective-permute-done.from_near = f32[96,128]{1,0:T(8,128)S(1)} collective-permute-done((f32[96,128]{1,0:T(8,128)S(1)}, f32[96,128]{1,0:T(8,128)S(1)}, u32[]{:S(2)}, u32[]{:S(2)}) %collective-permute-start) | collective-permute-done | bytes 49184 | tf_op jit(solution)/shard_map/ppermute | solution.py:457
  13.2 0.8 %shard_map.69 = (f32[18,64,128]{2,1,0:T(8,128)S(1)}, f32[18,64,128]{2,1,0:T(8,128)S(1)}, f32[32,1,1152]{2,1,0:T(1,128)}) custom-call(f32[96,128]{1,0:T(8,128)S(1)} %collective-permute-done.from_near, f32[96,128]{1,0:T(8,128)S(1)} %collective-permute-done.1.from_far, f32[96,128]{1,0:T(8,128)S(1)} %get-tuple-element.18.sent, ...), custom_call_target="tpu_custom_call" | custom-call | tf_op jit(solution)/shard_map/pallas_call | solution.py:440
  14.0 2.1 %collective-permute-start.3 = (f32[18,64,128]{2,1,0:T(8,128)S(1)}, f32[18,64,128]{2,1,0:T(8,128)S(1)}, u32[]{:S(2)}, u32[]{:S(2)}) collective-permute-start(f32[18,64,128]{2,1,0:T(8,128)S(1)} %get-tuple-element.23), channel_id=1, source_target_pairs={{0,248},{8,16},{16,8},{24,32},{32,24},{40,48},{48,40},{56,64},{64,... | collective-permute-start | bytes 1769480 | tf_op jit(solution)/shard_map/ppermute | solution.py:457
  16.1 3.7 %collective-permute-start.2 = (f32[18,64,128]{2,1,0:T(8,128)S(1)}, f32[18,64,128]{2,1,0:T(8,128)S(1)}, u32[]{:S(2)}, u32[]{:S(2)}) collective-permute-start(f32[18,64,128]{2,1,0:T(8,128)S(1)} %get-tuple-element.22.mine), channel_id=1, source_target_pairs={{0,8},{8,0},{16,24},{24,16},{32,40},{40,32},{48,56},{56,48},{64,72... | collective-permute-start | bytes 1769480 | tf_op jit(solution)/shard_map/ppermute | solution.py:457
  19.8 6.7 %all-to-all-start = ((f32[32,1,1152]{2,1,0:T(1,128)}), f32[32,1,1152]{2,1,0:T(1,128)S(1)}, u32[]{:S(2)}, u32[]{:S(2)}) async-start(f32[32,1,1152]{2,1,0:T(1,128)} %get-tuple-element.24), calls=%async_computation | async-start | bytes 294912 | tf_op jit(solution)/shard_map/all_to_all | solution.py:487
  27.1 8.9 %all-to-all-done.turned = f32[32,1,1152]{2,1,0:T(1,128)S(1)} async-done(((f32[32,1,1152]{2,1,0:T(1,128)}), f32[32,1,1152]{2,1,0:T(1,128)S(1)}, u32[]{:S(2)}, u32[]{:S(2)}) %all-to-all-start) | async-done | bytes 147488 | tf_op jit(solution)/shard_map/all_to_all | solution.py:487
  36.0 0.0 collective-permute-done.3.far
  36.0 0.0 collective-permute-done.2.near
  36.0 3.2 %shard_map.70 = (f32[10,160,128]{2,1,0:T(8,128)S(1)}, f32[10,160,128]{2,1,0:T(8,128)S(1)}, f32[10,160,128]{2,1,0:T(8,128)S(1)}, f32[10,160,128]{2,1,0:T(8,128)S(...) custom-call(s32[1]{0:T(128)S(6)} %copy.7.offset, ...), custom_call_target="tpu_custom_call" | custom-call | tf_op jit(solution)/shard_map/pallas_call | solution.py:440
  39.2 20.3 %all_to_all.10.sums = f32[256,1,128]{2,1,0:T(1,128)S(1)} all-to-all(f32[256,1,128]{2,1,0:T(1,128)S(1)} %get-tuple-element.25), channel_id=1, replica_groups=mesh['azim'=32,'radax'=8] {'azim','radax'}, dimensions={0} | all-to-all | bytes 262144 | tf_op jit(solution)/shard_map/all_to_all | solution.py:505
  59.6 1.9 %shard_map.71 = (f32[3,8,64,128]{3,2,1,0:T(8,128)}, f32[8,64,128]{2,1,0:T(8,128)}) custom-call(f32[256,1,128]{2,1,0:T(1,128)S(1)} %all_to_all.10.sums, f32[10,160,128]{2,1,0:T(8,128)S(1)} %get-tuple-element.26.p0, f32[10,160,128]{2,1,0:T(8,128)S(1)} %get-tuple-element.27.p1, f32[10,160,128]{2,1,0:T(8,128)S(1)} %get-tuple-element.28.p2, ...), custom_call_target="tpu_custom_call" | custom-call | tf_op jit(solution)/shard_map/pallas_call | solution.py:440
Async XLA Ops:
  2.3 7.5 %collective-permute-start.1 = (f32[96,128]{1,0:T(8,128)S(1)}, f32[96,128]{1,0:T(8,128)S(1)}, u32[]{:S(2)}, u32[]{:S(2)}) collective-permute-start(f32[96,128]{1,0:T(8,128)S(1)} %get-tuple-element.19), channel_id=1, source_target_pairs={{0,7},{1,2},{2,1},{3,4},{4,3},{5,6},{6,5},{7,0},{8,15},{9,10},{10,... | collective-permute-start | bytes 147464 | tf_op jit(solution)/shard_map/ppermute | solution.py:457
  8.3 4.8 %collective-permute-start = (f32[96,128]{1,0:T(8,128)S(1)}, f32[96,128]{1,0:T(8,128)S(1)}, u32[]{:S(2)}, u32[]{:S(2)}) collective-permute-start(f32[96,128]{1,0:T(8,128)S(1)} %get-tuple-element.18.sent), channel_id=1, source_target_pairs={{0,1},{1,0},{2,3},{3,2},{4,5},{5,4},{6,7},{7,6},{8,9},{9,8},{10,11... | collective-permute-start | bytes 147464 | tf_op jit(solution)/shard_map/ppermute | solution.py:457
  14.0 22.0 %collective-permute-start.3 = (f32[18,64,128]{2,1,0:T(8,128)S(1)}, f32[18,64,128]{2,1,0:T(8,128)S(1)}, u32[]{:S(2)}, u32[]{:S(2)}) collective-permute-start(f32[18,64,128]{2,1,0:T(8,128)S(1)} %get-tuple-element.23), channel_id=1, source_target_pairs={{0,248},{8,16},{16,8},{24,32},{32,24},{40,48},{48,40},{56,64},{64,... | collective-permute-start | bytes 1769480 | tf_op jit(solution)/shard_map/ppermute | solution.py:457
  16.1 19.9 %collective-permute-start.2 = (f32[18,64,128]{2,1,0:T(8,128)S(1)}, f32[18,64,128]{2,1,0:T(8,128)S(1)}, u32[]{:S(2)}, u32[]{:S(2)}) collective-permute-start(f32[18,64,128]{2,1,0:T(8,128)S(1)} %get-tuple-element.22.mine), channel_id=1, source_target_pairs={{0,8},{8,0},{16,24},{24,16},{32,40},{40,32},{48,56},{56,48},{64,72... | collective-permute-start | bytes 1769480 | tf_op jit(solution)/shard_map/ppermute | solution.py:457
  19.8 16.2 %all-to-all-start = ((f32[32,1,1152]{2,1,0:T(1,128)}), f32[32,1,1152]{2,1,0:T(1,128)S(1)}, u32[]{:S(2)}, u32[]{:S(2)}) async-start(f32[32,1,1152]{2,1,0:T(1,128)} %get-tuple-element.24), calls=%async_computation | async-start | bytes 294912 | tf_op jit(solution)/shard_map/all_to_all | solution.py:487

commit v6 on v4

--- a/solution.py
+++ b/solution.py
@@ -18,10 +18,21 @@
 STARTS = (0, 5, 9, 13)
 PLANES = 15
 REACH = (4, 4, 5, 2)
-FROM = (0, 4, 8, 13)
+LAG = (0, 1, 0, 3)
 STRIP = 16
-RIM = 16
+RIM = 8
 BODY = slice(FRONT, FRONT + LANES)
+
+
+def strips(pairs):
+    table, row = {}, 0
+    for i in range(HALO + pairs):
+        for number in range(4):
+            reach = max(min(i - LAG[number], REACH[number]), 0)
+            if reach:
+                table[number, i] = (row, reach)
+            row += reach
+    return table, row + -row % 8
 
 
 def iota(shape, dim):
@@ -41,96 +52,110 @@
     return jnp.concatenate([first, second], axis=0).T
 
 
-def edge_kernel(
+def plane_kernel(
+    velocity, damping, weight, rotor, near, far, spread, vel, damp, lines, ready, sems
+):
+    cells, rows = damping.shape[0], damping.shape[1]
+    even = lax.rem(lax.axis_index("azim"), 2) == 0
+    first = pltpu.make_async_copy(rotor, lines, sems.at[0])
+    first.start()
+    copies = []
+
+    def copy(source, target):
+        copies.append(pltpu.make_async_copy(source, target, sems.at[1 + len(copies)]))
+        copies[-1].start()
+
+    fields = [velocity.at[0], velocity.at[1], velocity.at[2], damping]
+    for field, depth, start in zip(fields, DEPTHS, STARTS):
+        target = slice(start, start + depth)
+        copy(field.at[pl.ds(jnp.where(even, cells - depth, 0), depth)], near.at[target])
+        copy(field.at[pl.ds(jnp.where(even, 0, cells - depth), depth)], far.at[target])
+    for tap in range(3):
+        target = slice(tap * cells, (tap + 1) * cells)
+        copy(weight.at[tap], near.at[PLANES, target])
+        copy(weight.at[tap], far.at[PLANES, target])
+    copy(velocity, vel)
+    copy(damping, damp)
+    for message in (near, far):
+        message[PLANES, 3 * cells : rows] = jnp.zeros((rows - 3 * cells, LANES), jnp.float32)
+    first.wait()
+    ready[...] = jnp.broadcast_to(lines[...][None], ready.shape)
+    copy(ready, spread)
+    for each in copies:
+        each.wait()
+
+
+def gather_kernel(
+    offset,
     velocity,
     damping,
-    weight,
-    rotor,
-    to_left,
-    to_right,
-    low,
-    high,
-    own,
-    vel,
-    damp,
-    wt,
-    rt,
-    sems,
+    mine,
+    near,
+    far,
+    turned,
+    beside_near,
+    beside_far,
+    blocks,
+    taps,
+    rot,
+    halves,
 ):
-    cells, rows = damping.shape[0], damping.shape[1]
+    cells = damping.shape[0]
     pairs = cells // 2
-    copies = [pltpu.make_async_copy(velocity.at[k], vel.at[k], sems.at[k]) for k in range(3)]
-    copies += [pltpu.make_async_copy(damping, damp, sems.at[3])]
-    copies += [pltpu.make_async_copy(weight, wt, sems.at[4])]
-    copies += [pltpu.make_async_copy(rotor, rt, sems.at[5])]
-    for copy in copies:
-        copy.start()
-    fields = [vel.at[0], vel.at[1], vel.at[2], damp]
+    odd = lax.rem(lax.axis_index("azim"), 2)
+    even_axial = lax.rem(lax.axis_index("radax"), 2) == 0
+    halves[1 - odd] = near[...]
+    halves[odd] = far[...]
+    lower, upper = halves.at[0], halves.at[1]
+
+    total = turned.shape[0] * cells
+    begin = lax.axis_index("azim") * cells - offset[0] - 4 + 2 * total
+    for k in range(cells + 8):
+        source = lax.rem(begin + k, total)
+        rot[k : k + 1] = turned[source // cells, pl.ds(lax.rem(source, cells), 1)]
+    wide = cells + 6
+    for tap in range(3):
+        k = tap * cells
+        taps[tap, 0:3] = lower[PLANES, k + cells - 3 : k + cells]
+        taps[tap, 3 : 3 + cells] = mine[PLANES, k : k + cells]
+        taps[tap, 3 + cells : wide] = upper[PLANES, k : k + 3]
+        taps[tap, wide : wide + 2] = jnp.zeros((2, LANES), jnp.float32)
+
+    table, count = strips(pairs)
+    group = iota((STRIP, LANES), 1) // RIM
+    firsts = finals = jnp.zeros((STRIP, LANES), jnp.float32)
+    for k, tile in enumerate((taps[0], taps[1], taps[2], rot[...])):
+        firsts = jnp.where(group == k, spin(tile, RIM * k), firsts)
+        finals = jnp.where(group == k, spin(tile, RIM * k + RIM), finals)
+    beside_near[count:] = jnp.where(even_axial, finals, firsts)
+    beside_far[count:] = jnp.where(even_axial, firsts, finals)
+    beside_near[count - 8 : count] = jnp.zeros((8, LANES), jnp.float32)
+    beside_far[count - 8 : count] = jnp.zeros((8, LANES), jnp.float32)
+
+    fields = [velocity.at[0], velocity.at[1], velocity.at[2], damping]
     for number, field in enumerate(fields):
-        copies[number].wait()
-        reach, start = REACH[number], FROM[number]
-        for i in range(pairs):
-            base = STRIP * i + start
-            own[number, i] = paired(field[i], field[cells - 1 - i])
-            to_left[base : base + reach] = own[number, i, 0:reach]
-            to_right[base : base + reach] = own[number, i, LANES - reach : LANES]
         depth, start = DEPTHS[number], STARTS[number]
-        low[start : start + depth] = field[0:depth]
-        high[start : start + depth] = field[cells - depth : cells]
-    for message in (to_left, to_right):
-        for i in range(pairs):
-            row = STRIP * i + STRIP - 1
-            message[row : row + 1] = jnp.zeros((1, LANES), jnp.float32)
-    for copy in copies[4:]:
-        copy.wait()
-    base = STRIP * pairs
-    for tap in range(3):
-        rows = slice(tap * cells, (tap + 1) * cells)
-        low[PLANES, rows] = wt[tap]
-        high[PLANES, rows] = wt[tap]
-        rows = slice(base + tap * cells, base + (tap + 1) * cells)
-        to_left[rows] = wt[tap]
-        to_right[rows] = wt[tap]
-    rows = slice(base + 3 * cells, base + 4 * cells)
-    to_left[rows] = rt[...]
-    to_right[rows] = rt[...]
-
-
-def corner_kernel(before, after, sent, low_in, high_in, low, high, spread, ready, sem):
-    rows, cells = low.shape[1], ready.shape[2] // LANES - 1
-    strips = before.shape[0] - 4 * cells
-    lines = strips + 3 * cells
-    left = iota((3 * cells, LANES), 1) < HALF
-    rims = jnp.where(left, after[strips:lines], before[strips:lines])
-    own = sent[lines : lines + cells]
-    rim = jnp.where(left[0:cells], after[lines : lines + cells], before[lines : lines + cells])
-    group = iota((1, LANES), 1) // RIM
-    packed = jnp.zeros((1, LANES), jnp.float32)
-    for r in range(cells):
-        packed = jnp.where(group == r, spin(rim[r : r + 1], RIM // 2 + RIM * r), packed)
-    for k in range(ready.shape[0]):
-        for r in range(cells):
-            ready[k, :, LANES * r : LANES * r + LANES] = own[r : r + 1]
-        ready[k, :, LANES * cells :] = packed
-    copy = pltpu.make_async_copy(ready, spread, sem.at[0])
-    copy.start()
-    for message, base in ((low, low_in), (high, high_in)):
-        message[0:PLANES] = base[0:PLANES]
-        message[PLANES, 0 : 3 * cells] = base[PLANES, 0 : 3 * cells]
-        message[PLANES, 3 * cells : 6 * cells] = rims
-        message[PLANES, 6 * cells : rows] = jnp.zeros((rows - 6 * cells, LANES), jnp.float32)
-        message[PLANES + 1] = before[0:strips]
-        message[PLANES + 2] = after[0:strips]
-    copy.wait()
+        for i in range(HALO - depth, HALO + pairs):
+            if i < HALO:
+                block = paired(lower[start + i - HALO + depth], upper[start + HALO - 1 - i])
+            else:
+                block = paired(field[i - HALO], field[cells - 1 - i + HALO])
+            blocks[number, i] = block
+            if (number, i) not in table:
+                continue
+            row, reach = table[number, i]
+            rows = slice(row, row + reach)
+            first, final = blocks[number, i, 0:reach], blocks[number, i, LANES - reach : LANES]
+            beside_near[rows] = jnp.where(even_axial, final, first)
+            beside_far[rows] = jnp.where(even_axial, first, final)
 
 
 def basis_kernel(
-    offset,
-    own,
-    mine,
-    lower,
-    upper,
-    turned,
+    blocks,
+    taps,
+    rot,
+    far,
+    near,
     p0,
     p1,
     p2,
@@ -142,17 +167,19 @@
     v1,
     v2,
     diag,
-    strip,
-    taps,
-    rot,
+    rims,
     mirror,
     line,
     face,
+    both,
 ):
-    pairs = own.shape[1]
+    odd = lax.rem(lax.axis_index("radax"), 2)
+    both[1 - odd] = near[...]
+    both[odd] = far[...]
+    before, after = both.at[0], both.at[1]
+    pairs = blocks.shape[1] - HALO
     cells = 2 * pairs
     last = HALO + pairs - 1
-    total = turned.shape[0] * cells
     every = range(TILES + 2)
     place = lax.axis_index("radax")
     has_before, has_after = place > 0, place < lax.axis_size("radax") - 1
@@ -173,63 +200,36 @@
         for t in every:
             field[last + 1, at(t)] = spin(field[last, at(t)], HALF)
 
+    table, count = strips(pairs)
     shift = 6.0 - CENTER
     for number, field in enumerate((v0, v1, v2, diag)):
-        extra = shift if number == 3 else 0.0
-        depth, start = DEPTHS[number], STARTS[number]
-        for i in range(HALO - depth, HALO):
-            block = paired(lower[start + i - HALO + depth], upper[start + HALO - 1 - i])
-            field[i, BODY] = block + extra if number == 3 else block
-
-        def fill(i, carry):
-            block = own[number, i]
-            field[HALO + i, BODY] = block + extra if number == 3 else block
-            return carry
-
-        lax.fori_loop(0, pairs, fill, 0, unroll=True)
-
-    left = iota((STRIP, LANES), 1) < HALF
-    for side in range(2):
-        for i in range(HALO + pairs):
-            pair = i - HALO if i >= HALO else min(HALO - 1 - i, pairs - 1)
-            rows = slice(STRIP * pair, STRIP * pair + STRIP)
-            under, over = lower[PLANES + 1 + side, rows], upper[PLANES + 1 + side, rows]
-            if i >= HALO:
-                strip[side, i] = mine[PLANES + 1 + side, rows]
-            elif i:
-                strip[side, i] = spin(jnp.where(left, over, under), HALF)
-            else:
-                strip[side, i] = jnp.where(left, under, over)
-    for number, field in enumerate((v0, v1, v2, diag)):
-        reach, start = REACH[number], FROM[number]
-        for i in range(HALO - DEPTHS[number], HALO + pairs):
-            for side, t in ((0, 0), (1, TILES + 1)):
-                value = walled(t, strip[side, i, start : start + reach])
+        for i in range(HALO - DEPTHS[number], last + 1):
+            block = blocks[number, i]
+            field[i, BODY] = block + shift if number == 3 else block
+            if (number, i) not in table:
+                continue
+            for message, t in ((before, 0), (after, TILES + 1)):
+                row, reach = table[number, i]
+                value = walled(t, message[row : row + reach])
                 value = value + shift if number == 3 else value
-                row = FRONT - reach if side == 0 else FRONT + LANES
+                row = FRONT - reach if t == 0 else FRONT + LANES
                 field[i, row : row + reach] = value
     for field in (v0, v1, v2):
         seam(field)
 
     wide = cells + 6
-    for part in range(2):
-        for tap in range(3):
-            k = (3 * part + tap) * cells
-            taps[part, tap, 0:3] = lower[PLANES, k + cells - 3 : k + cells]
-            taps[part, tap, 3 : 3 + cells] = mine[PLANES, k : k + cells]
-            taps[part, tap, 3 + cells : wide] = upper[PLANES, k : k + 3]
-    begin = lax.axis_index("azim") * cells - offset[0] - 4 + 2 * total
-    for k in range(wide + 2):
-        source = lax.rem(begin + k, total)
-        block = source // cells
-        row = lax.rem(source, cells)
-        rot[0, k : k + 1] = turned[block, :, pl.ds(pl.multiple_of(row * LANES, LANES), LANES)]
-        packed = turned[block, :, LANES * cells :]
-        rot[1, k : k + 1] = pltpu.roll(packed, 2 * LANES - RIM // 2 - RIM * row, 1)
+    left = iota((STRIP, LANES), 1) < HALF
+    for k in range(4):
+        rims[k] = jnp.where(
+            left, spin(after[count:], -RIM * k), spin(before[count:], -RIM - RIM * k)
+        )
     for part in range(2):
         flux = jnp.zeros((wide, LANES), jnp.float32)
         for tap in range(3):
-            flux += taps[part, tap, 0:wide] * rot[part, tap : tap + wide]
+            if part == 0:
+                flux += taps[tap, 0:wide] * rot[tap : tap + wide]
+            else:
+                flux += rims[tap, 0:wide] * rims[3, tap : tap + wide]
         mirror[2 : 2 + wide // 2] = flux[0 : wide // 2]
         for i in range(2, last + 1):
             mirror[HALF + i : HALF + i + 1] = flux[wide + 1 - i : wide + 2 - i]
@@ -436,11 +436,11 @@
     )(*operands)
 
 
-def swap(low, high, axis):
+def trade(near, far, axis):
     count = lax.axis_size(axis)
-    up = [(i, (i + 1) % count) for i in range(count)]
-    down = [(j, i) for i, j in up]
-    return lax.ppermute(high, axis, up), lax.ppermute(low, axis, down)
+    first = [(i, i ^ 1) for i in range(count)]
+    second = [(i, (i + 2 * (i % 2) - 1) % count) for i in range(count)]
+    return lax.ppermute(far, axis, second), lax.ppermute(near, axis, first)
 
 
 def per_device(velocity, rotor_flux, correlation_weight, damping, offset):
@@ -450,42 +450,34 @@
     plane = (rows, LANES)
     block = (LANES, LANES)
     pairs = cells // 2
-    strips = (STRIP * pairs + 4 * cells, LANES)
-    message = (PLANES + 3,) + plane
-    to_left, to_right, low, high, own = call(
-        edge_kernel,
-        [strips, strips, message, message, (4, pairs) + block],
+    message = (PLANES + 1,) + plane
+    near, far, spread, vel, damp = call(
+        plane_kernel,
+        [message, message, (azim, cells, LANES), velocity.shape, damping.shape],
         (velocity, damping, correlation_weight, rotor_flux),
-        scratch=[(3, cells) + plane, (cells,) + plane, (3, cells, LANES), (cells, LANES)],
+        scratch=[(cells, LANES), (azim, cells, LANES)],
         spaces=[pltpu.HBM] * 4,
-        sems=6,
+        outs=[pltpu.VMEM, pltpu.VMEM, pltpu.HBM, pltpu.VMEM, pltpu.VMEM],
+        sems=18,
     )
-    before, after = swap(to_left, to_right, "radax")
-    low, high, spread = call(
-        corner_kernel,
-        [message, message, (azim, 1, LANES * (cells + 1))],
-        (before, after, to_left, low, high),
-        scratch=[(azim, 1, LANES * (cells + 1))],
-        outs=[pltpu.VMEM, pltpu.VMEM, pltpu.HBM],
-        sems=1,
+    from_far, from_near = trade(near, far, "azim")
+    turned = lax.all_to_all(spread, "azim", 0, 0, tiled=True)
+    beside = (strips(pairs)[1] + STRIP, LANES)
+    beside_near, beside_far, blocks, taps, rot = call(
+        gather_kernel,
+        [beside, beside, (4, HALO + pairs) + block, (3, cells + 8, LANES), (cells + 8, LANES)],
+        (offset, vel, damp, near, from_near, from_far, turned),
+        scratch=[(2,) + message],
+        spaces=[pltpu.SMEM] + [pltpu.VMEM] * 6,
     )
-    lower, upper = swap(low, high, "azim")
-    turned = lax.all_to_all(spread, "azim", 0, 0, tiled=True)
+    beside_from_far, beside_from_near = trade(beside_near, beside_far, "radax")
     field = (HALO + pairs + 1, TALL, LANES)
     *fields, sums = call(
         basis_kernel,
         [field] * 6 + [(devices, 1, LANES)],
-        (offset, own, low, lower, upper, turned),
+        (blocks, taps, rot, beside_from_far, beside_from_near),
         scratch=[field] * 4
-        + [
-            (2, HALO + pairs, STRIP, LANES),
-            (2, 3, cells + 8, LANES),
-            (2, cells + 8, LANES),
-            block,
-            (TALL, LANES),
-            field,
-        ],
-        spaces=[pltpu.SMEM] + [pltpu.VMEM] * 5,
+        + [(4, STRIP, LANES), block, (TALL, LANES), field, (2,) + beside],
     )
     sums = lax.all_to_all(sums, ("azim", "radax"), 0, 0, tiled=True)
     return call(

time: 63.8 us -> 59.9 us (0.939)
  starting transfers between devices: 20.8 us -> 17.4 us
  blocking collectives: 23.2 us -> 20.6 us
  waiting for transfers between devices: 11 us -> 13.1 us
    all_to_all x1, starting transfers between devices: 11.7 us -> 4.34 us  [per_device(): turned = lax.all_to_all(spread, 'azim', 0, 0, tiled=True)]
    ppermute x4, starting transfers between devices: 9.03 us -> 13.1 us  [trade(): return (lax.ppermute(far, axis, second), lax.ppermute(near, axis, first))]
    all_to_all x1, blocking collectives: 23.2 us -> 20.6 us  [per_device(): sums = lax.all_to_all(sums, ('azim', 'radax'), 0, 0, tiled=True)]
    ppermute x4, waiting for transfers between devices: 2.16 us -> 4.49 us  [trade(): return (lax.ppermute(far, axis, second), lax.ppermute(near, axis, first))]
where the time goes in v6:
time: 59.9 us; the launch traced here: 59.7 us
  blocking collectives  20.6 us (34%)
  starting transfers between devices  17.4 us (29%)
  waiting for transfers between devices  13.1 us (22%)
  Pallas kernels  7.23 us (12%)
  between operations  1.31 us (2%)
    all_to_all x1, blocking collectives, per_device(): sums = lax.all_to_all(sums, ('azim', 'radax'), 0, 0, tiled=True)  20.6 us
    ppermute x4, starting transfers between devices, trade(): return (lax.ppermute(far, axis, second), lax.ppermute(near, axis, first))  13.1 us
    all_to_all x1, waiting for transfers between devices, per_device(): turned = lax.all_to_all(spread, 'azim', 0, 0, tiled=True)  8.61 us
    pallas_call x4, Pallas kernels, call(): pl.pallas_call(kernel, out_shape=[space(s, jnp.float32) if space is pltpu...  7.23 us
    ppermute x4, waiting for transfers between devices, trade(): return (lax.ppermute(far, axis, second), lax.ppermute(near, axis, first))  4.49 us
    all_to_all x1, starting transfers between devices, per_device(): turned = lax.all_to_all(spread, 'azim', 0, 0, tiled=True)  4.34 us
  transfers between devices with their start and end apart: 5, of which 3 were waited for; matrix products, arithmetic and copies ran while one was open for 0% of the time, Pallas kernels for 0%

profile of v6, /device:TPU:1, one launch (start us, length us, event | category | flops | bytes accessed | tf_op | source)
XLA Modules:
  0.0 59.7 jit_solution(4497792006560673615)
XLA Ops:
  0.6 1.8 %shard_map.68 = (f32[16,64,128]{2,1,0:T(8,128)S(1)}, f32[16,64,128]{2,1,0:T(8,128)S(1)}, f32[32,8,128]{2,1,0:T(8,128)}, f32[3,8,64,128]{3,2,1,0:T(8,128)S(1)}, f32[8,64,128]{2,1,0:T(8,128)S(1)}) custom-call(f32[3,8,64,128]{3,2,1,0:T(8,128)} %velocity.1, f32[8,64,128]{2,1,0:T(8,128)} %damping.1, f32[3,8,128]{2,1,0:T(8,128)} %weight.1, f32[8,128]{1,0:T(8,128)} %rotor.1), custom_call_target="tpu_custom_call" | custom-call | tf_op jit(solution)/shard_map/pallas_call | solution.py:426
  2.5 2.8 %collective-permute-start.1 = (f32[16,64,128]{2,1,0:T(8,128)S(1)}, f32[16,64,128]{2,1,0:T(8,128)S(1)}, u32[]{:S(2)}, u32[]{:S(2)}) collective-permute-start(f32[16,64,128]{2,1,0:T(8,128)S(1)} %get-tuple-element.22), channel_id=1, source_target_pairs={{0,248},{8,16},{16,8},{24,32},{32,24},{40,48},{48,40},{56,64},{64,... | collective-permute-start | bytes 1572872 | tf_op jit(solution)/shard_map/ppermute | solution.py:443
  5.3 5.1 %collective-permute-start = (f32[16,64,128]{2,1,0:T(8,128)S(1)}, f32[16,64,128]{2,1,0:T(8,128)S(1)}, u32[]{:S(2)}, u32[]{:S(2)}) collective-permute-start(f32[16,64,128]{2,1,0:T(8,128)S(1)} %get-tuple-element.21.mine), channel_id=1, source_target_pairs={{0,8},{8,0},{16,24},{24,16},{32,40},{40,32},{48,56},{56,48},{64,72... | collective-permute-start | bytes 1572872 | tf_op jit(solution)/shard_map/ppermute | solution.py:443
  10.4 4.3 %all-to-all-start = ((f32[32,8,128]{2,1,0:T(8,128)}), f32[32,8,128]{2,1,0:T(8,128)S(1)}, u32[]{:S(2)}, u32[]{:S(2)}) async-start(f32[32,8,128]{2,1,0:T(8,128)} %get-tuple-element.23), calls=%async_computation | async-start | bytes 262144 | tf_op jit(solution)/shard_map/all_to_all | solution.py:464
  15.4 8.6 %all-to-all-done.turned = f32[32,8,128]{2,1,0:T(8,128)S(1)} async-done(((f32[32,8,128]{2,1,0:T(8,128)}), f32[32,8,128]{2,1,0:T(8,128)S(1)}, u32[]{:S(2)}, u32[]{:S(2)}) %all-to-all-start) | async-done | bytes 131104 | tf_op jit(solution)/shard_map/all_to_all | solution.py:464
  24.0 0.0 collective-permute-done.1.far
  24.0 0.0 collective-permute-done.near
  24.0 0.8 %shard_map.69 = (f32[104,128]{1,0:T(8,128)S(1)}, f32[104,128]{1,0:T(8,128)S(1)}, f32[4,9,128,128]{3,2,1,0:T(8,128)S(1)}, f32[3,16,128]{2,1,0:T(8,128)S(1)}, f32[16,128]{1,0:T(8,128)S(1)}) custom-call(s32[1]{0:T(128)S(6)} %copy.7.offset, f32[3,8,64,128]{3,2,1,0:T(8,128)S(1)} %get-tuple-element.19.velocity, f32[8,64,128]{2,1,0:T(8,128)S(1)} %get-tuple-element.20.damping, ...), custom_call_target="tpu_custom_call" | custom-call | tf_op jit(solution)/shard_map/pallas_call | solution.py:426
  24.8 5.2 %collective-permute-start.2 = (f32[104,128]{1,0:T(8,128)S(1)}, f32[104,128]{1,0:T(8,128)S(1)}, u32[]{:S(2)}, u32[]{:S(2)}) collective-permute-start(f32[104,128]{1,0:T(8,128)S(1)} %get-tuple-element.27), channel_id=1, source_target_pairs={{0,7},{1,2},{2,1},{3,4},{4,3},{5,6},{6,5},{7,0},{8,15},{9,10},{10,... | collective-permute-start | bytes 159752 | tf_op jit(solution)/shard_map/ppermute | solution.py:443
  30.0 0.0 collective-permute-start.3
  30.0 1.5 %collective-permute-done.2.far = f32[104,128]{1,0:T(8,128)S(1)} collective-permute-done((f32[104,128]{1,0:T(8,128)S(1)}, f32[104,128]{1,0:T(8,128)S(1)}, u32[]{:S(2)}, u32[]{:S(2)}) %collective-permute-start.2) | collective-permute-done | bytes 53280 | tf_op jit(solution)/shard_map/ppermute | solution.py:443
  31.5 3.0 %collective-permute-done.3.near = f32[104,128]{1,0:T(8,128)S(1)} collective-permute-done((f32[104,128]{1,0:T(8,128)S(1)}, f32[104,128]{1,0:T(8,128)S(1)}, u32[]{:S(2)}, u32[]{:S(2)}) %collective-permute-start.3) | collective-permute-done | bytes 53280 | tf_op jit(solution)/shard_map/ppermute | solution.py:443
  34.5 2.7 %shard_map.70 = (f32[10,160,128]{2,1,0:T(8,128)S(1)}, f32[10,160,128]{2,1,0:T(8,128)S(1)}, f32[10,160,128]{2,1,0:T(8,128)S(1)}, f32[10,160,128]{2,1,0:T(8,128)S(...) custom-call(f32[4,9,128,128]{3,2,1,0:T(8,128)S(1)} %get-tuple-element.24.blocks, ...), custom_call_target="tpu_custom_call" | custom-call | tf_op jit(solution)/shard_map/pallas_call | solution.py:426
  37.2 20.6 %all_to_all.10.sums = f32[256,1,128]{2,1,0:T(1,128)S(1)} all-to-all(f32[256,1,128]{2,1,0:T(1,128)S(1)} %get-tuple-element.29), channel_id=1, replica_groups=mesh['azim'=32,'radax'=8] {'azim','radax'}, dimensions={0} | all-to-all | bytes 262144 | tf_op jit(solution)/shard_map/all_to_all | solution.py:482
  57.8 1.9 %shard_map.71 = (f32[3,8,64,128]{3,2,1,0:T(8,128)}, f32[8,64,128]{2,1,0:T(8,128)}) custom-call(f32[256,1,128]{2,1,0:T(1,128)S(1)} %all_to_all.10.sums, f32[10,160,128]{2,1,0:T(8,128)S(1)} %get-tuple-element.30.p0, f32[10,160,128]{2,1,0:T(8,128)S(1)} %get-tuple-element.31.p1, f32[10,160,128]{2,1,0:T(8,128)S(1)} %get-tuple-element.32.p2, ...), custom_call_target="tpu_custom_call" | custom-call | tf_op jit(solution)/shard_map/pallas_call | solution.py:426
Async XLA Ops:
  2.5 21.5 %collective-permute-start.1 = (f32[16,64,128]{2,1,0:T(8,128)S(1)}, f32[16,64,128]{2,1,0:T(8,128)S(1)}, u32[]{:S(2)}, u32[]{:S(2)}) collective-permute-start(f32[16,64,128]{2,1,0:T(8,128)S(1)} %get-tuple-element.22), channel_id=1, source_target_pairs={{0,248},{8,16},{16,8},{24,32},{32,24},{40,48},{48,40},{56,64},{64,... | collective-permute-start | bytes 1572872 | tf_op jit(solution)/shard_map/ppermute | solution.py:443
  5.3 18.7 %collective-permute-start = (f32[16,64,128]{2,1,0:T(8,128)S(1)}, f32[16,64,128]{2,1,0:T(8,128)S(1)}, u32[]{:S(2)}, u32[]{:S(2)}) collective-permute-start(f32[16,64,128]{2,1,0:T(8,128)S(1)} %get-tuple-element.21.mine), channel_id=1, source_target_pairs={{0,8},{8,0},{16,24},{24,16},{32,40},{40,32},{48,56},{56,48},{64,72... | collective-permute-start | bytes 1572872 | tf_op jit(solution)/shard_map/ppermute | solution.py:443
  10.4 13.6 %all-to-all-start = ((f32[32,8,128]{2,1,0:T(8,128)}), f32[32,8,128]{2,1,0:T(8,128)S(1)}, u32[]{:S(2)}, u32[]{:S(2)}) async-start(f32[32,8,128]{2,1,0:T(8,128)} %get-tuple-element.23), calls=%async_computation | async-start | bytes 262144 | tf_op jit(solution)/shard_map/all_to_all | solution.py:464
  24.8 6.7 %collective-permute-start.2 = (f32[104,128]{1,0:T(8,128)S(1)}, f32[104,128]{1,0:T(8,128)S(1)}, u32[]{:S(2)}, u32[]{:S(2)}) collective-permute-start(f32[104,128]{1,0:T(8,128)S(1)} %get-tuple-element.27), channel_id=1, source_target_pairs={{0,7},{1,2},{2,1},{3,4},{4,3},{5,6},{6,5},{7,0},{8,15},{9,10},{10,... | collective-permute-start | bytes 159752 | tf_op jit(solution)/shard_map/ppermute | solution.py:443
  30.0 4.5 %collective-permute-start.3 = (f32[104,128]{1,0:T(8,128)S(1)}, f32[104,128]{1,0:T(8,128)S(1)}, u32[]{:S(2)}, u32[]{:S(2)}) collective-permute-start(f32[104,128]{1,0:T(8,128)S(1)} %get-tuple-element.28), channel_id=1, source_target_pairs={{0,1},{1,0},{2,3},{3,2},{4,5},{5,4},{6,7},{7,6},{8,9},{9,8},{10,11... | collective-permute-start | bytes 159752 | tf_op jit(solution)/shard_map/ppermute | solution.py:443

commit v7 on v6

--- a/solution.py
+++ b/solution.py
@@ -372,7 +372,7 @@
     first_cell = lane % HALF == 0
     last_cell = lane % HALF == HALF - 1
     half = jnp.where(lane < HALF, 0.5, -0.5)
-    total = jnp.sum(sums[...], axis=0)
+    total = jnp.sum(jnp.sum(sums[...], axis=0), axis=0, keepdims=True)
     group = iota((1, LANES), 1) // 16
     nu = [jnp.sum(jnp.where(group == k, total, 0.0), axis=1, keepdims=True) for k in range(6)]
     c0, c1, c2 = coefficients(nu)
@@ -474,12 +474,14 @@
     field = (HALO + pairs + 1, TALL, LANES)
     *fields, sums = call(
         basis_kernel,
-        [field] * 6 + [(devices, 1, LANES)],
+        [field] * 6 + [(devices // 8, 8, LANES)],
         (blocks, taps, rot, beside_from_far, beside_from_near),
         scratch=[field] * 4
         + [(4, STRIP, LANES), block, (TALL, LANES), field, (2,) + beside],
     )
+    sums = sums.reshape(devices, 1, LANES)
     sums = lax.all_to_all(sums, ("azim", "radax"), 0, 0, tiled=True)
+    sums = sums.reshape(devices // 8, 8, LANES)
     return call(
         project_kernel,
         [(3, cells) + plane, (cells,) + plane],

time: 59.9 us -> 59.6 us (level)
  no operation moved by 1% of the time
where the time goes in v7:
time: 59.6 us; the launch traced here: 59.4 us
  blocking collectives  20.6 us (35%)
  starting transfers between devices  17.4 us (29%)
  waiting for transfers between devices  13.1 us (22%)
  Pallas kernels  6.94 us (12%)
  between operations  1.31 us (2%)
    all_to_all x1, blocking collectives, per_device(): sums = lax.all_to_all(sums, ('azim', 'radax'), 0, 0, tiled=True)  20.6 us
    ppermute x4, starting transfers between devices, trade(): return (lax.ppermute(far, axis, second), lax.ppermute(near, axis, first))  13.1 us
    all_to_all x1, waiting for transfers between devices, per_device(): turned = lax.all_to_all(spread, 'azim', 0, 0, tiled=True)  8.61 us
    pallas_call x4, Pallas kernels, call(): pl.pallas_call(kernel, out_shape=[space(s, jnp.float32) if space is pltpu...  6.94 us
    ppermute x4, waiting for transfers between devices, trade(): return (lax.ppermute(far, axis, second), lax.ppermute(near, axis, first))  4.49 us
    all_to_all x1, starting transfers between devices, per_device(): turned = lax.all_to_all(spread, 'azim', 0, 0, tiled=True)  4.34 us
  transfers between devices with their start and end apart: 5, of which 3 were waited for; matrix products, arithmetic and copies ran while one was open for 0% of the time, Pallas kernels for 0%

profile of v7, /device:TPU:1, one launch (start us, length us, event | category | flops | bytes accessed | tf_op | source)
XLA Modules:
  0.0 59.4 jit_solution(7736739098647876609)
XLA Ops:
  0.6 1.8 %shard_map.68 = (f32[16,64,128]{2,1,0:T(8,128)S(1)}, f32[16,64,128]{2,1,0:T(8,128)S(1)}, f32[32,8,128]{2,1,0:T(8,128)}, f32[3,8,64,128]{3,2,1,0:T(8,128)S(1)}, f32[8,64,128]{2,1,0:T(8,128)S(1)}) custom-call(f32[3,8,64,128]{3,2,1,0:T(8,128)} %velocity.1, f32[8,64,128]{2,1,0:T(8,128)} %damping.1, f32[3,8,128]{2,1,0:T(8,128)} %weight.1, f32[8,128]{1,0:T(8,128)} %rotor.1), custom_call_target="tpu_custom_call" | custom-call | tf_op jit(solution)/shard_map/pallas_call | solution.py:426
  2.5 2.8 %collective-permute-start.1 = (f32[16,64,128]{2,1,0:T(8,128)S(1)}, f32[16,64,128]{2,1,0:T(8,128)S(1)}, u32[]{:S(2)}, u32[]{:S(2)}) collective-permute-start(f32[16,64,128]{2,1,0:T(8,128)S(1)} %get-tuple-element.22), channel_id=1, source_target_pairs={{0,248},{8,16},{16,8},{24,32},{32,24},{40,48},{48,40},{56,64},{64,... | collective-permute-start | bytes 1572872 | tf_op jit(solution)/shard_map/ppermute | solution.py:443
  5.3 5.1 %collective-permute-start = (f32[16,64,128]{2,1,0:T(8,128)S(1)}, f32[16,64,128]{2,1,0:T(8,128)S(1)}, u32[]{:S(2)}, u32[]{:S(2)}) collective-permute-start(f32[16,64,128]{2,1,0:T(8,128)S(1)} %get-tuple-element.21.mine), channel_id=1, source_target_pairs={{0,8},{8,0},{16,24},{24,16},{32,40},{40,32},{48,56},{56,48},{64,72... | collective-permute-start | bytes 1572872 | tf_op jit(solution)/shard_map/ppermute | solution.py:443
  10.4 4.3 %all-to-all-start = ((f32[32,8,128]{2,1,0:T(8,128)}), f32[32,8,128]{2,1,0:T(8,128)S(1)}, u32[]{:S(2)}, u32[]{:S(2)}) async-start(f32[32,8,128]{2,1,0:T(8,128)} %get-tuple-element.23), calls=%async_computation | async-start | bytes 262144 | tf_op jit(solution)/shard_map/all_to_all | solution.py:464
  15.4 8.6 %all-to-all-done.turned = f32[32,8,128]{2,1,0:T(8,128)S(1)} async-done(((f32[32,8,128]{2,1,0:T(8,128)}), f32[32,8,128]{2,1,0:T(8,128)S(1)}, u32[]{:S(2)}, u32[]{:S(2)}) %all-to-all-start) | async-done | bytes 131104 | tf_op jit(solution)/shard_map/all_to_all | solution.py:464
  24.0 0.0 collective-permute-done.1.far
  24.0 0.0 collective-permute-done.near
  24.0 0.8 %shard_map.69 = (f32[104,128]{1,0:T(8,128)S(1)}, f32[104,128]{1,0:T(8,128)S(1)}, f32[4,9,128,128]{3,2,1,0:T(8,128)S(1)}, f32[3,16,128]{2,1,0:T(8,128)S(1)}, f32[16,128]{1,0:T(8,128)S(1)}) custom-call(s32[1]{0:T(128)S(6)} %copy.8.offset, f32[3,8,64,128]{3,2,1,0:T(8,128)S(1)} %get-tuple-element.19.velocity, f32[8,64,128]{2,1,0:T(8,128)S(1)} %get-tuple-element.20.damping, ...), custom_call_target="tpu_custom_call" | custom-call | tf_op jit(solution)/shard_map/pallas_call | solution.py:426
  24.8 5.2 %collective-permute-start.2 = (f32[104,128]{1,0:T(8,128)S(1)}, f32[104,128]{1,0:T(8,128)S(1)}, u32[]{:S(2)}, u32[]{:S(2)}) collective-permute-start(f32[104,128]{1,0:T(8,128)S(1)} %get-tuple-element.27), channel_id=1, source_target_pairs={{0,7},{1,2},{2,1},{3,4},{4,3},{5,6},{6,5},{7,0},{8,15},{9,10},{10,... | collective-permute-start | bytes 159752 | tf_op jit(solution)/shard_map/ppermute | solution.py:443
  30.0 0.0 collective-permute-start.3
  30.0 1.5 %collective-permute-done.2.far = f32[104,128]{1,0:T(8,128)S(1)} collective-permute-done((f32[104,128]{1,0:T(8,128)S(1)}, f32[104,128]{1,0:T(8,128)S(1)}, u32[]{:S(2)}, u32[]{:S(2)}) %collective-permute-start.2) | collective-permute-done | bytes 53280 | tf_op jit(solution)/shard_map/ppermute | solution.py:443
  31.5 3.0 %collective-permute-done.3.near = f32[104,128]{1,0:T(8,128)S(1)} collective-permute-done((f32[104,128]{1,0:T(8,128)S(1)}, f32[104,128]{1,0:T(8,128)S(1)}, u32[]{:S(2)}, u32[]{:S(2)}) %collective-permute-start.3) | collective-permute-done | bytes 53280 | tf_op jit(solution)/shard_map/ppermute | solution.py:443
  34.5 2.6 %shard_map.70 = (f32[10,160,128]{2,1,0:T(8,128)S(1)}, f32[10,160,128]{2,1,0:T(8,128)S(1)}, f32[10,160,128]{2,1,0:T(8,128)S(1)}, f32[10,160,128]{2,1,0:T(8,128)S(...) custom-call(f32[4,9,128,128]{3,2,1,0:T(8,128)S(1)} %get-tuple-element.24.blocks, ...), custom_call_target="tpu_custom_call" | custom-call | tf_op jit(solution)/shard_map/pallas_call | solution.py:426
  37.1 20.6 %all_to_all.10 = f32[256,1,128]{2,1,0:T(1,128)S(1)} all-to-all(f32[256,1,128]{2,1,0:T(1,128)S(1)} %bitcast.5), channel_id=1, replica_groups=mesh['azim'=32,'radax'=8] {'azim','radax'}, dimensions={0} | all-to-all | bytes 262144 | tf_op jit(solution)/shard_map/all_to_all | solution.py:483
  57.7 1.7 %shard_map.71 = (f32[3,8,64,128]{3,2,1,0:T(8,128)}, f32[8,64,128]{2,1,0:T(8,128)}) custom-call(f32[32,8,128]{2,1,0:T(8,128)S(1)} %bitcast.4, f32[10,160,128]{2,1,0:T(8,128)S(1)} %get-tuple-element.30.p0, f32[10,160,128]{2,1,0:T(8,128)S(1)} %get-tuple-element.31.p1, f32[10,160,128]{2,1,0:T(8,128)S(1)} %get-tuple-element.32.p2, ...), custom_call_target="tpu_custom_call" | custom-call | tf_op jit(solution)/shard_map/pallas_call | solution.py:426
Async XLA Ops:
  2.5 21.5 %collective-permute-start.1 = (f32[16,64,128]{2,1,0:T(8,128)S(1)}, f32[16,64,128]{2,1,0:T(8,128)S(1)}, u32[]{:S(2)}, u32[]{:S(2)}) collective-permute-start(f32[16,64,128]{2,1,0:T(8,128)S(1)} %get-tuple-element.22), channel_id=1, source_target_pairs={{0,248},{8,16},{16,8},{24,32},{32,24},{40,48},{48,40},{56,64},{64,... | collective-permute-start | bytes 1572872 | tf_op jit(solution)/shard_map/ppermute | solution.py:443
  5.3 18.7 %collective-permute-start = (f32[16,64,128]{2,1,0:T(8,128)S(1)}, f32[16,64,128]{2,1,0:T(8,128)S(1)}, u32[]{:S(2)}, u32[]{:S(2)}) collective-permute-start(f32[16,64,128]{2,1,0:T(8,128)S(1)} %get-tuple-element.21.mine), channel_id=1, source_target_pairs={{0,8},{8,0},{16,24},{24,16},{32,40},{40,32},{48,56},{56,48},{64,72... | collective-permute-start | bytes 1572872 | tf_op jit(solution)/shard_map/ppermute | solution.py:443
  10.4 13.6 %all-to-all-start = ((f32[32,8,128]{2,1,0:T(8,128)}), f32[32,8,128]{2,1,0:T(8,128)S(1)}, u32[]{:S(2)}, u32[]{:S(2)}) async-start(f32[32,8,128]{2,1,0:T(8,128)} %get-tuple-element.23), calls=%async_computation | async-start | bytes 262144 | tf_op jit(solution)/shard_map/all_to_all | solution.py:464
  24.8 6.7 %collective-permute-start.2 = (f32[104,128]{1,0:T(8,128)S(1)}, f32[104,128]{1,0:T(8,128)S(1)}, u32[]{:S(2)}, u32[]{:S(2)}) collective-permute-start(f32[104,128]{1,0:T(8,128)S(1)} %get-tuple-element.27), channel_id=1, source_target_pairs={{0,7},{1,2},{2,1},{3,4},{4,3},{5,6},{6,5},{7,0},{8,15},{9,10},{10,... | collective-permute-start | bytes 159752 | tf_op jit(solution)/shard_map/ppermute | solution.py:443
  30.0 4.5 %collective-permute-start.3 = (f32[104,128]{1,0:T(8,128)S(1)}, f32[104,128]{1,0:T(8,128)S(1)}, u32[]{:S(2)}, u32[]{:S(2)}) collective-permute-start(f32[104,128]{1,0:T(8,128)S(1)} %get-tuple-element.28), channel_id=1, source_target_pairs={{0,1},{1,0},{2,3},{3,2},{4,5},{5,4},{6,7},{7,6},{8,9},{9,8},{10,11... | collective-permute-start | bytes 159752 | tf_op jit(solution)/shard_map/ppermute | solution.py:443
